TPU v7x, 32 devices: a whole 2x2x4 slice. The times are simulated.
32 devices in a mesh: groups: 2 (over x), replica: 8 (over z, y), channel: 2 (over core).
Axes of the slice: x: 2, y: 2, z: 4, core: 2. Of those that a mesh axis runs over, the one named last changes fastest.
Arguments:
- queries: bfloat16 [16, 2, 32, 4096], P(('groups', 'replica'), None, None, 'channel'), parts along dimension 0, may hold values from -360 to 360
- new_kv: bfloat16 [16, 2, 32, 1024], P(('groups', 'replica'), None, None, 'channel'), parts along dimension 0, may hold values from -6 to 6
- cached_lookup_pairs: bfloat16 [16, 1024, 1024], P(('groups', 'replica'), None, 'channel'), parts along dimension 0, may hold values from -6 to 6
- prefix_ssm: bfloat16 [16, 16, 8192], P(('groups', 'replica'), None, 'channel'), parts along dimension 0, may hold values from -6 to 6
- prefix_conv: bfloat16 [16, 3, 8192], P(('groups', 'replica'), None, 'channel'), parts along dimension 0, may hold values from -6 to 6
- pool_kv: bfloat16 [16, 4, 256, 1024], P(('groups', 'replica'), None, None, 'channel'), parts along dimension 0, may hold values from -6 to 6
- pool_ssm: bfloat16 [16, 16, 8192], P(('groups', 'replica'), None, 'channel'), parts along dimension 0, may hold values from -6 to 6
- pool_conv: bfloat16 [16, 3, 8192], P(('groups', 'replica'), None, 'channel'), parts along dimension 0, may hold values from -6 to 6
- owner_id: int32 [2], P('groups'), parts along dimension 0, may hold values from 0 to 7
- readers: int32 [16], P(('groups', 'replica')), parts along dimension 0, may hold values 0 or 1
- restore_src: int32 [16, 4], P('groups'), parts along dimension 0, may hold values from 0 to 7, as said below
- restore_blk: int32 [16, 4], P('groups'), parts along dimension 0, may hold values from 0 to 3, as said below
- state_src: int32 [16], P('groups'), parts along dimension 0, may hold values from 0 to 7, as said below
- ctx_blocks: int32 [16], P(('groups', 'replica')), parts along dimension 0, may hold values from 1 to 4, as said below
- mamba_x: bfloat16 [16, 2, 32, 8192], P(('groups', 'replica'), None, None, 'channel'), parts along dimension 0, may hold values from -6 to 6
- mamba_z: bfloat16 [16, 2, 32, 8192], P(('groups', 'replica'), None, None, 'channel'), parts along dimension 0, may hold values from -6 to 6
- mamba_dt: bfloat16 [16, 2, 32, 8192], P(('groups', 'replica'), None, None, 'channel'), parts along dimension 0, may hold values from -2 to 8
- dt_bias: float32 [8192], P('channel'), may hold values from -6 to -2.5
- a_log: float32 [16, 8192], P(None, 'channel'), may hold values from 0 to 2
- bypass_gain: float32 [8192], P('channel'), may hold values from 0.5 to 1.5
- conv_w: float32 [4, 8192], P(None, 'channel'), may hold values from -3 to 3
- conv_b: float32 [8192], P('channel'), may hold values from -0.5 to 0.5
- w_bc: bfloat16 [8192, 32], P('channel'), may hold values from -0.0625 to 0.0625
Outputs:
- attention_out: bfloat16 [16, 2, 32, 4096], P(('groups', 'replica'), None, None, 'channel'), parts along dimension 0
- mamba_out: bfloat16 [16, 2, 32, 8192], P(('groups', 'replica'), None, None, 'channel'), parts along dimension 0
There are 2 independent parts, one for each index of `groups`. A program takes and returns all parts, laid end to end along the dimension named above; an argument that names none is the same for every part. Nothing has to cross between parts.
Inputs may be any that keep to these rules, and one draw needn't show every extreme that they name: `restore_src`: each row names 4 different replicas, and each replica is named in exactly 4 rows, so at most one block goes from one replica to one row's replica. Every pair (restore_src, restore_blk) is different: each stored block of each replica is listed exactly once. `state_src`: A permutation of the replicas. Only slots j < ctx_blocks[d] of row d are read; some replica has 4.
All inputs are finite; a program needn't handle non-finite values. No bound on the sum of `readers` on one device may be relied on, other than what follows from the above.
Results may differ from a plain program's by a relative error of at most 0.0049.
Values may be sent and summed in bfloat16 or wider, within the bound.
No kernel may reach another device: no remote copies, remote signals or barrier semaphores. Data moves between devices by JAX's collectives and lax.ppermute only.
A program may use at most 128 MiB of HBM per device.

v0:
```python
import functools
import math

import jax
import jax.numpy as jnp
from jax import lax
from jax.experimental import pallas as pl
from jax.experimental.pallas import tpu as pltpu
from jax.sharding import PartitionSpec as P

HD = 128
Q_PER_KV = 8
F32 = jnp.float32
BF16 = jnp.bfloat16
LOG2E = math.log2(math.e)
SCORE2 = HD ** (-0.5) * LOG2E
LOW = -1e30
STAT = 16
VMEM_LIMIT = 48 * 1024 * 1024

VSPEC = pl.BlockSpec(memory_space=pltpu.VMEM)
SSPEC = pl.BlockSpec(memory_space=pltpu.SMEM)


def call(body, out_shape, specs, scratch=(), cost=None):
    return pl.pallas_call(
        body,
        out_shape=out_shape,
        in_specs=specs,
        out_specs=jax.tree.map(lambda _: VSPEC, out_shape),
        scratch_shapes=list(scratch),
        compiler_params=pltpu.CompilerParams(vmem_limit_bytes=VMEM_LIMIT),
        cost_estimate=cost,
    )


def dot(a, b, ca, cb):
    return lax.dot_general(a, b, (((ca,), (cb,)), ((), ())), preferred_element_type=F32)


def pieces(row, count):
    out = []
    for _ in range(count):
        part = row.astype(BF16).astype(F32)
        out.append(part)
        row = row - part
    return out


def stat_block(rows, width):
    index = lax.broadcasted_iota(jnp.int32, (STAT, width), 0)
    block = jnp.zeros((STAT, width), F32)
    for i, row in enumerate(rows):
        block = jnp.where(index == i, row, block)
    return block.astype(BF16)


def stats_of(part_ref, base, head):
    block = part_ref[base : base + STAT, :].astype(F32)
    o = 5 * head
    top = block[o : o + 1] + block[o + 1 : o + 2] + block[o + 2 : o + 3]
    total = block[o + 3 : o + 4] + block[o + 4 : o + 5]
    return top, total


def prefix_body(heads, spans, *refs):
    info, own, nbr = refs[:3]
    qs = refs[3 : 3 + spans]
    outs = refs[3 + spans : 3 + 2 * spans]
    kv = refs[3 + 2 * spans]
    here, mine = info[0], info[1]
    rows = heads * HD

    @pl.when(here == 1)
    def _():
        kv[...] = jnp.where(mine == 1, own[...], nbr[...])
        for q, out in zip(qs, outs):
            wide = Q_PER_KV * (q.shape[0] - STAT) // (2 * heads * Q_PER_KV)
            stats = []
            for h in range(heads):
                qh = q[h * wide : (h + 1) * wide, :]
                s = dot(kv[:, 2 * h * HD : (2 * h + 1) * HD], qh, 1, 1)
                m = jnp.max(s, axis=0, keepdims=True)
                p = jnp.exp2((s - m) * SCORE2)
                l = jnp.sum(p, axis=0, keepdims=True)
                o = dot(kv[:, (2 * h + 1) * HD : (2 * h + 2) * HD], p.astype(BF16), 0, 0)
                out[h * HD : (h + 1) * HD, :] = o.astype(BF16)
                stats += pieces(m, 3) + pieces(l, 2)
            out[rows:, :] = stat_block(stats, wide)

    @pl.when(here != 1)
    def _():
        for q, out in zip(qs, outs):
            wide = out.shape[1]
            out[:rows, :] = jnp.zeros((rows, wide), BF16)
            low = jnp.full((1, wide), LOW, F32)
            zero = jnp.zeros((1, wide), F32)
            out[rows:, :] = stat_block((pieces(low, 3) + [zero, zero]) * heads, wide)


def blocks_body(heads, spans, slots, pair, *refs):
    info, src, blk, own, nbr = refs[:5]
    qs = refs[5 : 5 + spans]
    outs = refs[5 + spans : 5 + 2 * spans]
    acc, top, tot = refs[5 + 2 * spans :]
    z, y = info[0], info[1]
    rows = heads * HD
    for k, (q, out) in enumerate(zip(qs, outs)):
        half = q.shape[0] - STAT
        wide = half // (2 * heads)
        reader = lax.rem(z + (spans - k), spans) * pair + y
        ctx = jnp.max(q[half:, :].astype(F32))
        acc[...] = jnp.zeros_like(acc)
        top[...] = jnp.full(top.shape, LOW, F32)
        tot[...] = jnp.zeros_like(tot)

        def slot(j, carry, q=q, half=half, wide=wide, reader=reader, ctx=ctx):
            source = src[reader, j]
            live = (source // pair == z) & (j.astype(F32) < ctx)

            @pl.when(live)
            def _():
                b = blk[reader, j]
                kv = jnp.where(lax.rem(source, pair) == y, own[b], nbr[b])
                for h in range(heads):
                    lo = half // 2 + h * wide
                    s = dot(kv[:, 2 * h * HD : (2 * h + 1) * HD], q[lo : lo + wide, :], 1, 1)
                    old = top[h]
                    m = jnp.maximum(old, jnp.max(s, axis=0, keepdims=True))
                    p = jnp.exp2((s - m) * SCORE2)
                    fade = jnp.exp2((old - m) * SCORE2)
                    o = dot(kv[:, (2 * h + 1) * HD : (2 * h + 2) * HD], p.astype(BF16), 0, 0)
                    acc[h] = acc[h] * fade + o
                    tot[h] = tot[h] * fade + jnp.sum(p, axis=0, keepdims=True)
                    top[h] = m

            return carry

        lax.fori_loop(0, slots, slot, 0)
        stats = []
        for h in range(heads):
            out[h * HD : (h + 1) * HD, :] = acc[h].astype(BF16)
            stats += pieces(top[h], 3) + pieces(tot[h], 2)
        out[rows:, :] = stat_block(stats, wide)


def join_body(heads, spans, *refs):
    flag, q, new = refs[:3]
    parts = (refs[3 : 3 + spans], refs[3 + spans : 3 + 2 * spans])
    out = refs[3 + 2 * spans]
    fresh = new.shape[1]
    half = q.shape[0] - STAT
    wide = half // (2 * heads)
    rows = heads * HD
    for r in range(2):
        for h in range(heads):
            lo = r * half // 2 + h * wide
            s = dot(new[r, :, 2 * h * HD : (2 * h + 1) * HD], q[lo : lo + wide, :], 1, 1)
            key = lax.broadcasted_iota(jnp.int32, (fresh, wide), 0)
            token = lax.rem(lax.broadcasted_iota(jnp.int32, (fresh, wide), 1), fresh)
            seen = key <= token
            s = jnp.where(seen, s, LOW)
            best = jnp.max(s, axis=0, keepdims=True)
            stats = [stats_of(part, rows, h) for part in parts[r]]
            if r == 0:
                stats = [(jnp.where(flag[0] > 0, m, LOW), l) for m, l in stats]
            for m, _ in stats:
                best = jnp.maximum(best, m)
            p = jnp.where(seen, jnp.exp2((s - best) * SCORE2), 0.0)
            total = jnp.sum(p, axis=0, keepdims=True)
            o = dot(new[r, :, (2 * h + 1) * HD : (2 * h + 2) * HD], p.astype(BF16), 0, 0)
            for part, (m, l) in zip(parts[r], stats):
                w = jnp.exp2((m - best) * SCORE2)
                total = total + w * l
                o = o + w * part[h * HD : (h + 1) * HD, :].astype(F32)
            done = jnp.transpose(o / total).astype(BF16)
            for g in range(Q_PER_KV):
                col = (h * Q_PER_KV + g) * HD
                out[r, :, col : col + HD] = done[g * fresh : (g + 1) * fresh, :]


def silu(x):
    return x / (1.0 + jnp.exp(-x))


def gains_body(state, chunk, flag, st0, st1, x, w, b, wbc, out, pad):
    taps = w.shape[0]
    keep = taps - 1
    length = x.shape[1]
    lead = 8
    total = [jnp.zeros((length, wbc.shape[1]), F32) for _ in range(2)]
    for c in range(0, x.shape[2], chunk):
        at = slice(c, c + chunk)
        for r, st in enumerate((st0, st1)):
            first = st[state : state + keep, at].astype(F32)
            if r == 0:
                first = jnp.where(flag[0] > 0, first, 0.0)
            pad[r, lead - keep : lead, :] = first
            pad[r, lead:, :] = x[r, :, at].astype(F32)
            acc = b[:, at] + w[0:1, at] * pad[r, lead - keep : lead - keep + length, :]
            for k in range(1, taps):
                acc = acc + w[k : k + 1, at] * pad[r, lead - keep + k : lead - keep + k + length, :]
            total[r] = total[r] + dot(silu(acc).astype(BF16), wbc[at, :], 1, 0)
    for r in range(2):
        out[r] = total[r]


def scan_body(state, flag, bc, st0, st1, x, dt, zg, dtb, alog, gain, w, b, out, pad, step, push, res, dec):
    taps = w.shape[0]
    keep = taps - 1
    length = x.shape[1]
    sub = x.shape[2]
    block = 16
    dec[...] = jnp.exp(alog[...]) * (-LOG2E)
    for r, st in enumerate((st0, st1)):
        first = st[state : state + keep].astype(F32)
        if r == 0:
            first = jnp.where(flag[0] > 0, first, 0.0)
        pad[0:keep] = first
        pad[keep:] = x[r].astype(F32)

        def prepare(t, carry, r=r):
            acc = b[...] + w[0] * pad[t]
            for k in range(1, taps):
                acc = acc + w[k] * pad[t + k]
            sig = silu(acc)
            raw = dt[r, t].astype(F32) + dtb[...]
            now = jnp.maximum(raw, 0.0) + jnp.log1p(jnp.exp(-jnp.abs(raw)))
            step[r, t] = now
            push[r, t] = now * sig
            res[r, t] = gain[...] * sig
            return carry

        lax.fori_loop(0, length, prepare, 0)

    for r, st in enumerate((st0, st1)):
        for c in range(0, sub, block):
            at = slice(c, c + block)
            start = []
            for n in range(state):
                h = st[n, at, :].astype(F32)
                if r == 0:
                    h = jnp.where(flag[0] > 0, h, 0.0)
                start.append(h)

            def advance(t, hs, r=r, at=at):
                now = step[r, t, at, :]
                add = push[r, t, at, :]
                sums = [res[r, t, at, :], None, None, None]
                after = []
                for n in range(state):
                    h = jnp.exp2(now * dec[n, at, :]) * hs[n] + bc[r * length + t, n] * add
                    term = bc[r * length + t, state + n] * h
                    i = n % 4
                    sums[i] = term if sums[i] is None else sums[i] + term
                    after.append(h)
                y = (sums[0] + sums[1]) + (sums[2] + sums[3])
                gate = silu(zg[r, t, at, :].astype(F32))
                out[r, t, at, :] = (y * gate).astype(BF16)
                return tuple(after)

            lax.fori_loop(0, length, advance, tuple(start))


def local(
    size,
    queries,
    new_kv,
    cached_lookup_pairs,
    prefix_ssm,
    prefix_conv,
    pool_kv,
    pool_ssm,
    pool_conv,
    owner_id,
    readers,
    restore_src,
    restore_blk,
    state_src,
    ctx_blocks,
    mamba_x,
    mamba_z,
    mamba_dt,
    dt_bias,
    a_log,
    bypass_gain,
    conv_w,
    conv_b,
    w_bc,
):
    axis = "replica"
    pair = 2
    spans = size // pair
    length = queries.shape[2]
    heads = new_kv.shape[3] // (2 * HD)
    wide = Q_PER_KV * length
    slots = restore_src.shape[1]
    inner = mamba_x.shape[3]
    state = a_log.shape[0]
    keep = prefix_conv.shape[1]
    me = lax.axis_index(axis)
    z, y = me // pair, me % pair
    owner = owner_id[0]

    def across(value):
        return lax.ppermute(value, axis, [(s, s ^ 1) for s in range(size)])

    def turn(value, k):
        return lax.ppermute(value, axis, [(s, (s + k * pair) % size) for s in range(size)])

    states = jnp.concatenate([pool_ssm[0], pool_conv[0], prefix_ssm[0], prefix_conv[0]], axis=0)
    states_nbr = across(states)

    folded = queries[0].reshape(2, length, heads * Q_PER_KV, HD).transpose(0, 2, 1, 3)
    folded = folded.reshape(2 * heads * wide, HD)
    length_rows = jnp.full((STAT, HD), ctx_blocks[0].astype(BF16), BF16)
    message = jnp.concatenate([folded, length_rows], axis=0)
    asked = [message] + [turn(message, k) for k in range(1, spans)]

    prefix_nbr = across(cached_lookup_pairs[0])
    pool_nbr = across(pool_kv[0])

    part_shape = jax.ShapeDtypeStruct((heads * HD + STAT, wide), BF16)
    info0 = jnp.stack([(owner // pair == z), (owner % pair == y)]).astype(jnp.int32)
    keys = cached_lookup_pairs.shape[1]
    part0 = call(
        functools.partial(prefix_body, heads, spans),
        [part_shape] * spans,
        [SSPEC] + [VSPEC] * (2 + spans),
        [pltpu.VMEM(cached_lookup_pairs.shape[1:], BF16)],
        pl.CostEstimate(flops=spans * heads * keys * wide * HD * 4, bytes_accessed=4 << 20, transcendentals=spans * heads * keys * wide),
    )(info0, cached_lookup_pairs[0], prefix_nbr, *asked)
    got0 = [part0[0]] + [turn(part0[k], spans - k) for k in range(1, spans)]

    info1 = jnp.stack([z, y]).astype(jnp.int32)
    block_len = pool_kv.shape[2]
    part1 = call(
        functools.partial(blocks_body, heads, spans, slots, pair),
        [part_shape] * spans,
        [SSPEC] * 3 + [VSPEC] * (2 + spans),
        [
            pltpu.VMEM((heads, HD, wide), F32),
            pltpu.VMEM((heads, 1, wide), F32),
            pltpu.VMEM((heads, 1, wide), F32),
        ],
        pl.CostEstimate(flops=slots * heads * block_len * wide * HD * 4, bytes_accessed=4 << 20, transcendentals=slots * heads * block_len * wide),
    )(info1, restore_src, restore_blk, pool_kv[0], pool_nbr, *asked)
    got1 = [part1[0]] + [turn(part1[k], spans - k) for k in range(1, spans)]

    rows = state + keep

    def stored(holder):
        return jnp.where(holder % pair == y, states[:rows], states_nbr[:rows])

    back = [stored(state_src[me])]
    for k in range(1, spans):
        reader = ((z + k) % spans) * pair + y
        back.append(turn(stored(state_src[reader]), k))
    came = (z - state_src[me] // pair) % spans
    state1 = back[0]
    for k in range(1, spans):
        state1 = jnp.where(came == k, back[k], state1)
    state0 = jnp.where(owner % pair == y, states[rows:], states_nbr[rows:])
    away = owner // pair
    hop = 1
    while hop < spans:
        other = lax.ppermute(
            state0, axis, [(s, ((s // pair) ^ hop) * pair + s % pair) for s in range(size)]
        )
        state0 = jnp.where((away ^ z) & hop != 0, other, state0)
        hop *= 2

    chunk = math.gcd(inner, 512)
    partial = call(
        functools.partial(gains_body, state, chunk),
        jax.ShapeDtypeStruct((2, length, w_bc.shape[1]), F32),
        [SSPEC] + [VSPEC] * 6,
        [pltpu.VMEM((2, length + 8, chunk), F32)],
        pl.CostEstimate(flops=2 * 2 * length * inner * 32, bytes_accessed=2 << 20, transcendentals=2 * length * inner),
    )(readers, state0, state1, mamba_x[0], conv_w, conv_b[None], w_bc)
    both = partial + lax.ppermute(partial, "channel", [(0, 1), (1, 0)])
    bc = both.reshape(2 * length, w_bc.shape[1])
    sub = inner // HD

    def tiled(value):
        return value.reshape(value.shape[:-1] + (sub, HD))

    scan_out = call(
        functools.partial(scan_body, state),
        jax.ShapeDtypeStruct((2, length, sub, HD), BF16),
        [SSPEC] * 2 + [VSPEC] * 10,
        [
            pltpu.VMEM((length + keep, sub, HD), F32),
            pltpu.VMEM((2, length, sub, HD), F32),
            pltpu.VMEM((2, length, sub, HD), F32),
            pltpu.VMEM((2, length, sub, HD), F32),
            pltpu.VMEM((state, sub, HD), F32),
        ],
        pl.CostEstimate(flops=2 * length * inner * state * 6, bytes_accessed=4 << 20, transcendentals=2 * length * inner * state),
    )(
        readers,
        bc,
        tiled(state0),
        tiled(state1),
        tiled(mamba_x[0]),
        tiled(mamba_dt[0]),
        tiled(mamba_z[0]),
        tiled(dt_bias),
        tiled(a_log),
        tiled(bypass_gain),
        tiled(conv_w),
        tiled(conv_b),
    )
    mamba_out = scan_out.reshape(1, 2, length, inner)

    attention_out = call(
        functools.partial(join_body, heads, spans),
        jax.ShapeDtypeStruct((2, length, heads * Q_PER_KV * HD), BF16),
        [SSPEC] + [VSPEC] * (2 + 2 * spans),
        (),
        pl.CostEstimate(flops=1 << 24, bytes_accessed=2 << 20, transcendentals=1 << 16),
    )(readers, message, new_kv[0], *got0, *got1)[None]
    return (attention_out, mamba_out)


def solution(mesh):
    row = ("groups", "replica")
    placed = (
        P(row, None, None, "channel"),
        P(row, None, None, "channel"),
        P(row, None, "channel"),
        P(row, None, "channel"),
        P(row, None, "channel"),
        P(row, None, None, "channel"),
        P(row, None, "channel"),
        P(row, None, "channel"),
        P("groups"),
        P(row),
        P("groups", None),
        P("groups", None),
        P("groups"),
        P(row),
        P(row, None, None, "channel"),
        P(row, None, None, "channel"),
        P(row, None, None, "channel"),
        P("channel"),
        P(None, "channel"),
        P("channel"),
        P(None, "channel"),
        P("channel"),
        P("channel", None),
    )
    return jax.shard_map(
        functools.partial(local, mesh.shape["replica"]),
        mesh=mesh,
        in_specs=placed,
        out_specs=(P(row, None, None, "channel"), P(row, None, None, "channel")),
        check_vma=False,
    )
```

profile of v0, /device:TPU:0, one launch (start us, length us, event | category | flops | bytes accessed | tf_op | source)
XLA Modules:
  0.0 110.3 jit_solution(18412940373809619263)
XLA Ops:
  0.6 1.1 pad_maximum_fusion
  1.7 3.0 %collective-permute-start.11 = (bf16[38,4096]{1,0:T(8,128)(2,1)S(1)}, bf16[38,4096]{1,0:T(8,128)(2,1)S(1)}, u32[]{:S(2)}, u32[]{:S(2)}) collective-permute-start(bf16[38,4096]{1,0:T(8,128)(2,1)S(1)} %pad_maximum_fusion), channel_id=1, source_target_pairs={{0,2},{2,0},{4,6},{6,4},{8,10},{10,8},{12,14},{14,12},{1,3},{3,1},... | collective-permute-start | bytes 933896 | tf_op jit(solution)/shard_map/ppermute | solution.py:306
  4.8 0.7 copy-done.19
  5.4 0.7 fusion
  12.0 0.5 collective-permute-done.11
  12.5 0.1 broadcast_select_fusion
  12.6 3.9 %collective-permute-start.14 = (bf16[19,4096]{1,0:T(8,128)(2,1)S(1)}, bf16[19,4096]{1,0:T(8,128)(2,1)S(1)}, u32[]{:S(2)}, u32[]{:S(2)}) collective-permute-start(bf16[19,4096]{1,0:T(8,128)(2,1)S(1)} %get-tuple-element.20), channel_id=1, source_target_pairs={{0,12},{2,14},{4,0},{6,2},{8,4},{10,6},{12,8},{14,10},{1,13},{3,15... | collective-permute-start | bytes 466952 | tf_op jit(solution)/shard_map/ppermute | solution.py:309
  16.5 1.0 collective-permute-start.16
  20.8 1.0 collective-permute-done.14
  21.9 10.4 %collective-permute-done.15 = bf16[19,4096]{1,0:T(8,128)(2,1)S(1)} collective-permute-done((bf16[19,4096]{1,0:T(8,128)(2,1)S(1)}, bf16[19,4096]{1,0:T(8,128)(2,1)S(1)}, u32[]{:S(2)}, u32[]{:S(2)}) %collective-permute-start.15) | collective-permute-done | bytes 155680 | tf_op jit(solution)/shard_map/ppermute | solution.py:309
  32.3 0.2 select_select_fusion
  32.5 0.9 collective-permute-start.12
  33.5 0.1 copy.25
  34.3 1.2 %collective-permute-start.1 = (bf16[1040,128]{1,0:T(8,128)(2,1)S(1)}, bf16[1040,128]{1,0:T(8,128)(2,1)S(1)}, u32[]{:S(2)}, u32[]{:S(2)}) collective-permute-start(bf16[1040,128]{1,0:T(8,128)(2,1)S(1)} %concatenate.12.refs_3_.refs_5_.refs_1_), channel_id=1, source_target_pairs={{0,4},{2,6},{4,8},{6,10},{8,12},{10,14},{12,0},{14,2},{1,5},{3,7},... | collective-permute-start | bytes 798728 | tf_op jit(solution)/shard_map/ppermute | solution.py:309
  35.5 2.8 %collective-permute-start.2 = (bf16[1040,128]{1,0:T(8,128)(2,1)S(1)}, bf16[1040,128]{1,0:T(8,128)(2,1)S(1)}, u32[]{:S(2)}, u32[]{:S(2)}) collective-permute-start(bf16[1040,128]{1,0:T(8,128)(2,1)S(1)} %concatenate.12.refs_3_.refs_5_.refs_1_), channel_id=1, source_target_pairs={{0,8},{2,10},{4,12},{6,14},{8,0},{10,2},{12,4},{14,6},{1,9},{3,11}... | collective-permute-start | bytes 798728 | tf_op jit(solution)/shard_map/ppermute | solution.py:309
  38.2 1.0 collective-permute-start.3
  39.3 1.5 %collective-permute-start = (bf16[1024,512]{1,0:T(8,128)(2,1)}, bf16[1024,512]{1,0:T(8,128)(2,1)}, u32[]{:S(2)}, u32[]{:S(2)}) collective-permute-start(bf16[1024,512]{1,0:T(8,128)(2,1)} %bitcast.7.refs_1_), channel_id=1, source_target_pairs={{0,2},{2,0},{4,6},{6,4},{8,10},{10,8},{12,14},{14,12},{1,3},{3,1},... | collective-permute-start | bytes 3145736 | tf_op jit(solution)/shard_map/ppermute | solution.py:306
  40.8 0.1 add_convert_fusion.refs_0_
  40.9 6.4 %collective-permute-done.12 = bf16[19,4096]{1,0:T(8,128)(2,1)S(1)} collective-permute-done((bf16[19,4096]{1,0:T(8,128)(2,1)S(1)}, bf16[19,4096]{1,0:T(8,128)(2,1)S(1)}, u32[]{:S(2)}, u32[]{:S(2)}) %collective-permute-start.12) | collective-permute-done | bytes 155680 | tf_op jit(solution)/shard_map/ppermute | solution.py:367
  47.3 1.5 %collective-permute-start.7 = (bf16[4,256,512]{2,1,0:T(8,128)(2,1)S(1)}, bf16[4,256,512]{2,1,0:T(8,128)(2,1)}, u32[]{:S(2)}, u32[]{:S(2)}) collective-permute-start(bf16[4,256,512]{2,1,0:T(8,128)(2,1)S(1)} %bitcast.69), channel_id=1, source_target_pairs={{0,2},{2,0},{4,6},{6,4},{8,10},{10,8},{12,14},{14,12},{1,3},{3,1},... | collective-permute-start | bytes 3145736 | tf_op jit(solution)/shard_map/ppermute | solution.py:306
  48.8 0.7 broadcast_select_fusion.3
  49.5 0.1 pad_add_fusion.refs_0_
  50.3 0.1 copy.26.refs_1_
  50.4 0.6 copy-done.21
  51.0 0.1 copy.27.refs_2_
  51.1 1.4 %copy.28.wbc = bf16[4096,32]{1,0:T(8,128)(2,1)S(1)} copy(bf16[4096,32]{0,1:T(8,128)(2,1)} %param.45) | data formatting | bytes 524288 | tf_op args[22]
  52.5 4.6 %collective-permute-done.2.refs_5_.refs_7_ = bf16[1040,128]{1,0:T(8,128)(2,1)S(1)} collective-permute-done((bf16[1040,128]{1,0:T(8,128)(2,1)S(1)}, bf16[1040,128]{1,0:T(8,128)(2,1)S(1)}, u32[]{:S(2)}, u32[]{:S(2)}) %collective-permute-start.2) | collective-permute-done | bytes 266272 | tf_op jit(solution)/shard_map/ppermute | solution.py:309
  57.1 8.6 %collective-permute-done.refs_2_ = bf16[1024,512]{1,0:T(8,128)(2,1)} collective-permute-done((bf16[1024,512]{1,0:T(8,128)(2,1)}, bf16[1024,512]{1,0:T(8,128)(2,1)}, u32[]{:S(2)}, u32[]{:S(2)}) %collective-permute-start) | collective-permute-done | bytes 1048608 | tf_op jit(solution)/shard_map/ppermute | solution.py:306
  65.7 2.3 %shard_map.230 = (bf16[272,256]{1,0:T(8,128)(2,1)S(1)}, bf16[272,256]{1,0:T(8,128)(2,1)S(1)}, bf16[272,256]{1,0:T(8,128)(2,1)}, bf16[272,256]{1,0:T(8,128)(2,1)}) custom-call(s32[2]{0:T(128)S(1)} %add_convert_fusion.refs_0_, bf16[1024,512]{1,0:T(8,128)(2,1)} %bitcast.7.refs_1_, bf16[1024,512]{1,0:T(8,128)(2,1)} %collective-permute-done.refs_2_, ...), custom_call_target="tpu_custom_call" | custom-call | flops 1073741824 | bytes 4194304 | tf_op jit(solution)/shard_map/pallas_call | solution.py:326
  68.0 7.9 %collective-permute-start.4 = (bf16[272,256]{1,0:T(8,128)(2,1)S(1)}, bf16[272,256]{1,0:T(8,128)(2,1)S(1)}, u32[]{:S(2)}, u32[]{:S(2)}) collective-permute-start(bf16[272,256]{1,0:T(8,128)(2,1)S(1)} %get-tuple-element.11), channel_id=1, source_target_pairs={{0,12},{2,14},{4,0},{6,2},{8,4},{10,6},{12,8},{14,10},{1,13},{3,15... | collective-permute-start | bytes 417800 | tf_op jit(solution)/shard_map/ppermute | solution.py:309
  75.9 1.0 broadcast_select_fusion.4.st0
  76.9 1.3 %shard_map.233 = f32[2,32,32]{2,1,0:T(8,128)S(1)} custom-call(s32[1]{0:T(128)S(6)} %copy.40.refs_0_.flag, bf16[19,4096]{1,0:T(8,128)(2,1)S(1)} %broadcast_select_fusion.4.st0, bf16[19,4096]{1,0:T(8,128)(2,1)S(1)} %get-tuple-element.21.st1, bf16[2,32,4096]{2,1,0:T(8,128)(2,1)S(1)} %bitcast.65, f32[4,4096]{1,0:T(4,128)S(1)} %copy-done.2, ...), custom_call_target="tpu_custom_call" | custom-call | flops 16777216 | bytes 2097152 | tf_op jit(solution)/shard_map/pallas_call | solution.py:374
  78.2 0.1 collective-permute-start.5
  78.3 0.7 collective-permute-start.6
  79.0 6.5 %collective-permute-done.7.refs_4_ = bf16[4,256,512]{2,1,0:T(8,128)(2,1)} collective-permute-done((bf16[4,256,512]{2,1,0:T(8,128)(2,1)S(1)}, bf16[4,256,512]{2,1,0:T(8,128)(2,1)}, u32[]{:S(2)}, u32[]{:S(2)}) %collective-permute-start.7) | collective-permute-done | bytes 1048608 | tf_op jit(solution)/shard_map/ppermute | solution.py:306
  85.5 5.0 %shard_map.231 = (bf16[272,256]{1,0:T(8,128)(2,1)S(1)}, bf16[272,256]{1,0:T(8,128)(2,1)}, bf16[272,256]{1,0:T(8,128)(2,1)}, bf16[272,256]{1,0:T(8,128)(2,1)}) custom-call(s32[2]{0:T(128)S(1)} %pad_add_fusion.refs_0_, s32[8,4]{1,0:T(8,128)S(1)} %copy.26.refs_1_, s32[8,4]{1,0:T(8,128)S(1)} %copy.27.refs_2_, bf16[4,256,512]{2,1,0:T(8,128)(2,1)S(1)} %bitcast.70, ...), custom_call_target="tpu_custom_call" | custom-call | flops 268435456 | bytes 4194304 | tf_op jit(solution)/shard_map/pallas_call | solution.py:337
  90.5 2.2 %collective-permute-start.9 = (bf16[272,256]{1,0:T(8,128)(2,1)}, bf16[272,256]{1,0:T(8,128)(2,1)S(1)}, u32[]{:S(2)}, u32[]{:S(2)}) collective-permute-start(bf16[272,256]{1,0:T(8,128)(2,1)} %get-tuple-element.16), channel_id=1, source_target_pairs={{0,8},{2,10},{4,12},{6,14},{8,0},{10,2},{12,4},{14,6},{1,9},{3,11}... | collective-permute-start | bytes 417800 | tf_op jit(solution)/shard_map/ppermute | solution.py:309
  92.7 0.1 copy.32
  92.8 0.5 copy-done.3
  93.3 0.4 copy-done.13
  93.8 0.1 copy.33
  93.9 0.9 copy-done.14
  94.8 0.1 copy.34
  94.9 0.9 copy-done.17
  96.0 0.7 copy-done.10
  96.7 9.9 %shard_map.234 = bf16[2,32,32,128]{3,2,1,0:T(8,128)(2,1)S(1)} custom-call(s32[1]{0:T(128)S(6)} %copy.40.refs_0_.flag, f32[64,32]{1,0:T(8,128)S(1)} %bitcast.78, bf16[19,32,128]{2,1,0:T(8,128)(2,1)S(1)} %slice.20.st0, bf16[19,32,128]{2,1,0:T(8,128)(2,1)S(1)} %slice.21.st1, bf16[2,32,32,128]{3,2,1,0:T(8,128)(2,1)S(1)} %bitcast.71, ...), custom_call_target="tpu_custom_call" | custom-call | flops 25165824 | bytes 4194304 | tf_op jit(solution)/shard_map/pallas_call | solution.py:388
  106.6 1.0 reshape.44
  107.7 2.6 %shard_map.232 = bf16[2,32,2048]{2,1,0:T(8,128)(2,1)} custom-call(s32[1]{0:T(128)S(6)} %copy.40.refs_0_.flag, bf16[1040,128]{1,0:T(8,128)(2,1)S(1)} %concatenate.12.refs_3_.refs_5_.refs_1_, bf16[2,32,512]{2,1,0:T(8,128)(2,1)S(1)} %bitcast.76, bf16[272,256]{1,0:T(8,128)(2,1)S(1)} %get-tuple-element.10.refs_3_, bf16[272,256]{1,0:T(8,128)(2,1)S(1)} %copy-done.4, ...), custom_call_target="tpu_custom_call" | custom-call | flops 16777216 | bytes 2097152 | tf_op jit(solution)/shard_map/pallas_call | solution.py:416
  (62 shorter events, 0.5 us)
Async XLA Ops:
  1.7 10.8 %copy-start.11 = (bf16[1,16,4096]{2,1,0:T(8,128)(2,1)S(1)}, bf16[1,16,4096]{2,1,0:T(8,128)(2,1)}, u32[]{:S(2)}) copy-start(bf16[1,16,4096]{2,1,0:T(8,128)(2,1)} %param.29) | copy-start | bytes 393220
  1.7 10.7 %collective-permute-start.11 = (bf16[38,4096]{1,0:T(8,128)(2,1)S(1)}, bf16[38,4096]{1,0:T(8,128)(2,1)S(1)}, u32[]{:S(2)}, u32[]{:S(2)}) collective-permute-start(bf16[38,4096]{1,0:T(8,128)(2,1)S(1)} %pad_maximum_fusion), channel_id=1, source_target_pairs={{0,2},{2,0},{4,6},{6,4},{8,10},{10,8},{12,14},{14,12},{1,3},{3,1},... | collective-permute-start | bytes 933896 | tf_op jit(solution)/shard_map/ppermute | solution.py:306
  4.8 0.7 copy-start.19
  7.9 4.5 %copy-start.15 = (bf16[1,3,4096]{2,1,0:T(4,128)(2,1)S(1)}, bf16[1,3,4096]{2,1,0:T(4,128)(2,1)}, u32[]{:S(2)}) copy-start(bf16[1,3,4096]{2,1,0:T(4,128)(2,1)} %param.30) | copy-start | bytes 73732
  12.5 19.8 %copy-start.12 = (bf16[1,16,4096]{2,1,0:T(8,128)(2,1)S(1)}, bf16[1,16,4096]{2,1,0:T(8,128)(2,1)}, u32[]{:S(2)}) copy-start(bf16[1,16,4096]{2,1,0:T(8,128)(2,1)} %param.26) | copy-start | bytes 393220
  12.6 9.3 %collective-permute-start.14 = (bf16[19,4096]{1,0:T(8,128)(2,1)S(1)}, bf16[19,4096]{1,0:T(8,128)(2,1)S(1)}, u32[]{:S(2)}, u32[]{:S(2)}) collective-permute-start(bf16[19,4096]{1,0:T(8,128)(2,1)S(1)} %get-tuple-element.20), channel_id=1, source_target_pairs={{0,12},{2,14},{4,0},{6,2},{8,4},{10,6},{12,8},{14,10},{1,13},{3,15... | collective-permute-start | bytes 466952 | tf_op jit(solution)/shard_map/ppermute | solution.py:309
  16.5 15.8 %collective-permute-start.15 = (bf16[19,4096]{1,0:T(8,128)(2,1)S(1)}, bf16[19,4096]{1,0:T(8,128)(2,1)S(1)}, u32[]{:S(2)}, u32[]{:S(2)}) collective-permute-start(bf16[19,4096]{1,0:T(8,128)(2,1)S(1)} %get-tuple-element.19), channel_id=1, source_target_pairs={{0,8},{2,10},{4,12},{6,14},{8,0},{10,2},{12,4},{14,6},{1,9},{3,11}... | collective-permute-start | bytes 466952 | tf_op jit(solution)/shard_map/ppermute | solution.py:309
  16.5 15.8 %collective-permute-start.16 = (bf16[19,4096]{1,0:T(8,128)(2,1)S(1)}, bf16[19,4096]{1,0:T(8,128)(2,1)S(1)}, u32[]{:S(2)}, u32[]{:S(2)}) collective-permute-start(bf16[19,4096]{1,0:T(8,128)(2,1)S(1)} %get-tuple-element.18), channel_id=1, source_target_pairs={{0,4},{2,6},{4,8},{6,10},{8,12},{10,14},{12,0},{14,2},{1,5},{3,7},... | collective-permute-start | bytes 466952 | tf_op jit(solution)/shard_map/ppermute | solution.py:309
  20.1 12.2 %copy-start.18 = (bf16[1,3,4096]{2,1,0:T(4,128)(2,1)S(1)}, bf16[1,3,4096]{2,1,0:T(4,128)(2,1)}, u32[]{:S(2)}) copy-start(bf16[1,3,4096]{2,1,0:T(4,128)(2,1)} %param.27) | copy-start | bytes 73732
  20.8 12.7 %copy-start.16 = (bf16[1,2,32,2048]{3,2,1,0:T(8,128)(2,1)S(1)}, bf16[1,2,32,2048]{3,2,1,0:T(8,128)(2,1)}, u32[]{:S(2)}) copy-start(bf16[1,2,32,2048]{3,2,1,0:T(8,128)(2,1)} %param.23) | copy-start | bytes 786436
  32.5 14.8 %copy-start.1 = (bf16[1,4,256,512]{3,2,1,0:T(8,128)(2,1)S(1)}, bf16[1,4,256,512]{3,2,1,0:T(8,128)(2,1)}, u32[]{:S(2)}) copy-start(bf16[1,4,256,512]{3,2,1,0:T(8,128)(2,1)} %param.28) | copy-start | bytes 3145732
  32.5 14.8 %collective-permute-start.12 = (bf16[19,4096]{1,0:T(8,128)(2,1)S(1)}, bf16[19,4096]{1,0:T(8,128)(2,1)S(1)}, u32[]{:S(2)}, u32[]{:S(2)}) collective-permute-start(bf16[19,4096]{1,0:T(8,128)(2,1)S(1)} %get-tuple-element.22), channel_id=1, source_target_pairs={{0,4},{2,6},{4,0},{6,2},{8,12},{10,14},{12,8},{14,10},{1,5},{3,7},... | collective-permute-start | bytes 466952 | tf_op jit(solution)/shard_map/ppermute | solution.py:367
  34.3 15.3 %collective-permute-start.1 = (bf16[1040,128]{1,0:T(8,128)(2,1)S(1)}, bf16[1040,128]{1,0:T(8,128)(2,1)S(1)}, u32[]{:S(2)}, u32[]{:S(2)}) collective-permute-start(bf16[1040,128]{1,0:T(8,128)(2,1)S(1)} %concatenate.12.refs_3_.refs_5_.refs_1_), channel_id=1, source_target_pairs={{0,4},{2,6},{4,8},{6,10},{8,12},{10,14},{12,0},{14,2},{1,5},{3,7},... | collective-permute-start | bytes 798728 | tf_op jit(solution)/shard_map/ppermute | solution.py:309
  35.5 21.7 %collective-permute-start.2 = (bf16[1040,128]{1,0:T(8,128)(2,1)S(1)}, bf16[1040,128]{1,0:T(8,128)(2,1)S(1)}, u32[]{:S(2)}, u32[]{:S(2)}) collective-permute-start(bf16[1040,128]{1,0:T(8,128)(2,1)S(1)} %concatenate.12.refs_3_.refs_5_.refs_1_), channel_id=1, source_target_pairs={{0,8},{2,10},{4,12},{6,14},{8,0},{10,2},{12,4},{14,6},{1,9},{3,11}... | collective-permute-start | bytes 798728 | tf_op jit(solution)/shard_map/ppermute | solution.py:309
  38.2 18.9 %collective-permute-start.3 = (bf16[1040,128]{1,0:T(8,128)(2,1)S(1)}, bf16[1040,128]{1,0:T(8,128)(2,1)S(1)}, u32[]{:S(2)}, u32[]{:S(2)}) collective-permute-start(bf16[1040,128]{1,0:T(8,128)(2,1)S(1)} %concatenate.12.refs_3_.refs_5_.refs_1_), channel_id=1, source_target_pairs={{0,12},{2,14},{4,0},{6,2},{8,4},{10,6},{12,8},{14,10},{1,13},{3,15... | collective-permute-start | bytes 798728 | tf_op jit(solution)/shard_map/ppermute | solution.py:309
  39.3 26.4 %collective-permute-start = (bf16[1024,512]{1,0:T(8,128)(2,1)}, bf16[1024,512]{1,0:T(8,128)(2,1)}, u32[]{:S(2)}, u32[]{:S(2)}) collective-permute-start(bf16[1024,512]{1,0:T(8,128)(2,1)} %bitcast.7.refs_1_), channel_id=1, source_target_pairs={{0,2},{2,0},{4,6},{6,4},{8,10},{10,8},{12,14},{14,12},{1,3},{3,1},... | collective-permute-start | bytes 3145736 | tf_op jit(solution)/shard_map/ppermute | solution.py:306
  47.3 38.2 %collective-permute-start.7 = (bf16[4,256,512]{2,1,0:T(8,128)(2,1)S(1)}, bf16[4,256,512]{2,1,0:T(8,128)(2,1)}, u32[]{:S(2)}, u32[]{:S(2)}) collective-permute-start(bf16[4,256,512]{2,1,0:T(8,128)(2,1)S(1)} %bitcast.69), channel_id=1, source_target_pairs={{0,2},{2,0},{4,6},{6,4},{8,10},{10,8},{12,14},{14,12},{1,3},{3,1},... | collective-permute-start | bytes 3145736 | tf_op jit(solution)/shard_map/ppermute | solution.py:306
  49.5 26.4 %collective-permute-start.13 = (bf16[19,4096]{1,0:T(8,128)(2,1)}, bf16[19,4096]{1,0:T(8,128)(2,1)}, u32[]{:S(2)}, u32[]{:S(2)}) collective-permute-start(bf16[19,4096]{1,0:T(8,128)(2,1)} %broadcast_select_fusion.3), channel_id=1, source_target_pairs={{0,8},{2,10},{4,12},{6,14},{8,0},{10,2},{12,4},{14,6},{1,9},{3,11}... | collective-permute-start | bytes 466952 | tf_op jit(solution)/shard_map/ppermute | solution.py:367
  49.6 0.7 copy-start.20
  50.3 0.7 copy-start.21
  65.7 11.2 %copy-start.8 = (f32[4096]{0:T(1024)S(1)}, f32[4096]{0:T(1024)}, u32[]{:S(2)}) copy-start(f32[4096]{0:T(1024)} %param.44) | copy-start | bytes 49156
  68.0 8.8 %copy-start = (bf16[1,2,32,4096]{3,2,1,0:T(8,128)(2,1)S(1)}, bf16[1,2,32,4096]{3,2,1,0:T(8,128)(2,1)}, u32[]{:S(2)}) copy-start(bf16[1,2,32,4096]{3,2,1,0:T(8,128)(2,1)} %param.37) | copy-start | bytes 1572868
  68.0 8.8 %copy-start.2 = (f32[4,4096]{1,0:T(4,128)S(1)}, f32[4,4096]{1,0:T(4,128)}, u32[]{:S(2)}) copy-start(f32[4,4096]{1,0:T(4,128)} %w.1) | copy-start | bytes 196612
  68.0 24.6 %collective-permute-start.4 = (bf16[272,256]{1,0:T(8,128)(2,1)S(1)}, bf16[272,256]{1,0:T(8,128)(2,1)S(1)}, u32[]{:S(2)}, u32[]{:S(2)}) collective-permute-start(bf16[272,256]{1,0:T(8,128)(2,1)S(1)} %get-tuple-element.11), channel_id=1, source_target_pairs={{0,12},{2,14},{4,0},{6,2},{8,4},{10,6},{12,8},{14,10},{1,13},{3,15... | collective-permute-start | bytes 417800 | tf_op jit(solution)/shard_map/ppermute | solution.py:309
  78.1 12.3 %collective-permute-start.17 = (f32[2,32,32]{2,1,0:T(8,128)S(1)}, f32[2,32,32]{2,1,0:T(8,128)S(1)}, u32[]{:S(2)}, u32[]{:S(2)}) collective-permute-start(f32[2,32,32]{2,1,0:T(8,128)S(1)} %shard_map.233), channel_id=1, source_target_pairs={{0,1},{1,0},{2,3},{3,2},{4,5},{5,4},{6,7},{7,6},{8,9},{9,8},{10,11... | collective-permute-start | bytes 24584 | tf_op jit(solution)/shard_map/ppermute | solution.py:381
  78.2 29.4 %collective-permute-start.5 = (bf16[272,256]{1,0:T(8,128)(2,1)}, bf16[272,256]{1,0:T(8,128)(2,1)S(1)}, u32[]{:S(2)}, u32[]{:S(2)}) collective-permute-start(bf16[272,256]{1,0:T(8,128)(2,1)} %get-tuple-element.12), channel_id=1, source_target_pairs={{0,8},{2,10},{4,12},{6,14},{8,0},{10,2},{12,4},{14,6},{1,9},{3,11}... | collective-permute-start | bytes 417800 | tf_op jit(solution)/shard_map/ppermute | solution.py:309
  78.3 29.4 %collective-permute-start.6 = (bf16[272,256]{1,0:T(8,128)(2,1)}, bf16[272,256]{1,0:T(8,128)(2,1)}, u32[]{:S(2)}, u32[]{:S(2)}) collective-permute-start(bf16[272,256]{1,0:T(8,128)(2,1)} %get-tuple-element.13), channel_id=1, source_target_pairs={{0,4},{2,6},{4,8},{6,10},{8,12},{10,14},{12,0},{14,2},{1,5},{3,7},... | collective-permute-start | bytes 417800 | tf_op jit(solution)/shard_map/ppermute | solution.py:309
  90.5 2.3 %copy-start.5 = (bf16[272,256]{1,0:T(8,128)(2,1)}, bf16[272,256]{1,0:T(8,128)(2,1)S(1)}, u32[]{:S(2)}) copy-start(bf16[272,256]{1,0:T(8,128)(2,1)S(1)} %get-tuple-element.14.refs_7_) | copy-start | bytes 417796
  90.5 17.2 %collective-permute-start.8 = (bf16[272,256]{1,0:T(8,128)(2,1)}, bf16[272,256]{1,0:T(8,128)(2,1)S(1)}, u32[]{:S(2)}, u32[]{:S(2)}) collective-permute-start(bf16[272,256]{1,0:T(8,128)(2,1)} %get-tuple-element.15), channel_id=1, source_target_pairs={{0,12},{2,14},{4,0},{6,2},{8,4},{10,6},{12,8},{14,10},{1,13},{3,15... | collective-permute-start | bytes 417800 | tf_op jit(solution)/shard_map/ppermute | solution.py:309
  90.5 17.2 %collective-permute-start.9 = (bf16[272,256]{1,0:T(8,128)(2,1)}, bf16[272,256]{1,0:T(8,128)(2,1)S(1)}, u32[]{:S(2)}, u32[]{:S(2)}) collective-permute-start(bf16[272,256]{1,0:T(8,128)(2,1)} %get-tuple-element.16), channel_id=1, source_target_pairs={{0,8},{2,10},{4,12},{6,14},{8,0},{10,2},{12,4},{14,6},{1,9},{3,11}... | collective-permute-start | bytes 417800 | tf_op jit(solution)/shard_map/ppermute | solution.py:309
  92.7 0.7 copy-start.3
  92.7 15.0 %collective-permute-start.10 = (bf16[272,256]{1,0:T(8,128)(2,1)}, bf16[272,256]{1,0:T(8,128)(2,1)S(1)}, u32[]{:S(2)}, u32[]{:S(2)}) collective-permute-start(bf16[272,256]{1,0:T(8,128)(2,1)} %get-tuple-element.17), channel_id=1, source_target_pairs={{0,4},{2,6},{4,8},{6,10},{8,12},{10,14},{12,0},{14,2},{1,5},{3,7},... | collective-permute-start | bytes 417800 | tf_op jit(solution)/shard_map/ppermute | solution.py:309
  92.7 1.1 copy-start.13
  93.8 1.0 copy-start.14
  94.8 0.9 copy-start.17
  95.9 0.7 copy-start.10
  96.0 0.7 copy-start.9
  106.6 1.1 copy-start.4
  106.6 1.1 copy-start.6
  106.6 1.1 copy-start.7
where the time goes:
time: 112 us; the launch traced here: 110 us
  waiting for transfers between devices  38.2 us (34%)
  starting transfers between devices  27.8 us (25%)
  Pallas kernels  21.1 us (19%)
  between operations  11.5 us (10%)
  local copies, waits for them, and re-layouts  8.62 us (8%)
  other arithmetic  3.2 us (3%)
    ppermute x12, starting transfers between devices, turn(): lax.ppermute(value, axis, [(s, (s + k * pair) % size) for s in range(size)])  20.7 us
    ppermute x12, waiting for transfers between devices, turn(): lax.ppermute(value, axis, [(s, (s + k * pair) % size) for s in range(size)])  16.1 us
    ppermute x3, waiting for transfers between devices, across(): return lax.ppermute(value, axis, [(s, s ^ 1) for s in range(size)])  15.6 us
    pallas_call x1, Pallas kernels, local(): call(functools.partial(scan_body, state), jax.ShapeDtypeStruct((2, length...  9.9 us
    unnamed x55, local copies, waits for them, and re-layouts  6.83 us
    ppermute x2, waiting for transfers between devices, local(): lax.ppermute(state0, axis, [(s, (s // pair ^ hop) * pair + s % pair) for...  6.44 us
    ppermute x3, starting transfers between devices, across(): return lax.ppermute(value, axis, [(s, s ^ 1) for s in range(size)])  6.07 us
    pallas_call x1, Pallas kernels, local(): call(functools.partial(blocks_body, heads, spans, slots, pair), [part_sha...  4.96 us
  transfers between devices with their start and end apart: 18, of which 7 were waited for; matrix products, arithmetic and copies ran while one was open for 5% of the time, Pallas kernels for 17%

commit v1 on v0

--- a/solution.py
+++ b/solution.py
@@ -63,17 +63,17 @@
     return top, total
 
 
-def prefix_body(heads, spans, *refs):
-    info, own, nbr = refs[:3]
-    qs = refs[3 : 3 + spans]
-    outs = refs[3 + spans : 3 + 2 * spans]
-    kv = refs[3 + 2 * spans]
-    here, mine = info[0], info[1]
+def prefix_body(heads, spans, pair, *refs):
+    me, owner, own, nbr = refs[:4]
+    qs = refs[4 : 4 + spans]
+    outs = refs[4 + spans : 4 + 2 * spans]
+    kv = refs[4 + 2 * spans]
+    here = owner[0] // pair == me[0] // pair
     rows = heads * HD
 
-    @pl.when(here == 1)
+    @pl.when(here)
     def _():
-        kv[...] = jnp.where(mine == 1, own[...], nbr[...])
+        kv[...] = jnp.where(owner[0] == me[0], own[...], nbr[...])
         for q, out in zip(qs, outs):
             wide = Q_PER_KV * (q.shape[0] - STAT) // (2 * heads * Q_PER_KV)
             stats = []
@@ -88,7 +88,7 @@
                 stats += pieces(m, 3) + pieces(l, 2)
             out[rows:, :] = stat_block(stats, wide)
 
-    @pl.when(here != 1)
+    @pl.when(jnp.logical_not(here))
     def _():
         for q, out in zip(qs, outs):
             wide = out.shape[1]
@@ -98,56 +98,51 @@
             out[rows:, :] = stat_block((pieces(low, 3) + [zero, zero]) * heads, wide)
 
 
-def blocks_body(heads, spans, slots, pair, *refs):
-    info, src, blk, own, nbr = refs[:5]
+def blocks_body(head, spans, slots, pair, *refs):
+    me, src, blk, own, nbr = refs[:5]
     qs = refs[5 : 5 + spans]
     outs = refs[5 + spans : 5 + 2 * spans]
     acc, top, tot = refs[5 + 2 * spans :]
-    z, y = info[0], info[1]
-    rows = heads * HD
+    z, y = me[0] // pair, lax.rem(me[0], pair)
     for k, (q, out) in enumerate(zip(qs, outs)):
-        half = q.shape[0] - STAT
-        wide = half // (2 * heads)
+        full = q.shape[0] - STAT
+        wide = out.shape[1]
+        lo = full // 2 + head * wide
         reader = lax.rem(z + (spans - k), spans) * pair + y
-        ctx = jnp.max(q[half:, :].astype(F32))
+        ctx = jnp.max(q[full:, :].astype(F32))
         acc[...] = jnp.zeros_like(acc)
         top[...] = jnp.full(top.shape, LOW, F32)
         tot[...] = jnp.zeros_like(tot)
 
-        def slot(j, carry, q=q, half=half, wide=wide, reader=reader, ctx=ctx):
+        def slot(j, carry, q=q, lo=lo, wide=wide, reader=reader, ctx=ctx):
             source = src[reader, j]
             live = (source // pair == z) & (j.astype(F32) < ctx)
 
             @pl.when(live)
             def _():
                 b = blk[reader, j]
-                kv = jnp.where(lax.rem(source, pair) == y, own[b], nbr[b])
-                for h in range(heads):
-                    lo = half // 2 + h * wide
-                    s = dot(kv[:, 2 * h * HD : (2 * h + 1) * HD], q[lo : lo + wide, :], 1, 1)
-                    old = top[h]
-                    m = jnp.maximum(old, jnp.max(s, axis=0, keepdims=True))
-                    p = jnp.exp2((s - m) * SCORE2)
-                    fade = jnp.exp2((old - m) * SCORE2)
-                    o = dot(kv[:, (2 * h + 1) * HD : (2 * h + 2) * HD], p.astype(BF16), 0, 0)
-                    acc[h] = acc[h] * fade + o
-                    tot[h] = tot[h] * fade + jnp.sum(p, axis=0, keepdims=True)
-                    top[h] = m
+                kv = jnp.where(lax.rem(source, pair) == y, own[b, :, 2 * head * HD : 2 * (head + 1) * HD], nbr[b])
+                s = dot(kv[:, :HD], q[lo : lo + wide, :], 1, 1)
+                old = top[...]
+                m = jnp.maximum(old, jnp.max(s, axis=0, keepdims=True))
+                p = jnp.exp2((s - m) * SCORE2)
+                fade = jnp.exp2((old - m) * SCORE2)
+                o = dot(kv[:, HD:], p.astype(BF16), 0, 0)
+                acc[...] = acc[...] * fade + o
+                tot[...] = tot[...] * fade + jnp.sum(p, axis=0, keepdims=True)
+                top[...] = m
 
             return carry
 
         lax.fori_loop(0, slots, slot, 0)
-        stats = []
-        for h in range(heads):
-            out[h * HD : (h + 1) * HD, :] = acc[h].astype(BF16)
-            stats += pieces(top[h], 3) + pieces(tot[h], 2)
-        out[rows:, :] = stat_block(stats, wide)
+        out[:HD, :] = acc[...].astype(BF16)
+        out[HD:, :] = stat_block(pieces(top[...], 3) + pieces(tot[...], 2), wide)
 
 
 def join_body(heads, spans, *refs):
     flag, q, new = refs[:3]
-    parts = (refs[3 : 3 + spans], refs[3 + spans : 3 + 2 * spans])
-    out = refs[3 + 2 * spans]
+    parts = [refs[3 + i * spans : 3 + (i + 1) * spans] for i in range(1 + heads)]
+    out = refs[3 + (1 + heads) * spans]
     fresh = new.shape[1]
     half = q.shape[0] - STAT
     wide = half // (2 * heads)
@@ -161,7 +156,8 @@
             seen = key <= token
             s = jnp.where(seen, s, LOW)
             best = jnp.max(s, axis=0, keepdims=True)
-            stats = [stats_of(part, rows, h) for part in parts[r]]
+            mine, at, base, place = (parts[0], h * HD, rows, h) if r == 0 else (parts[1 + h], 0, HD, 0)
+            stats = [stats_of(part, base, place) for part in mine]
             if r == 0:
                 stats = [(jnp.where(flag[0] > 0, m, LOW), l) for m, l in stats]
             for m, _ in stats:
@@ -169,30 +165,70 @@
             p = jnp.where(seen, jnp.exp2((s - best) * SCORE2), 0.0)
             total = jnp.sum(p, axis=0, keepdims=True)
             o = dot(new[r, :, (2 * h + 1) * HD : (2 * h + 2) * HD], p.astype(BF16), 0, 0)
-            for part, (m, l) in zip(parts[r], stats):
+            for part, (m, l) in zip(mine, stats):
                 w = jnp.exp2((m - best) * SCORE2)
                 total = total + w * l
-                o = o + w * part[h * HD : (h + 1) * HD, :].astype(F32)
+                o = o + w * part[at : at + HD, :].astype(F32)
             done = jnp.transpose(o / total).astype(BF16)
             for g in range(Q_PER_KV):
                 col = (h * Q_PER_KV + g) * HD
                 out[r, :, col : col + HD] = done[g * fresh : (g + 1) * fresh, :]
 
 
+def reach(away, spans, rounds, here):
+    low = high = away
+    for r in range(rounds):
+        odd = r % 2
+        below = jnp.where((lax.rem(low, 2) != odd) & (low > 0), low - 1, low)
+        above = jnp.where((lax.rem(high, 2) == odd) & (high < spans - 1), high + 1, high)
+        low, high = below, above
+    return (low <= here) & (here <= high)
+
+
+def shared_body(spans, pair, unit, rounds, me, owner, kept, came, out):
+    z, y = me[0] // pair, lax.rem(me[0], pair)
+    if rounds == 0:
+        take = lax.rem(owner[0], pair) != y
+        base = unit
+    else:
+        away = owner[0] // pair
+        take = jnp.logical_not(reach(away, spans, rounds - 1, z))
+        base = 0
+    out[...] = jnp.where(take, came[base:, :], kept[base:, :])
+
+
+def state_send_body(spans, pair, unit, me, src, own, nbr, *outs):
+    z, y = me[0] // pair, lax.rem(me[0], pair)
+    for k, out in enumerate(outs):
+        source = src[lax.rem(z + k, spans) * pair + y]
+        out[...] = jnp.where(lax.rem(source, pair) == y, own[:unit, :], nbr[:unit, :])
+
+
+def state_take_body(spans, pair, me, src, *refs):
+    came, out = refs[:spans], refs[spans]
+    z = me[0] // pair
+    k1 = lax.rem(z + spans - src[me[0]] // pair, spans)
+    for k in range(spans):
+
+        @pl.when(k1 == k)
+        def _(k=k):
+            out[...] = came[k][...]
+
+
 def silu(x):
     return x / (1.0 + jnp.exp(-x))
 
 
-def gains_body(state, chunk, flag, st0, st1, x, w, b, wbc, out, pad):
+def gains_body(chunk, flag, st0, st1, x, w, b, wbc, out, pad):
     taps = w.shape[0]
     keep = taps - 1
     length = x.shape[1]
     lead = 8
-    total = [jnp.zeros((length, wbc.shape[1]), F32) for _ in range(2)]
+    total = [jnp.zeros((length, wbc.shape[0]), F32) for _ in range(2)]
     for c in range(0, x.shape[2], chunk):
         at = slice(c, c + chunk)
         for r, st in enumerate((st0, st1)):
-            first = st[state : state + keep, at].astype(F32)
+            first = st[:, at].astype(F32)
             if r == 0:
                 first = jnp.where(flag[0] > 0, first, 0.0)
             pad[r, lead - keep : lead, :] = first
@@ -200,7 +236,7 @@
             acc = b[:, at] + w[0:1, at] * pad[r, lead - keep : lead - keep + length, :]
             for k in range(1, taps):
                 acc = acc + w[k : k + 1, at] * pad[r, lead - keep + k : lead - keep + k + length, :]
-            total[r] = total[r] + dot(silu(acc).astype(BF16), wbc[at, :], 1, 0)
+            total[r] = total[r] + dot(silu(acc).astype(BF16), wbc[:, at], 1, 1)
     for r in range(2):
         out[r] = total[r]
 
@@ -298,9 +334,7 @@
     inner = mamba_x.shape[3]
     state = a_log.shape[0]
     keep = prefix_conv.shape[1]
-    me = lax.axis_index(axis)
-    z, y = me // pair, me % pair
-    owner = owner_id[0]
+    me = lax.axis_index(axis)[None]
 
     def across(value):
         return lax.ppermute(value, axis, [(s, s ^ 1) for s in range(size)])
@@ -308,7 +342,19 @@
     def turn(value, k):
         return lax.ppermute(value, axis, [(s, (s + k * pair) % size) for s in range(size)])
 
+    def after(value, *others):
+        return lax.optimization_barrier((value, *others))[0]
+
+    sub = inner // HD
+
+    def tiled(value):
+        return value.reshape(value.shape[:-1] + (sub, HD))
+
+    cols = 2 * HD
+    rows = state + keep
+    unit = rows * inner // cols
     states = jnp.concatenate([pool_ssm[0], pool_conv[0], prefix_ssm[0], prefix_conv[0]], axis=0)
+    states = states.reshape(2 * unit, cols)
     states_nbr = across(states)
 
     folded = queries[0].reshape(2, length, heads * Q_PER_KV, HD).transpose(0, 2, 1, 3)
@@ -317,74 +363,87 @@
     message = jnp.concatenate([folded, length_rows], axis=0)
     asked = [message] + [turn(message, k) for k in range(1, spans)]
 
+    x_t, dt_t, z_t = tiled(mamba_x[0]), tiled(mamba_dt[0]), tiled(mamba_z[0])
+    halves = [pool_kv[0, :, :, h * cols : (h + 1) * cols] for h in range(heads)]
     prefix_nbr = across(cached_lookup_pairs[0])
-    pool_nbr = across(pool_kv[0])
-
+
+    one = jax.ShapeDtypeStruct((unit, cols), BF16)
+
+    def shared(rounds, kept, came):
+        return call(
+            functools.partial(shared_body, spans, pair, unit, rounds),
+            one,
+            [SSPEC] * 2 + [VSPEC] * 2,
+        )(me, owner_id, kept, came)
+
+    def hop(value, r):
+        odd = r % 2
+        near = [(i, i + 1) for i in range(odd, spans - 1, 2)]
+        links = [(pair * u + j, pair * v + j) for i, n in near for u, v in ((i, n), (n, i)) for j in range(pair)]
+        return lax.ppermute(value, axis, links)
+
+    state0 = shared(0, states, states_nbr)
+    hops = [hop(state0, 0)] if spans > 1 else []
+
+    sent = call(
+        functools.partial(state_send_body, spans, pair, unit),
+        [one] * spans,
+        [SSPEC] * 2 + [VSPEC] * 2,
+        (),
+        pl.CostEstimate(flops=50 * 10**9, bytes_accessed=150 * 10**6, transcendentals=0),
+    )(after(me, x_t, dt_t, z_t, *halves, *asked[1:], *hops[:1]), state_src, states, states_nbr)
+    came = [sent[0]] + [turn(sent[k], k) for k in range(1, spans)]
+    state1 = call(
+        functools.partial(state_take_body, spans, pair),
+        one,
+        [SSPEC] * 2 + [VSPEC] * spans,
+    )(me, state_src, *came)
     part_shape = jax.ShapeDtypeStruct((heads * HD + STAT, wide), BF16)
-    info0 = jnp.stack([(owner // pair == z), (owner % pair == y)]).astype(jnp.int32)
     keys = cached_lookup_pairs.shape[1]
     part0 = call(
-        functools.partial(prefix_body, heads, spans),
+        functools.partial(prefix_body, heads, spans, pair),
         [part_shape] * spans,
-        [SSPEC] + [VSPEC] * (2 + spans),
+        [SSPEC] * 2 + [VSPEC] * (2 + spans),
         [pltpu.VMEM(cached_lookup_pairs.shape[1:], BF16)],
-        pl.CostEstimate(flops=spans * heads * keys * wide * HD * 4, bytes_accessed=4 << 20, transcendentals=spans * heads * keys * wide),
-    )(info0, cached_lookup_pairs[0], prefix_nbr, *asked)
+        pl.CostEstimate(flops=50 * 10**9, bytes_accessed=150 * 10**6, transcendentals=0),
+    )(me, owner_id, cached_lookup_pairs[0], prefix_nbr, *asked)
+    for r in range(1, spans):
+        state0 = shared(r, state0, hops[-1])
+        if r < spans - 1:
+            hops.append(hop(after(state0, part0[0]), r))
     got0 = [part0[0]] + [turn(part0[k], spans - k) for k in range(1, spans)]
 
-    info1 = jnp.stack([z, y]).astype(jnp.int32)
     block_len = pool_kv.shape[2]
-    part1 = call(
-        functools.partial(blocks_body, heads, spans, slots, pair),
-        [part_shape] * spans,
-        [SSPEC] * 3 + [VSPEC] * (2 + spans),
-        [
-            pltpu.VMEM((heads, HD, wide), F32),
-            pltpu.VMEM((heads, 1, wide), F32),
-            pltpu.VMEM((heads, 1, wide), F32),
-        ],
-        pl.CostEstimate(flops=slots * heads * block_len * wide * HD * 4, bytes_accessed=4 << 20, transcendentals=slots * heads * block_len * wide),
-    )(info1, restore_src, restore_blk, pool_kv[0], pool_nbr, *asked)
-    got1 = [part1[0]] + [turn(part1[k], spans - k) for k in range(1, spans)]
-
-    rows = state + keep
-
-    def stored(holder):
-        return jnp.where(holder % pair == y, states[:rows], states_nbr[:rows])
-
-    back = [stored(state_src[me])]
-    for k in range(1, spans):
-        reader = ((z + k) % spans) * pair + y
-        back.append(turn(stored(state_src[reader]), k))
-    came = (z - state_src[me] // pair) % spans
-    state1 = back[0]
-    for k in range(1, spans):
-        state1 = jnp.where(came == k, back[k], state1)
-    state0 = jnp.where(owner % pair == y, states[rows:], states_nbr[rows:])
-    away = owner // pair
-    hop = 1
-    while hop < spans:
-        other = lax.ppermute(
-            state0, axis, [(s, ((s // pair) ^ hop) * pair + s % pair) for s in range(size)]
-        )
-        state0 = jnp.where((away ^ z) & hop != 0, other, state0)
-        hop *= 2
+    head_shape = jax.ShapeDtypeStruct((HD + STAT, wide), BF16)
+    got1 = []
+    last = [sent[0]]
+    for h in range(heads):
+        pool_nbr = across(after(halves[h], *last))
+        last = [pool_nbr, part0[0]]
+        part1 = call(
+            functools.partial(blocks_body, h, spans, slots, pair),
+            [head_shape] * spans,
+            [SSPEC] * 3 + [VSPEC] * (2 + spans),
+            [pltpu.VMEM((HD, wide), F32), pltpu.VMEM((1, wide), F32), pltpu.VMEM((1, wide), F32)],
+            pl.CostEstimate(flops=20 * 10**9, bytes_accessed=60 * 10**6, transcendentals=0),
+        )(after(me, part0[0], *(got0[1:] if h else ())), restore_src, restore_blk, pool_kv[0], pool_nbr, *asked)
+        got1 += [part1[0]] + [turn(part1[k], spans - k) for k in range(1, spans)]
+
+    first = state * inner // cols
+
+    def taps_of(value):
+        return value[first:].reshape(keep, inner)
 
     chunk = math.gcd(inner, 512)
     partial = call(
-        functools.partial(gains_body, state, chunk),
+        functools.partial(gains_body, chunk),
         jax.ShapeDtypeStruct((2, length, w_bc.shape[1]), F32),
         [SSPEC] + [VSPEC] * 6,
         [pltpu.VMEM((2, length + 8, chunk), F32)],
         pl.CostEstimate(flops=2 * 2 * length * inner * 32, bytes_accessed=2 << 20, transcendentals=2 * length * inner),
-    )(readers, state0, state1, mamba_x[0], conv_w, conv_b[None], w_bc)
+    )(readers, taps_of(state0), taps_of(state1), mamba_x[0], conv_w, conv_b[None], w_bc.T)
     both = partial + lax.ppermute(partial, "channel", [(0, 1), (1, 0)])
     bc = both.reshape(2 * length, w_bc.shape[1])
-    sub = inner // HD
-
-    def tiled(value):
-        return value.reshape(value.shape[:-1] + (sub, HD))
-
     scan_out = call(
         functools.partial(scan_body, state),
         jax.ShapeDtypeStruct((2, length, sub, HD), BF16),
@@ -400,11 +459,11 @@
     )(
         readers,
         bc,
-        tiled(state0),
-        tiled(state1),
-        tiled(mamba_x[0]),
-        tiled(mamba_dt[0]),
-        tiled(mamba_z[0]),
+        state0.reshape(rows, sub, HD),
+        state1.reshape(rows, sub, HD),
+        x_t,
+        dt_t,
+        z_t,
         tiled(dt_bias),
         tiled(a_log),
         tiled(bypass_gain),
@@ -416,7 +475,7 @@
     attention_out = call(
         functools.partial(join_body, heads, spans),
         jax.ShapeDtypeStruct((2, length, heads * Q_PER_KV * HD), BF16),
-        [SSPEC] + [VSPEC] * (2 + 2 * spans),
+        [SSPEC] + [VSPEC] * (2 + (1 + heads) * spans),
         (),
         pl.CostEstimate(flops=1 << 24, bytes_accessed=2 << 20, transcendentals=1 << 16),
     )(readers, message, new_kv[0], *got0, *got1)[None]

time: 112 us -> 102 us (0.911)
  waiting for transfers between devices: 38.2 us -> 15.5 us
  local copies, waits for them, and re-layouts: 8.62 us -> 17.9 us
  Pallas kernels: 21.1 us -> 30.1 us
  between operations: 11.5 us -> 3.13 us
  starting transfers between devices: 27.8 us -> 32.8 us
  other arithmetic: 3.2 us -> 1.09 us
    ppermute x3 -> x4, waiting for transfers between devices: 15.6 us -> 0.01 us  [across(): return lax.ppermute(value, axis, [(s, s ^ 1) for s in range(size)])]
    pallas_call x3 -> x10, Pallas kernels: 8.57 us -> 17.6 us  [the longest x1 7.45 us: local(): call(functools.partial(prefix_body, heads, spans, pair), [part_shape] * s...]
    unnamed x55 -> x90, local copies, waits for them, and re-layouts: 6.83 us -> 12.9 us
    ppermute x12 -> x15, waiting for transfers between devices: 16.1 us -> 12.4 us  [turn(): lax.ppermute(value, axis, [(s, (s + k * pair) % size) for s in range(size)])]
    ppermute x2 -> x3, starting transfers between devices: 0.94 us -> 4.52 us  [hop(): return lax.ppermute(value, axis, links)]
    ppermute x2 -> x3, waiting for transfers between devices: 6.44 us -> 3.05 us  [hop(): return lax.ppermute(value, axis, links)]
    reshape x2 -> x5, local copies, waits for them, and re-layouts: 0.02 us -> 2.28 us  [the longest x2 1.97 us: taps_of(): return value[first:].reshape(keep, inner)]
    select_n x4 -> x0, other arithmetic: 1.95 us -> none  [the longest x2 1.65 us: local(): state0 = jnp.where((away ^ z) & hop != 0, other, state0)]
  transfers between devices with their start and end apart: 18 -> 23, of which waited for: 7 -> 3; matrix products, arithmetic and copies ran while one was open for 5% -> 6% of each run, Pallas kernels for 17% -> 27%
where the time goes in v1:
time: 102 us; the launch traced here: 100 us
  starting transfers between devices  32.8 us (32%)
  Pallas kernels  30.1 us (30%)
  local copies, waits for them, and re-layouts  17.9 us (18%)
  waiting for transfers between devices  15.5 us (15%)
  between operations  3.13 us (3%)
  other arithmetic  1.09 us (1%)
    ppermute x15, starting transfers between devices, turn(): lax.ppermute(value, axis, [(s, (s + k * pair) % size) for s in range(size)])  22.5 us
    unnamed x90, local copies, waits for them, and re-layouts  12.9 us
    ppermute x15, waiting for transfers between devices, turn(): lax.ppermute(value, axis, [(s, (s + k * pair) % size) for s in range(size)])  12.4 us
    pallas_call x1, Pallas kernels, local(): call(functools.partial(scan_body, state), jax.ShapeDtypeStruct((2, length...  9.8 us
    pallas_call x1, Pallas kernels, local(): call(functools.partial(prefix_body, heads, spans, pair), [part_shape] * s...  7.45 us
    pallas_call x2, Pallas kernels, local(): call(functools.partial(blocks_body, h, spans, slots, pair), [head_shape]...  6.47 us
    ppermute x4, starting transfers between devices, across(): return lax.ppermute(value, axis, [(s, s ^ 1) for s in range(size)])  5.72 us
    ppermute x3, starting transfers between devices, hop(): return lax.ppermute(value, axis, links)  4.52 us
  transfers between devices with their start and end apart: 23, of which 3 were waited for; matrix products, arithmetic and copies ran while one was open for 6% of the time, Pallas kernels for 27%

profile of v1, /device:TPU:0, one launch (start us, length us, event | category | flops | bytes accessed | tf_op | source)
XLA Modules:
  0.0 100.5 jit_solution(5161687589161520669)
XLA Ops:
  0.6 1.1 %pad_maximum_fusion = bf16[38,4096]{1,0:T(8,128)(2,1)S(1)} fusion(bf16[3,4096]{1,0:T(4,128)(2,1)} %bitcast.78, bf16[16,4096]{1,0:T(8,128)(2,1)} %bitcast.76, bf16[3,4096]{1,0:T(4,128)(2,1)} %bitcast.79, bf16[16,4096]{1,0:T(8,128)(2,1)} %bitcast.77), kind=kLoop, calls=%fused_computation.2 | loop fusion | flops 1245184 | bytes 622592 | tf_op jit(solution)/shard_map/concatenate | solution.py:356
  1.9 3.0 %collective-permute-start.7 = (bf16[608,256]{1,0:T(8,128)(2,1)S(1)}, bf16[608,256]{1,0:T(8,128)(2,1)S(1)}, u32[]{:S(2)}, u32[]{:S(2)}) collective-permute-start(bf16[608,256]{1,0:T(8,128)(2,1)S(1)} %reshape.45.kept.own), channel_id=1, source_target_pairs={{0,2},{2,0},{4,6},{6,4},{8,10},{10,8},{12,14},{14,12},{1,3},{3,1},... | collective-permute-start | bytes 933896 | tf_op jit(solution)/shard_map/ppermute | solution.py:340
  5.8 1.6 %collective-permute-start.1 = (bf16[1040,128]{1,0:T(8,128)(2,1)S(1)}, bf16[1040,128]{1,0:T(8,128)(2,1)}, u32[]{:S(2)}, u32[]{:S(2)}) collective-permute-start(bf16[1040,128]{1,0:T(8,128)(2,1)S(1)} %concatenate.6.refs_4_.refs_5_.refs_1_), channel_id=1, source_target_pairs={{0,4},{2,6},{4,8},{6,10},{8,12},{10,14},{12,0},{14,2},{1,5},{3,7},... | collective-permute-start | bytes 798728 | tf_op jit(solution)/shard_map/ppermute | solution.py:343
  7.5 2.6 %collective-permute-start.2 = (bf16[1040,128]{1,0:T(8,128)(2,1)S(1)}, bf16[1040,128]{1,0:T(8,128)(2,1)}, u32[]{:S(2)}, u32[]{:S(2)}) collective-permute-start(bf16[1040,128]{1,0:T(8,128)(2,1)S(1)} %concatenate.6.refs_4_.refs_5_.refs_1_), channel_id=1, source_target_pairs={{0,8},{2,10},{4,12},{6,14},{8,0},{10,2},{12,4},{14,6},{1,9},{3,11}... | collective-permute-start | bytes 798728 | tf_op jit(solution)/shard_map/ppermute | solution.py:343
  10.0 1.3 %collective-permute-start.3 = (bf16[1040,128]{1,0:T(8,128)(2,1)S(1)}, bf16[1040,128]{1,0:T(8,128)(2,1)}, u32[]{:S(2)}, u32[]{:S(2)}) collective-permute-start(bf16[1040,128]{1,0:T(8,128)(2,1)S(1)} %concatenate.6.refs_4_.refs_5_.refs_1_), channel_id=1, source_target_pairs={{0,12},{2,14},{4,0},{6,2},{8,4},{10,6},{12,8},{14,10},{1,13},{3,15... | collective-permute-start | bytes 798728 | tf_op jit(solution)/shard_map/ppermute | solution.py:343
  11.4 0.7 collective-permute-start
  12.8 0.9 copy-done.33
  13.9 0.9 copy-done.34
  14.8 0.9 copy.33
  15.7 0.7 collective-permute-start.8
  16.5 1.0 %slice_bitcast_fusion = (bf16[4,256,256]{2,1,0:T(8,128)(2,1)}, bf16[4,256,256]{2,1,0:T(8,128)(2,1)}) fusion(bf16[1,4,256,512]{3,2,1,0:T(8,128)(2,1)S(1)} %copy-done.1), kind=kLoop, calls=%fused_computation | loop fusion | bytes 2097152 | tf_op jit(solution)/shard_map/squeeze | solution.py:367
  17.5 9.8 %collective-permute-done.2.refs_6_.refs_7_ = bf16[1040,128]{1,0:T(8,128)(2,1)} collective-permute-done((bf16[1040,128]{1,0:T(8,128)(2,1)S(1)}, bf16[1040,128]{1,0:T(8,128)(2,1)}, u32[]{:S(2)}, u32[]{:S(2)}) %collective-permute-start.2) | collective-permute-done | bytes 266272 | tf_op jit(solution)/shard_map/ppermute | solution.py:343
  27.3 3.0 %collective-permute-done.8.came = bf16[304,256]{1,0:T(8,128)(2,1)S(1)} collective-permute-done((bf16[304,256]{1,0:T(8,128)(2,1)S(1)}, bf16[304,256]{1,0:T(8,128)(2,1)S(1)}, u32[]{:S(2)}, u32[]{:S(2)}) %collective-permute-start.8) | collective-permute-done | bytes 155680 | tf_op jit(solution)/shard_map/ppermute | solution.py:383
  30.3 0.7 copy-done.27
  31.0 1.3 %shard_map.232 = (bf16[304,256]{1,0:T(8,128)(2,1)S(1)}, bf16[304,256]{1,0:T(8,128)(2,1)}, bf16[304,256]{1,0:T(8,128)(2,1)}, bf16[304,256]{1,0:T(8,128)(2,1)}) custom-call(s32[1]{0:T(128)} %bitcast.4.refs_0_.me, s32[8]{0:T(128)S(1)} %copy-done.27, bf16[608,256]{1,0:T(8,128)(2,1)S(1)} %reshape.45.kept.own, bf16[608,256]{1,0:T(8,128)(2,1)S(1)} %collective-permute-done.7.came.nbr), custom_call_target="tpu_custom_call" | custom-call | flops 49999998976 | bytes 150000000 | tf_op jit(solution)/shard_map/pallas_call | solution.py:388
  32.3 0.9 collective-permute-start.9
  33.3 3.1 %collective-permute-start.19 = (bf16[304,256]{1,0:T(8,128)(2,1)}, bf16[304,256]{1,0:T(8,128)(2,1)S(1)}, u32[]{:S(2)}, u32[]{:S(2)}) collective-permute-start(bf16[304,256]{1,0:T(8,128)(2,1)} %get-tuple-element.45), channel_id=1, source_target_pairs={{0,4},{2,6},{4,8},{6,10},{8,12},{10,14},{12,0},{14,2},{1,5},{3,7},... | collective-permute-start | bytes 466952 | tf_op jit(solution)/shard_map/ppermute | solution.py:343
  36.4 1.6 %collective-permute-start.20 = (bf16[304,256]{1,0:T(8,128)(2,1)}, bf16[304,256]{1,0:T(8,128)(2,1)}, u32[]{:S(2)}, u32[]{:S(2)}) collective-permute-start(bf16[304,256]{1,0:T(8,128)(2,1)} %get-tuple-element.46), channel_id=1, source_target_pairs={{0,8},{2,10},{4,12},{6,14},{8,0},{10,2},{12,4},{14,6},{1,9},{3,11}... | collective-permute-start | bytes 466952 | tf_op jit(solution)/shard_map/ppermute | solution.py:343
  38.0 0.8 collective-permute-start.21
  38.8 7.5 %shard_map.230 = (bf16[272,256]{1,0:T(8,128)(2,1)S(1)}, bf16[272,256]{1,0:T(8,128)(2,1)S(1)}, bf16[272,256]{1,0:T(8,128)(2,1)S(1)}, bf16[272,256]{1,0:T(8,128)(2,1)S(1)}) custom-call(s32[1]{0:T(128)} %bitcast.4.refs_0_.me, s32[1]{0:T(128)S(6)} %copy.38.refs_1_.owner, bf16[1024,512]{1,0:T(8,128)(2,1)} %bitcast.5.refs_2_, ...), custom_call_target="tpu_custom_call" | custom-call | flops 49999998976 | bytes 150000000 | tf_op jit(solution)/shard_map/pallas_call | solution.py:403
  46.3 0.6 copy-done.9
  47.0 0.7 copy-done.28
  47.6 0.8 collective-permute-start.17
  49.2 0.6 copy-done.40
  49.9 0.7 copy-done.7
  50.6 0.9 copy-done.8
  51.5 1.0 %shard_map.239 = bf16[304,256]{1,0:T(8,128)(2,1)S(1)} custom-call(s32[1]{0:T(128)} %bitcast.4.refs_0_.me, s32[8]{0:T(128)S(1)} %copy-done.27, bf16[304,256]{1,0:T(8,128)(2,1)S(1)} %copy-done.6, bf16[304,256]{1,0:T(8,128)(2,1)S(1)} %copy-done.8, bf16[304,256]{1,0:T(8,128)(2,1)} %collective-permute-done.20.refs_2_, ...), custom_call_target="tpu_custom_call" | custom-call | tf_op jit(solution)/shard_map/pallas_call | solution.py:396
  52.5 0.6 reshape.47.st1
  53.1 3.4 %collective-permute-start.4 = (bf16[272,256]{1,0:T(8,128)(2,1)}, bf16[272,256]{1,0:T(8,128)(2,1)S(1)}, u32[]{:S(2)}, u32[]{:S(2)}) collective-permute-start(bf16[272,256]{1,0:T(8,128)(2,1)} %copy-done.30), channel_id=1, source_target_pairs={{0,12},{2,14},{4,0},{6,2},{8,4},{10,6},{12,8},{14,10},{1,13},{3,15... | collective-permute-start | bytes 417800 | tf_op jit(solution)/shard_map/ppermute | solution.py:343
  57.1 1.1 %collective-permute-start.13 = (bf16[4,256,256]{2,1,0:T(8,128)(2,1)}, bf16[4,256,256]{2,1,0:T(8,128)(2,1)}, u32[]{:S(2)}, u32[]{:S(2)}) collective-permute-start(bf16[4,256,256]{2,1,0:T(8,128)(2,1)} %get-tuple-element.38), channel_id=1, source_target_pairs={{0,2},{2,0},{4,6},{6,4},{8,10},{10,8},{12,14},{14,12},{1,3},{3,1},... | collective-permute-start | bytes 1572872 | tf_op jit(solution)/shard_map/ppermute | solution.py:340
  58.2 3.0 %collective-permute-start.18 = (bf16[304,256]{1,0:T(8,128)(2,1)S(1)}, bf16[304,256]{1,0:T(8,128)(2,1)S(1)}, u32[]{:S(2)}, u32[]{:S(2)}) collective-permute-start(bf16[304,256]{1,0:T(8,128)(2,1)S(1)} %shard_map.237.kept), channel_id=1, source_target_pairs={{0,4},{2,6},{4,0},{6,2},{8,12},{10,14},{12,8},{14,10},{1,5},{3,7},... | collective-permute-start | bytes 466952 | tf_op jit(solution)/shard_map/ppermute | solution.py:383
  61.2 3.2 %shard_map.233 = (bf16[144,256]{1,0:T(8,128)(2,1)S(1)}, bf16[144,256]{1,0:T(8,128)(2,1)}, bf16[144,256]{1,0:T(8,128)(2,1)}, bf16[144,256]{1,0:T(8,128)(2,1)}) custom-call(s32[1]{0:T(128)} %bitcast.4.refs_0_.me, s32[8,4]{1,0:T(8,128)S(1)} %copy.26.refs_1_, s32[8,4]{1,0:T(8,128)S(1)} %copy.27.refs_2_, bf16[4,256,512]{2,1,0:T(8,128)(2,1)S(1)} %bitcast.54, ...), custom_call_target="tpu_custom_call" | custom-call | flops 20000000000 | bytes 60000000 | tf_op jit(solution)/shard_map/pallas_call | solution.py:423
  64.5 0.6 copy-done.21
  65.1 0.7 copy-done.11
  65.8 1.7 %collective-permute-start.10 = (bf16[144,256]{1,0:T(8,128)(2,1)}, bf16[144,256]{1,0:T(8,128)(2,1)}, u32[]{:S(2)}, u32[]{:S(2)}) collective-permute-start(bf16[144,256]{1,0:T(8,128)(2,1)} %get-tuple-element.34), channel_id=1, source_target_pairs={{0,12},{2,14},{4,0},{6,2},{8,4},{10,6},{12,8},{14,10},{1,13},{3,15... | collective-permute-start | bytes 221192 | tf_op jit(solution)/shard_map/ppermute | solution.py:343
  67.5 2.6 %collective-permute-done.5.refs_5_ = bf16[272,256]{1,0:T(8,128)(2,1)S(1)} collective-permute-done((bf16[272,256]{1,0:T(8,128)(2,1)}, bf16[272,256]{1,0:T(8,128)(2,1)S(1)}, u32[]{:S(2)}, u32[]{:S(2)}) %collective-permute-start.5) | collective-permute-done | bytes 139296 | tf_op jit(solution)/shard_map/ppermute | solution.py:343
  70.8 0.6 slice.16
  71.4 1.4 %reshape.46.st0 = bf16[3,4096]{1,0:T(4,128)(2,1)} reshape(bf16[48,256]{1,0:T(8,128)(2,1)} %slice.16) | data formatting | bytes 49152 | tf_op jit(solution)/shard_map/reshape | solution.py:435
  72.8 0.7 copy-done.17
  73.6 0.8 copy-done.20
  74.3 1.2 %shard_map.240 = f32[2,32,32]{2,1,0:T(8,128)S(1)} custom-call(s32[1]{0:T(128)S(6)} %copy.39.refs_0_.flag, bf16[3,4096]{1,0:T(4,128)(2,1)S(1)} %copy-done.20, bf16[3,4096]{1,0:T(4,128)(2,1)S(1)} %copy-done.17, bf16[2,32,4096]{2,1,0:T(8,128)(2,1)S(1)} %bitcast.53, f32[4,4096]{1,0:T(4,128)S(1)} %copy-done.4, f32[1,4096]{1,0:T(1,128)S(1)} %bitcast.65, ...), custom_call_target="tpu_custom_call" | custom-call | flops 16777216 | bytes 2097152 | tf_op jit(solution)/shard_map/pallas_call | solution.py:438
  75.6 3.2 %shard_map.234 = (bf16[144,256]{1,0:T(8,128)(2,1)S(1)}, bf16[144,256]{1,0:T(8,128)(2,1)}, bf16[144,256]{1,0:T(8,128)(2,1)}, bf16[144,256]{1,0:T(8,128)(2,1)}) custom-call(s32[1]{0:T(128)} %bitcast.4.refs_0_.me, s32[8,4]{1,0:T(8,128)S(1)} %copy.26.refs_1_, s32[8,4]{1,0:T(8,128)S(1)} %copy.27.refs_2_, bf16[4,256,512]{2,1,0:T(8,128)(2,1)S(1)} %bitcast.55, ...), custom_call_target="tpu_custom_call" | custom-call | flops 20000000000 | bytes 60000000 | tf_op jit(solution)/shard_map/pallas_call | solution.py:423
  78.9 4.2 %collective-permute-start.14 = (bf16[144,256]{1,0:T(8,128)(2,1)}, bf16[144,256]{1,0:T(8,128)(2,1)S(1)}, u32[]{:S(2)}, u32[]{:S(2)}) collective-permute-start(bf16[144,256]{1,0:T(8,128)(2,1)} %get-tuple-element.40), channel_id=1, source_target_pairs={{0,12},{2,14},{4,0},{6,2},{8,4},{10,6},{12,8},{14,10},{1,13},{3,15... | collective-permute-start | bytes 221192 | tf_op jit(solution)/shard_map/ppermute | solution.py:343
  83.0 1.5 %collective-permute-start.15 = (bf16[144,256]{1,0:T(8,128)(2,1)}, bf16[144,256]{1,0:T(8,128)(2,1)S(1)}, u32[]{:S(2)}, u32[]{:S(2)}) collective-permute-start(bf16[144,256]{1,0:T(8,128)(2,1)} %get-tuple-element.41), channel_id=1, source_target_pairs={{0,8},{2,10},{4,12},{6,14},{8,0},{10,2},{12,4},{14,6},{1,9},{3,11}... | collective-permute-start | bytes 221192 | tf_op jit(solution)/shard_map/ppermute | solution.py:343
  85.3 0.7 copy-done.19
  86.8 9.8 %shard_map.241 = bf16[2,32,32,128]{3,2,1,0:T(8,128)(2,1)S(1)} custom-call(s32[1]{0:T(128)S(6)} %copy.39.refs_0_.flag, f32[64,32]{1,0:T(8,128)S(1)} %bitcast.64, bf16[19,32,128]{2,1,0:T(8,128)(2,1)S(1)} %reshape.49.st0, bf16[19,32,128]{2,1,0:T(8,128)(2,1)S(1)} %reshape.50.st1, bf16[2,32,32,128]{3,2,1,0:T(8,128)(2,1)S(1)} %bitcast.56, ...), custom_call_target="tpu_custom_call" | custom-call | flops 25165824 | bytes 4194304 | tf_op jit(solution)/shard_map/pallas_call | solution.py:447
  96.7 1.0 %reshape.56 = bf16[1,2,32,4096]{3,2,1,0:T(8,128)(2,1)} reshape(bf16[2,32,32,128]{3,2,1,0:T(8,128)(2,1)S(1)} %shard_map.241) | data formatting | bytes 1048576 | tf_op jit(solution)/shard_map/reshape | solution.py:473
  97.8 2.7 %shard_map.235 = bf16[2,32,2048]{2,1,0:T(8,128)(2,1)} custom-call(s32[1]{0:T(128)S(6)} %copy.39.refs_0_.flag, bf16[1040,128]{1,0:T(8,128)(2,1)S(1)} %concatenate.6.refs_4_.refs_5_.refs_1_, bf16[2,32,512]{2,1,0:T(8,128)(2,1)S(1)} %bitcast.62, bf16[272,256]{1,0:T(8,128)(2,1)S(1)} %copy-done.10, bf16[272,256]{1,0:T(8,128)(2,1)S(1)} %copy-done.12, ...), custom_call_target="tpu_custom_call" | custom-call | flops 16777216 | bytes 2097152 | tf_op jit(solution)/shard_map/pallas_call | solution.py:475
  (113 shorter events, 3.7 us)
Async XLA Ops:
  1.7 3.3 %copy-start.35 = (bf16[1,2,32,2048]{3,2,1,0:T(8,128)(2,1)S(1)}, bf16[1,2,32,2048]{3,2,1,0:T(8,128)(2,1)}, u32[]{:S(2)}) copy-start(bf16[1,2,32,2048]{3,2,1,0:T(8,128)(2,1)} %param.23) | copy-start | bytes 786436
  1.9 13.8 %collective-permute-start.7 = (bf16[608,256]{1,0:T(8,128)(2,1)S(1)}, bf16[608,256]{1,0:T(8,128)(2,1)S(1)}, u32[]{:S(2)}, u32[]{:S(2)}) collective-permute-start(bf16[608,256]{1,0:T(8,128)(2,1)S(1)} %reshape.45.kept.own), channel_id=1, source_target_pairs={{0,2},{2,0},{4,6},{6,4},{8,10},{10,8},{12,14},{14,12},{1,3},{3,1},... | collective-permute-start | bytes 933896 | tf_op jit(solution)/shard_map/ppermute | solution.py:340
  5.0 7.7 %copy-start = (bf16[1,2,32,4096]{3,2,1,0:T(8,128)(2,1)S(1)}, bf16[1,2,32,4096]{3,2,1,0:T(8,128)(2,1)}, u32[]{:S(2)}) copy-start(bf16[1,2,32,4096]{3,2,1,0:T(8,128)(2,1)} %param.37) | copy-start | bytes 1572868
  5.8 11.7 %collective-permute-start.1 = (bf16[1040,128]{1,0:T(8,128)(2,1)S(1)}, bf16[1040,128]{1,0:T(8,128)(2,1)}, u32[]{:S(2)}, u32[]{:S(2)}) collective-permute-start(bf16[1040,128]{1,0:T(8,128)(2,1)S(1)} %concatenate.6.refs_4_.refs_5_.refs_1_), channel_id=1, source_target_pairs={{0,4},{2,6},{4,8},{6,10},{8,12},{10,14},{12,0},{14,2},{1,5},{3,7},... | collective-permute-start | bytes 798728 | tf_op jit(solution)/shard_map/ppermute | solution.py:343
  7.5 19.8 %collective-permute-start.2 = (bf16[1040,128]{1,0:T(8,128)(2,1)S(1)}, bf16[1040,128]{1,0:T(8,128)(2,1)}, u32[]{:S(2)}, u32[]{:S(2)}) collective-permute-start(bf16[1040,128]{1,0:T(8,128)(2,1)S(1)} %concatenate.6.refs_4_.refs_5_.refs_1_), channel_id=1, source_target_pairs={{0,8},{2,10},{4,12},{6,14},{8,0},{10,2},{12,4},{14,6},{1,9},{3,11}... | collective-permute-start | bytes 798728 | tf_op jit(solution)/shard_map/ppermute | solution.py:343
  10.0 17.3 %collective-permute-start.3 = (bf16[1040,128]{1,0:T(8,128)(2,1)S(1)}, bf16[1040,128]{1,0:T(8,128)(2,1)}, u32[]{:S(2)}, u32[]{:S(2)}) collective-permute-start(bf16[1040,128]{1,0:T(8,128)(2,1)S(1)} %concatenate.6.refs_4_.refs_5_.refs_1_), channel_id=1, source_target_pairs={{0,12},{2,14},{4,0},{6,2},{8,4},{10,6},{12,8},{14,10},{1,13},{3,15... | collective-permute-start | bytes 798728 | tf_op jit(solution)/shard_map/ppermute | solution.py:343
  11.4 27.4 %collective-permute-start = (bf16[1024,512]{1,0:T(8,128)(2,1)}, bf16[1024,512]{1,0:T(8,128)(2,1)}, u32[]{:S(2)}, u32[]{:S(2)}) collective-permute-start(bf16[1024,512]{1,0:T(8,128)(2,1)} %bitcast.5.refs_2_), channel_id=1, source_target_pairs={{0,2},{2,0},{4,6},{6,4},{8,10},{10,8},{12,14},{14,12},{1,3},{3,1},... | collective-permute-start | bytes 3145736 | tf_op jit(solution)/shard_map/ppermute | solution.py:340
  12.7 1.0 %copy-start.33 = (bf16[1,2,32,4096]{3,2,1,0:T(8,128)(2,1)S(1)}, bf16[1,2,32,4096]{3,2,1,0:T(8,128)(2,1)}, u32[]{:S(2)}) copy-start(bf16[1,2,32,4096]{3,2,1,0:T(8,128)(2,1)} %param.39) | copy-start | bytes 1572868
  13.8 1.0 %copy-start.34 = (bf16[1,2,32,4096]{3,2,1,0:T(8,128)(2,1)S(1)}, bf16[1,2,32,4096]{3,2,1,0:T(8,128)(2,1)}, u32[]{:S(2)}) copy-start(bf16[1,2,32,4096]{3,2,1,0:T(8,128)(2,1)} %param.38) | copy-start | bytes 1572868
  13.9 2.6 %copy-start.1 = (bf16[1,4,256,512]{3,2,1,0:T(8,128)(2,1)S(1)}, bf16[1,4,256,512]{3,2,1,0:T(8,128)(2,1)}, u32[]{:S(2)}) copy-start(bf16[1,4,256,512]{3,2,1,0:T(8,128)(2,1)} %param.28) | copy-start | bytes 3145732
  15.7 14.6 %collective-permute-start.8 = (bf16[304,256]{1,0:T(8,128)(2,1)S(1)}, bf16[304,256]{1,0:T(8,128)(2,1)S(1)}, u32[]{:S(2)}, u32[]{:S(2)}) collective-permute-start(bf16[304,256]{1,0:T(8,128)(2,1)S(1)} %shard_map.231.kept), channel_id=1, source_target_pairs={{0,4},{2,6},{4,0},{6,2},{8,12},{10,14},{12,8},{14,10},{1,5},{3,7},... | collective-permute-start | bytes 466952 | tf_op jit(solution)/shard_map/ppermute | solution.py:383
  32.3 6.5 %copy-start.5 = (bf16[304,256]{1,0:T(8,128)(2,1)}, bf16[304,256]{1,0:T(8,128)(2,1)S(1)}, u32[]{:S(2)}) copy-start(bf16[304,256]{1,0:T(8,128)(2,1)S(1)} %get-tuple-element.31.refs_0_) | copy-start | bytes 466948
  32.3 24.8 %collective-permute-start.9 = (bf16[4,256,256]{2,1,0:T(8,128)(2,1)}, bf16[4,256,256]{2,1,0:T(8,128)(2,1)}, u32[]{:S(2)}, u32[]{:S(2)}) collective-permute-start(bf16[4,256,256]{2,1,0:T(8,128)(2,1)} %get-tuple-element.32), channel_id=1, source_target_pairs={{0,2},{2,0},{4,6},{6,4},{8,10},{10,8},{12,14},{14,12},{1,3},{3,1},... | collective-permute-start | bytes 1572872 | tf_op jit(solution)/shard_map/ppermute | solution.py:340
  33.3 16.6 %collective-permute-start.19 = (bf16[304,256]{1,0:T(8,128)(2,1)}, bf16[304,256]{1,0:T(8,128)(2,1)S(1)}, u32[]{:S(2)}, u32[]{:S(2)}) collective-permute-start(bf16[304,256]{1,0:T(8,128)(2,1)} %get-tuple-element.45), channel_id=1, source_target_pairs={{0,4},{2,6},{4,8},{6,10},{8,12},{10,14},{12,0},{14,2},{1,5},{3,7},... | collective-permute-start | bytes 466952 | tf_op jit(solution)/shard_map/ppermute | solution.py:343
  36.4 14.1 %collective-permute-start.20 = (bf16[304,256]{1,0:T(8,128)(2,1)}, bf16[304,256]{1,0:T(8,128)(2,1)}, u32[]{:S(2)}, u32[]{:S(2)}) collective-permute-start(bf16[304,256]{1,0:T(8,128)(2,1)} %get-tuple-element.46), channel_id=1, source_target_pairs={{0,8},{2,10},{4,12},{6,14},{8,0},{10,2},{12,4},{14,6},{1,9},{3,11}... | collective-permute-start | bytes 466952 | tf_op jit(solution)/shard_map/ppermute | solution.py:343
  38.0 12.5 %collective-permute-start.21 = (bf16[304,256]{1,0:T(8,128)(2,1)}, bf16[304,256]{1,0:T(8,128)(2,1)}, u32[]{:S(2)}, u32[]{:S(2)}) collective-permute-start(bf16[304,256]{1,0:T(8,128)(2,1)} %get-tuple-element.47), channel_id=1, source_target_pairs={{0,12},{2,14},{4,0},{6,2},{8,4},{10,6},{12,8},{14,10},{1,13},{3,15... | collective-permute-start | bytes 466952 | tf_op jit(solution)/shard_map/ppermute | solution.py:343
  38.8 11.7 %copy-start.6 = (bf16[304,256]{1,0:T(8,128)(2,1)S(1)}, bf16[304,256]{1,0:T(8,128)(2,1)}, u32[]{:S(2)}) copy-start(bf16[304,256]{1,0:T(8,128)(2,1)} %copy-done.5) | copy-start | bytes 466948
  47.6 0.8 copy-start.30
  47.6 1.5 %copy-start.39 = (s32[8,4]{0,1:T(4,128)S(1)}, s32[8,4]{0,1:T(4,128)}, u32[]{:S(2)}) copy-start(s32[8,4]{0,1:T(4,128)} %param.33) | copy-start | bytes 388
  47.6 10.6 %collective-permute-start.17 = (bf16[304,256]{1,0:T(8,128)(2,1)S(1)}, bf16[304,256]{1,0:T(8,128)(2,1)S(1)}, u32[]{:S(2)}, u32[]{:S(2)}) collective-permute-start(bf16[304,256]{1,0:T(8,128)(2,1)S(1)} %shard_map.236.kept), channel_id=1, source_target_pairs={{4,8},{6,10},{8,4},{10,6},{5,9},{7,11},{9,5},{11,7},{20,24},{22,26... | collective-permute-start | bytes 466952 | tf_op jit(solution)/shard_map/ppermute | solution.py:383
  50.5 0.9 copy-start.8
  53.1 12.0 %collective-permute-start.4 = (bf16[272,256]{1,0:T(8,128)(2,1)}, bf16[272,256]{1,0:T(8,128)(2,1)S(1)}, u32[]{:S(2)}, u32[]{:S(2)}) collective-permute-start(bf16[272,256]{1,0:T(8,128)(2,1)} %copy-done.30), channel_id=1, source_target_pairs={{0,12},{2,14},{4,0},{6,2},{8,4},{10,6},{12,8},{14,10},{1,13},{3,15... | collective-permute-start | bytes 417800 | tf_op jit(solution)/shard_map/ppermute | solution.py:343
  56.6 13.6 %collective-permute-start.5 = (bf16[272,256]{1,0:T(8,128)(2,1)}, bf16[272,256]{1,0:T(8,128)(2,1)S(1)}, u32[]{:S(2)}, u32[]{:S(2)}) collective-permute-start(bf16[272,256]{1,0:T(8,128)(2,1)} %copy-done.29), channel_id=1, source_target_pairs={{0,8},{2,10},{4,12},{6,14},{8,0},{10,2},{12,4},{14,6},{1,9},{3,11}... | collective-permute-start | bytes 417800 | tf_op jit(solution)/shard_map/ppermute | solution.py:343
  56.6 13.6 %collective-permute-start.6 = (bf16[272,256]{1,0:T(8,128)(2,1)}, bf16[272,256]{1,0:T(8,128)(2,1)S(1)}, u32[]{:S(2)}, u32[]{:S(2)}) collective-permute-start(bf16[272,256]{1,0:T(8,128)(2,1)} %copy-done.28), channel_id=1, source_target_pairs={{0,4},{2,6},{4,8},{6,10},{8,12},{10,14},{12,0},{14,2},{1,5},{3,7},... | collective-permute-start | bytes 417800 | tf_op jit(solution)/shard_map/ppermute | solution.py:343
  57.1 18.5 %collective-permute-start.13 = (bf16[4,256,256]{2,1,0:T(8,128)(2,1)}, bf16[4,256,256]{2,1,0:T(8,128)(2,1)}, u32[]{:S(2)}, u32[]{:S(2)}) collective-permute-start(bf16[4,256,256]{2,1,0:T(8,128)(2,1)} %get-tuple-element.38), channel_id=1, source_target_pairs={{0,2},{2,0},{4,6},{6,4},{8,10},{10,8},{12,14},{14,12},{1,3},{3,1},... | collective-permute-start | bytes 1572872 | tf_op jit(solution)/shard_map/ppermute | solution.py:340
  58.2 12.0 %collective-permute-start.18 = (bf16[304,256]{1,0:T(8,128)(2,1)S(1)}, bf16[304,256]{1,0:T(8,128)(2,1)S(1)}, u32[]{:S(2)}, u32[]{:S(2)}) collective-permute-start(bf16[304,256]{1,0:T(8,128)(2,1)S(1)} %shard_map.237.kept), channel_id=1, source_target_pairs={{0,4},{2,6},{4,0},{6,2},{8,12},{10,14},{12,8},{14,10},{1,5},{3,7},... | collective-permute-start | bytes 466952 | tf_op jit(solution)/shard_map/ppermute | solution.py:383
  61.2 11.6 %copy-start.26 = (f32[4096]{0:T(1024)S(1)}, f32[4096]{0:T(1024)}, u32[]{:S(2)}) copy-start(f32[4096]{0:T(1024)} %param.44) | copy-start | bytes 49156
  65.8 17.3 %collective-permute-start.10 = (bf16[144,256]{1,0:T(8,128)(2,1)}, bf16[144,256]{1,0:T(8,128)(2,1)}, u32[]{:S(2)}, u32[]{:S(2)}) collective-permute-start(bf16[144,256]{1,0:T(8,128)(2,1)} %get-tuple-element.34), channel_id=1, source_target_pairs={{0,12},{2,14},{4,0},{6,2},{8,4},{10,6},{12,8},{14,10},{1,13},{3,15... | collective-permute-start | bytes 221192 | tf_op jit(solution)/shard_map/ppermute | solution.py:343
  70.1 27.6 %collective-permute-start.11 = (bf16[144,256]{1,0:T(8,128)(2,1)}, bf16[144,256]{1,0:T(8,128)(2,1)}, u32[]{:S(2)}, u32[]{:S(2)}) collective-permute-start(bf16[144,256]{1,0:T(8,128)(2,1)} %get-tuple-element.35), channel_id=1, source_target_pairs={{0,8},{2,10},{4,12},{6,14},{8,0},{10,2},{12,4},{14,6},{1,9},{3,11}... | collective-permute-start | bytes 221192 | tf_op jit(solution)/shard_map/ppermute | solution.py:343
  70.1 2.7 %copy-start.3 = (bf16[4096,32]{0,1:T(8,128)(2,1)S(1)}, bf16[4096,32]{0,1:T(8,128)(2,1)}, u32[]{:S(2)}) copy-start(bf16[4096,32]{0,1:T(8,128)(2,1)} %param.45) | copy-start | bytes 786436
  70.1 27.5 %collective-permute-start.12 = (bf16[144,256]{1,0:T(8,128)(2,1)}, bf16[144,256]{1,0:T(8,128)(2,1)}, u32[]{:S(2)}, u32[]{:S(2)}) collective-permute-start(bf16[144,256]{1,0:T(8,128)(2,1)} %get-tuple-element.36), channel_id=1, source_target_pairs={{0,4},{2,6},{4,8},{6,10},{8,12},{10,14},{12,0},{14,2},{1,5},{3,7},... | collective-permute-start | bytes 221192 | tf_op jit(solution)/shard_map/ppermute | solution.py:343
  70.8 2.0 %copy-start.4 = (f32[4,4096]{1,0:T(4,128)S(1)}, f32[4,4096]{1,0:T(4,128)}, u32[]{:S(2)}) copy-start(f32[4,4096]{1,0:T(4,128)} %w.1) | copy-start | bytes 196612
  75.5 3.3 %copy-start.18 = (f32[2,32,32]{2,1,0:T(8,128)}, f32[2,32,32]{2,1,0:T(8,128)S(1)}, u32[]{:S(2)}) copy-start(f32[2,32,32]{2,1,0:T(8,128)S(1)} %shard_map.240) | copy-start | bytes 24580
  75.5 9.0 %copy-start.36 = (f32[16,4096]{1,0:T(8,128)S(1)}, f32[16,4096]{1,0:T(8,128)}, u32[]{:S(2)}) copy-start(f32[16,4096]{1,0:T(8,128)} %param.41) | copy-start | bytes 786436
  75.5 9.0 %collective-permute-start.22 = (f32[2,32,32]{2,1,0:T(8,128)S(1)}, f32[2,32,32]{2,1,0:T(8,128)S(1)}, u32[]{:S(2)}, u32[]{:S(2)}) collective-permute-start(f32[2,32,32]{2,1,0:T(8,128)S(1)} %shard_map.240), channel_id=1, source_target_pairs={{0,1},{1,0},{2,3},{3,2},{4,5},{5,4},{6,7},{7,6},{8,9},{9,8},{10,11... | collective-permute-start | bytes 24584 | tf_op jit(solution)/shard_map/ppermute | solution.py:445
  78.9 5.7 %copy-start.23 = (bf16[144,256]{1,0:T(8,128)(2,1)}, bf16[144,256]{1,0:T(8,128)(2,1)S(1)}, u32[]{:S(2)}) copy-start(bf16[144,256]{1,0:T(8,128)(2,1)S(1)} %get-tuple-element.39.refs_11_) | copy-start | bytes 221188
  78.9 18.8 %collective-permute-start.14 = (bf16[144,256]{1,0:T(8,128)(2,1)}, bf16[144,256]{1,0:T(8,128)(2,1)S(1)}, u32[]{:S(2)}, u32[]{:S(2)}) collective-permute-start(bf16[144,256]{1,0:T(8,128)(2,1)} %get-tuple-element.40), channel_id=1, source_target_pairs={{0,12},{2,14},{4,0},{6,2},{8,4},{10,6},{12,8},{14,10},{1,13},{3,15... | collective-permute-start | bytes 221192 | tf_op jit(solution)/shard_map/ppermute | solution.py:343
  83.0 14.7 %collective-permute-start.15 = (bf16[144,256]{1,0:T(8,128)(2,1)}, bf16[144,256]{1,0:T(8,128)(2,1)S(1)}, u32[]{:S(2)}, u32[]{:S(2)}) collective-permute-start(bf16[144,256]{1,0:T(8,128)(2,1)} %get-tuple-element.41), channel_id=1, source_target_pairs={{0,8},{2,10},{4,12},{6,14},{8,0},{10,2},{12,4},{14,6},{1,9},{3,11}... | collective-permute-start | bytes 221192 | tf_op jit(solution)/shard_map/ppermute | solution.py:343
  84.5 13.2 %collective-permute-start.16 = (bf16[144,256]{1,0:T(8,128)(2,1)}, bf16[144,256]{1,0:T(8,128)(2,1)S(1)}, u32[]{:S(2)}, u32[]{:S(2)}) collective-permute-start(bf16[144,256]{1,0:T(8,128)(2,1)} %get-tuple-element.42), channel_id=1, source_target_pairs={{0,4},{2,6},{4,8},{6,10},{8,12},{10,14},{12,0},{14,2},{1,5},{3,7},... | collective-permute-start | bytes 221192 | tf_op jit(solution)/shard_map/ppermute | solution.py:343
  85.1 1.1 %copy-start.2 = (bf16[8,8,32,128]{3,2,1,0:T(8,128)(2,1)S(1)}, bf16[8,8,32,128]{3,2,1,0:T(8,128)(2,1)}, u32[]{:S(2)}) copy-start(bf16[8,8,32,128]{3,2,1,0:T(8,128)(2,1)} %copy.33) | copy-start | bytes 1572868
  85.2 0.8 copy-start.38
  96.6 1.1 %copy-start.10 = (bf16[272,256]{1,0:T(8,128)(2,1)S(1)}, bf16[272,256]{1,0:T(8,128)(2,1)}, u32[]{:S(2)}) copy-start(bf16[272,256]{1,0:T(8,128)(2,1)} %copy-done.9) | copy-start | bytes 417796
  96.6 1.1 %copy-start.12 = (bf16[272,256]{1,0:T(8,128)(2,1)S(1)}, bf16[272,256]{1,0:T(8,128)(2,1)}, u32[]{:S(2)}) copy-start(bf16[272,256]{1,0:T(8,128)(2,1)} %copy-done.11) | copy-start | bytes 417796
  96.6 1.1 %copy-start.14 = (bf16[272,256]{1,0:T(8,128)(2,1)S(1)}, bf16[272,256]{1,0:T(8,128)(2,1)}, u32[]{:S(2)}) copy-start(bf16[272,256]{1,0:T(8,128)(2,1)} %copy-done.13) | copy-start | bytes 417796
  96.6 1.1 %copy-start.16 = (bf16[272,256]{1,0:T(8,128)(2,1)S(1)}, bf16[272,256]{1,0:T(8,128)(2,1)}, u32[]{:S(2)}) copy-start(bf16[272,256]{1,0:T(8,128)(2,1)} %copy-done.15) | copy-start | bytes 417796
  96.6 1.1 %copy-start.22 = (bf16[144,256]{1,0:T(8,128)(2,1)S(1)}, bf16[144,256]{1,0:T(8,128)(2,1)}, u32[]{:S(2)}) copy-start(bf16[144,256]{1,0:T(8,128)(2,1)} %copy-done.21) | copy-start | bytes 221188
  96.7 1.1 %copy-start.24 = (bf16[144,256]{1,0:T(8,128)(2,1)S(1)}, bf16[144,256]{1,0:T(8,128)(2,1)}, u32[]{:S(2)}) copy-start(bf16[144,256]{1,0:T(8,128)(2,1)} %copy-done.23) | copy-start | bytes 221188
  96.7 1.1 %copy-start.25 = (bf16[1,2,32,512]{3,2,1,0:T(8,128)(2,1)S(1)}, bf16[1,2,32,512]{3,2,1,0:T(8,128)(2,1)}, u32[]{:S(2)}) copy-start(bf16[1,2,32,512]{3,2,1,0:T(8,128)(2,1)} %param.24) | copy-start | bytes 196612
  (16 other events, 11.2 us)

commit v2 on v1

--- a/solution.py
+++ b/solution.py
@@ -63,6 +63,22 @@
     return top, total
 
 
+def folded_softmax(done, kv, at, q):
+    step = math.gcd(kv.shape[0], HD)
+    parts = list(done)
+    for c in range(0, kv.shape[0], step):
+        s = dot(kv[c : c + step, at : at + HD], q, 1, 1)
+        high = jnp.max(s, axis=0, keepdims=True)
+        p = jnp.exp2((s - high) * SCORE2)
+        value = dot(kv[c : c + step, at + HD : at + 2 * HD], p.astype(BF16), 0, 0)
+        parts.append((high, jnp.sum(p, axis=0, keepdims=True), value))
+    m = functools.reduce(jnp.maximum, [part[0] for part in parts])
+    fades = [jnp.exp2((part[0] - m) * SCORE2) for part in parts]
+    l = sum(f * part[1] for f, part in zip(fades, parts))
+    o = sum(f * part[2] for f, part in zip(fades, parts))
+    return m, l, o
+
+
 def prefix_body(heads, spans, pair, *refs):
     me, owner, own, nbr = refs[:4]
     qs = refs[4 : 4 + spans]
@@ -79,11 +95,7 @@
             stats = []
             for h in range(heads):
                 qh = q[h * wide : (h + 1) * wide, :]
-                s = dot(kv[:, 2 * h * HD : (2 * h + 1) * HD], qh, 1, 1)
-                m = jnp.max(s, axis=0, keepdims=True)
-                p = jnp.exp2((s - m) * SCORE2)
-                l = jnp.sum(p, axis=0, keepdims=True)
-                o = dot(kv[:, (2 * h + 1) * HD : (2 * h + 2) * HD], p.astype(BF16), 0, 0)
+                m, l, o = folded_softmax([], kv, 2 * h * HD, qh)
                 out[h * HD : (h + 1) * HD, :] = o.astype(BF16)
                 stats += pieces(m, 3) + pieces(l, 2)
             out[rows:, :] = stat_block(stats, wide)
@@ -98,51 +110,51 @@
             out[rows:, :] = stat_block((pieces(low, 3) + [zero, zero]) * heads, wide)
 
 
-def blocks_body(head, spans, slots, pair, *refs):
+def blocks_body(heads, spans, slots, pair, *refs):
     me, src, blk, own, nbr = refs[:5]
     qs = refs[5 : 5 + spans]
     outs = refs[5 + spans : 5 + 2 * spans]
     acc, top, tot = refs[5 + 2 * spans :]
     z, y = me[0] // pair, lax.rem(me[0], pair)
-    for k, (q, out) in enumerate(zip(qs, outs)):
-        full = q.shape[0] - STAT
-        wide = out.shape[1]
-        lo = full // 2 + head * wide
+    rows = heads * HD
+    full = qs[0].shape[0] - STAT
+    wide = outs[0].shape[1]
+    ctxs = [jnp.max(q[full:, :].astype(F32)) for q in qs]
+    for k, (q, out, ctx) in enumerate(zip(qs, outs, ctxs)):
         reader = lax.rem(z + (spans - k), spans) * pair + y
-        ctx = jnp.max(q[full:, :].astype(F32))
         acc[...] = jnp.zeros_like(acc)
         top[...] = jnp.full(top.shape, LOW, F32)
         tot[...] = jnp.zeros_like(tot)
 
-        def slot(j, carry, q=q, lo=lo, wide=wide, reader=reader, ctx=ctx):
+        def slot(j, carry, q=q, reader=reader, ctx=ctx):
             source = src[reader, j]
             live = (source // pair == z) & (j.astype(F32) < ctx)
 
             @pl.when(live)
             def _():
                 b = blk[reader, j]
-                kv = jnp.where(lax.rem(source, pair) == y, own[b, :, 2 * head * HD : 2 * (head + 1) * HD], nbr[b])
-                s = dot(kv[:, :HD], q[lo : lo + wide, :], 1, 1)
-                old = top[...]
-                m = jnp.maximum(old, jnp.max(s, axis=0, keepdims=True))
-                p = jnp.exp2((s - m) * SCORE2)
-                fade = jnp.exp2((old - m) * SCORE2)
-                o = dot(kv[:, HD:], p.astype(BF16), 0, 0)
-                acc[...] = acc[...] * fade + o
-                tot[...] = tot[...] * fade + jnp.sum(p, axis=0, keepdims=True)
-                top[...] = m
+                mine = lax.rem(source, pair) == y
+                for h in range(heads):
+                    at = slice(2 * h * HD, 2 * (h + 1) * HD)
+                    kv = jnp.where(mine, own[b, :, at], nbr[b, :, at])
+                    lo = full // 2 + h * wide
+                    done = [(top[h], tot[h], acc[h])]
+                    top[h], tot[h], acc[h] = folded_softmax(done, kv, 0, q[lo : lo + wide, :])
 
             return carry
 
         lax.fori_loop(0, slots, slot, 0)
-        out[:HD, :] = acc[...].astype(BF16)
-        out[HD:, :] = stat_block(pieces(top[...], 3) + pieces(tot[...], 2), wide)
+        stats = []
+        for h in range(heads):
+            out[h * HD : (h + 1) * HD, :] = acc[h].astype(BF16)
+            stats += pieces(top[h], 3) + pieces(tot[h], 2)
+        out[rows:, :] = stat_block(stats, wide)
 
 
 def join_body(heads, spans, *refs):
     flag, q, new = refs[:3]
-    parts = [refs[3 + i * spans : 3 + (i + 1) * spans] for i in range(1 + heads)]
-    out = refs[3 + (1 + heads) * spans]
+    parts = [refs[3 : 3 + spans], refs[3 + spans : 3 + 2 * spans]]
+    out = refs[3 + 2 * spans]
     fresh = new.shape[1]
     half = q.shape[0] - STAT
     wide = half // (2 * heads)
@@ -156,8 +168,8 @@
             seen = key <= token
             s = jnp.where(seen, s, LOW)
             best = jnp.max(s, axis=0, keepdims=True)
-            mine, at, base, place = (parts[0], h * HD, rows, h) if r == 0 else (parts[1 + h], 0, HD, 0)
-            stats = [stats_of(part, base, place) for part in mine]
+            at = h * HD
+            stats = [stats_of(part, rows, h) for part in parts[r]]
             if r == 0:
                 stats = [(jnp.where(flag[0] > 0, m, LOW), l) for m, l in stats]
             for m, _ in stats:
@@ -165,7 +177,7 @@
             p = jnp.where(seen, jnp.exp2((s - best) * SCORE2), 0.0)
             total = jnp.sum(p, axis=0, keepdims=True)
             o = dot(new[r, :, (2 * h + 1) * HD : (2 * h + 2) * HD], p.astype(BF16), 0, 0)
-            for part, (m, l) in zip(mine, stats):
+            for part, (m, l) in zip(parts[r], stats):
                 w = jnp.exp2((m - best) * SCORE2)
                 total = total + w * l
                 o = o + w * part[at : at + HD, :].astype(F32)
@@ -267,7 +279,7 @@
             res[r, t] = gain[...] * sig
             return carry
 
-        lax.fori_loop(0, length, prepare, 0)
+        lax.fori_loop(0, length, prepare, 0, unroll=4)
 
     for r, st in enumerate((st0, st1)):
         for c in range(0, sub, block):
@@ -295,7 +307,7 @@
                 out[r, t, at, :] = (y * gate).astype(BF16)
                 return tuple(after)
 
-            lax.fori_loop(0, length, advance, tuple(start))
+            lax.fori_loop(0, length, advance, tuple(start), unroll=2)
 
 
 def local(
@@ -364,7 +376,6 @@
     asked = [message] + [turn(message, k) for k in range(1, spans)]
 
     x_t, dt_t, z_t = tiled(mamba_x[0]), tiled(mamba_dt[0]), tiled(mamba_z[0])
-    halves = [pool_kv[0, :, :, h * cols : (h + 1) * cols] for h in range(heads)]
     prefix_nbr = across(cached_lookup_pairs[0])
 
     one = jax.ShapeDtypeStruct((unit, cols), BF16)
@@ -391,7 +402,7 @@
         [SSPEC] * 2 + [VSPEC] * 2,
         (),
         pl.CostEstimate(flops=50 * 10**9, bytes_accessed=150 * 10**6, transcendentals=0),
-    )(after(me, x_t, dt_t, z_t, *halves, *asked[1:], *hops[:1]), state_src, states, states_nbr)
+    )(after(me, x_t, dt_t, z_t, *asked[1:], *hops[:1]), state_src, states, states_nbr)
     came = [sent[0]] + [turn(sent[k], k) for k in range(1, spans)]
     state1 = call(
         functools.partial(state_take_body, spans, pair),
@@ -410,24 +421,18 @@
     for r in range(1, spans):
         state0 = shared(r, state0, hops[-1])
         if r < spans - 1:
-            hops.append(hop(after(state0, part0[0]), r))
-    got0 = [part0[0]] + [turn(part0[k], spans - k) for k in range(1, spans)]
-
-    block_len = pool_kv.shape[2]
-    head_shape = jax.ShapeDtypeStruct((HD + STAT, wide), BF16)
-    got1 = []
-    last = [sent[0]]
-    for h in range(heads):
-        pool_nbr = across(after(halves[h], *last))
-        last = [pool_nbr, part0[0]]
-        part1 = call(
-            functools.partial(blocks_body, h, spans, slots, pair),
-            [head_shape] * spans,
-            [SSPEC] * 3 + [VSPEC] * (2 + spans),
-            [pltpu.VMEM((HD, wide), F32), pltpu.VMEM((1, wide), F32), pltpu.VMEM((1, wide), F32)],
-            pl.CostEstimate(flops=20 * 10**9, bytes_accessed=60 * 10**6, transcendentals=0),
-        )(after(me, part0[0], *(got0[1:] if h else ())), restore_src, restore_blk, pool_kv[0], pool_nbr, *asked)
-        got1 += [part1[0]] + [turn(part1[k], spans - k) for k in range(1, spans)]
+            hops.append(hop(after(state0, sent[0]), r))
+    got0 = [part0[0]] + [turn(after(part0[k], came[spans - k]), spans - k) for k in range(1, spans)]
+
+    pool_nbr = across(after(pool_kv[0], sent[0]))
+    part1 = call(
+        functools.partial(blocks_body, heads, spans, slots, pair),
+        [part_shape] * spans,
+        [SSPEC] * 3 + [VSPEC] * (2 + spans),
+        [pltpu.VMEM((heads, HD, wide), F32), pltpu.VMEM((heads, 1, wide), F32), pltpu.VMEM((heads, 1, wide), F32)],
+        pl.CostEstimate(flops=20 * 10**9, bytes_accessed=60 * 10**6, transcendentals=0),
+    )(after(me, *got0[1:]), restore_src, restore_blk, pool_kv[0], pool_nbr, *asked)
+    got1 = [part1[0]] + [turn(part1[k], spans - k) for k in range(1, spans)]
 
     first = state * inner // cols
 
@@ -475,7 +480,7 @@
     attention_out = call(
         functools.partial(join_body, heads, spans),
         jax.ShapeDtypeStruct((2, length, heads * Q_PER_KV * HD), BF16),
-        [SSPEC] + [VSPEC] * (2 + (1 + heads) * spans),
+        [SSPEC] + [VSPEC] * (2 + 2 * spans),
         (),
         pl.CostEstimate(flops=1 << 24, bytes_accessed=2 << 20, transcendentals=1 << 16),
     )(readers, message, new_kv[0], *got0, *got1)[None]

time: 102 us -> 90.3 us (0.89)
  waiting for transfers between devices: 15.5 us -> 30.4 us
  local copies, waits for them, and re-layouts: 17.9 us -> 7.31 us
  Pallas kernels: 30.1 us -> 21.3 us
  starting transfers between devices: 32.8 us -> 26.7 us
    ppermute x15 -> x12, waiting for transfers between devices: 12.4 us -> 24.9 us  [turn(): lax.ppermute(value, axis, [(s, (s + k * pair) % size) for s in range(size)])]
    ppermute x15 -> x12, starting transfers between devices: 22.5 us -> 15 us  [turn(): lax.ppermute(value, axis, [(s, (s + k * pair) % size) for s in range(size)])]
    unnamed x90 -> x50, local copies, waits for them, and re-layouts: 12.9 us -> 5.85 us
    pallas_call x1, Pallas kernels: 7.45 us -> 2.13 us  [local(): call(functools.partial(prefix_body, heads, spans, pair), [part_shape] * s...]
    reshape x2, local copies, waits for them, and re-layouts: 1.97 us -> 0.04 us  [taps_of(): return value[first:].reshape(keep, inner)]
    pallas_call x1, Pallas kernels: 9.8 us -> 8.06 us  [local(): call(functools.partial(scan_body, state), jax.ShapeDtypeStruct((2, length...]
    ppermute x4 -> x3, waiting for transfers between devices: 0.01 us -> 1.48 us  [across(): return lax.ppermute(value, axis, [(s, s ^ 1) for s in range(size)])]
    ppermute x3, starting transfers between devices: 4.52 us -> 5.63 us  [hop(): return lax.ppermute(value, axis, links)]
  transfers between devices with their start and end apart: 23 -> 19, of which waited for: 3 -> 8; matrix products, arithmetic and copies ran while one was open for 6% -> 2% of each run, Pallas kernels for 27% -> 20%
where the time goes in v2:
time: 90.3 us; the launch traced here: 89.7 us
  waiting for transfers between devices  30.4 us (34%)
  starting transfers between devices  26.7 us (30%)
  Pallas kernels  21.3 us (24%)
  local copies, waits for them, and re-layouts  7.31 us (8%)
  between operations  2.97 us (3%)
  other arithmetic  1.09 us (1%)
    ppermute x12, waiting for transfers between devices, turn(): lax.ppermute(value, axis, [(s, (s + k * pair) % size) for s in range(size)])  24.9 us
    ppermute x12, starting transfers between devices, turn(): lax.ppermute(value, axis, [(s, (s + k * pair) % size) for s in range(size)])  15 us
    pallas_call x1, Pallas kernels, local(): call(functools.partial(scan_body, state), jax.ShapeDtypeStruct((2, length...  8.06 us
    ppermute x3, starting transfers between devices, across(): return lax.ppermute(value, axis, [(s, s ^ 1) for s in range(size)])  6.07 us
    unnamed x50, local copies, waits for them, and re-layouts  5.85 us
    pallas_call x1, Pallas kernels, local(): call(functools.partial(blocks_body, heads, spans, slots, pair), [part_sha...  5.67 us
    ppermute x3, starting transfers between devices, hop(): return lax.ppermute(value, axis, links)  5.63 us
    ppermute x3, waiting for transfers between devices, hop(): return lax.ppermute(value, axis, links)  3.05 us
  transfers between devices with their start and end apart: 19, of which 8 were waited for; matrix products, arithmetic and copies ran while one was open for 2% of the time, Pallas kernels for 20%

profile of v2, /device:TPU:0, one launch (start us, length us, event | category | flops | bytes accessed | tf_op | source)
XLA Modules:
  0.0 89.7 jit_solution(2622042410041450744)
XLA Ops:
  0.6 1.1 %pad_maximum_fusion = bf16[38,4096]{1,0:T(8,128)(2,1)S(1)} fusion(bf16[3,4096]{1,0:T(4,128)(2,1)} %bitcast.72, bf16[16,4096]{1,0:T(8,128)(2,1)} %bitcast.70, bf16[3,4096]{1,0:T(4,128)(2,1)} %bitcast.73, bf16[16,4096]{1,0:T(8,128)(2,1)} %bitcast.71), kind=kLoop, calls=%fused_computation | loop fusion | flops 1245184 | bytes 622592 | tf_op jit(solution)/shard_map/concatenate | solution.py:368
  1.7 0.2 reshape.45.kept.own
  1.9 3.0 %collective-permute-start.4 = (bf16[608,256]{1,0:T(8,128)(2,1)S(1)}, bf16[608,256]{1,0:T(8,128)(2,1)S(1)}, u32[]{:S(2)}, u32[]{:S(2)}) collective-permute-start(bf16[608,256]{1,0:T(8,128)(2,1)S(1)} %reshape.45.kept.own), channel_id=1, source_target_pairs={{0,2},{2,0},{4,6},{6,4},{8,10},{10,8},{12,14},{14,12},{1,3},{3,1},... | collective-permute-start | bytes 933896 | tf_op jit(solution)/shard_map/ppermute | solution.py:352
  5.0 0.1 copy.25
  5.8 1.6 %collective-permute-start.1 = (bf16[1040,128]{1,0:T(8,128)(2,1)S(1)}, bf16[1040,128]{1,0:T(8,128)(2,1)S(1)}, u32[]{:S(2)}, u32[]{:S(2)}) collective-permute-start(bf16[1040,128]{1,0:T(8,128)(2,1)S(1)} %concatenate.6.refs_4_.refs_5_.refs_1_), channel_id=1, source_target_pairs={{0,4},{2,6},{4,8},{6,10},{8,12},{10,14},{12,0},{14,2},{1,5},{3,7},... | collective-permute-start | bytes 798728 | tf_op jit(solution)/shard_map/ppermute | solution.py:355
  7.4 2.6 %collective-permute-start.2 = (bf16[1040,128]{1,0:T(8,128)(2,1)S(1)}, bf16[1040,128]{1,0:T(8,128)(2,1)}, u32[]{:S(2)}, u32[]{:S(2)}) collective-permute-start(bf16[1040,128]{1,0:T(8,128)(2,1)S(1)} %concatenate.6.refs_4_.refs_5_.refs_1_), channel_id=1, source_target_pairs={{0,8},{2,10},{4,12},{6,14},{8,0},{10,2},{12,4},{14,6},{1,9},{3,11}... | collective-permute-start | bytes 798728 | tf_op jit(solution)/shard_map/ppermute | solution.py:355
  10.0 1.3 %collective-permute-start.3 = (bf16[1040,128]{1,0:T(8,128)(2,1)S(1)}, bf16[1040,128]{1,0:T(8,128)(2,1)}, u32[]{:S(2)}, u32[]{:S(2)}) collective-permute-start(bf16[1040,128]{1,0:T(8,128)(2,1)S(1)} %concatenate.6.refs_4_.refs_5_.refs_1_), channel_id=1, source_target_pairs={{0,12},{2,14},{4,0},{6,2},{8,4},{10,6},{12,8},{14,10},{1,13},{3,15... | collective-permute-start | bytes 798728 | tf_op jit(solution)/shard_map/ppermute | solution.py:355
  12.0 0.3 collective-permute-done.4.came.nbr
  12.4 1.9 %collective-permute-start.5 = (bf16[304,256]{1,0:T(8,128)(2,1)S(1)}, bf16[304,256]{1,0:T(8,128)(2,1)S(1)}, u32[]{:S(2)}, u32[]{:S(2)}) collective-permute-start(bf16[304,256]{1,0:T(8,128)(2,1)S(1)} %shard_map.231.kept), channel_id=1, source_target_pairs={{0,4},{2,6},{4,0},{6,2},{8,12},{10,14},{12,8},{14,10},{1,5},{3,7},... | collective-permute-start | bytes 466952 | tf_op jit(solution)/shard_map/ppermute | solution.py:394
  14.2 1.5 %collective-permute-start = (bf16[1024,512]{1,0:T(8,128)(2,1)}, bf16[1024,512]{1,0:T(8,128)(2,1)S(1)}, u32[]{:S(2)}, u32[]{:S(2)}) collective-permute-start(bf16[1024,512]{1,0:T(8,128)(2,1)} %bitcast.5.refs_2_), channel_id=1, source_target_pairs={{0,2},{2,0},{4,6},{6,4},{8,10},{10,8},{12,14},{14,12},{1,3},{3,1},... | collective-permute-start | bytes 3145736 | tf_op jit(solution)/shard_map/ppermute | solution.py:352
  15.7 0.1 copy.29
  15.8 0.9 %copy-done.15 = bf16[1,2,32,4096]{3,2,1,0:T(8,128)(2,1)S(1)} copy-done((bf16[1,2,32,4096]{3,2,1,0:T(8,128)(2,1)S(1)}, bf16[1,2,32,4096]{3,2,1,0:T(8,128)(2,1)}, u32[]{:S(2)}) %copy-start.15) | copy-done | bytes 524312
  16.8 0.1 copy.30
  16.9 0.9 %copy-done.16 = bf16[1,2,32,4096]{3,2,1,0:T(8,128)(2,1)S(1)} copy-done((bf16[1,2,32,4096]{3,2,1,0:T(8,128)(2,1)S(1)}, bf16[1,2,32,4096]{3,2,1,0:T(8,128)(2,1)}, u32[]{:S(2)}) %copy-start.16) | copy-done | bytes 524312
  17.8 0.1 copy.31
  17.9 0.7 copy-done.10
  18.6 8.6 %collective-permute-done.2.refs_6_.refs_7_ = bf16[1040,128]{1,0:T(8,128)(2,1)} collective-permute-done((bf16[1040,128]{1,0:T(8,128)(2,1)S(1)}, bf16[1040,128]{1,0:T(8,128)(2,1)}, u32[]{:S(2)}, u32[]{:S(2)}) %collective-permute-start.2) | collective-permute-done | bytes 266272 | tf_op jit(solution)/shard_map/ppermute | solution.py:355
  27.3 3.0 %collective-permute-done.5.came = bf16[304,256]{1,0:T(8,128)(2,1)S(1)} collective-permute-done((bf16[304,256]{1,0:T(8,128)(2,1)S(1)}, bf16[304,256]{1,0:T(8,128)(2,1)S(1)}, u32[]{:S(2)}, u32[]{:S(2)}) %collective-permute-start.5) | collective-permute-done | bytes 155680 | tf_op jit(solution)/shard_map/ppermute | solution.py:394
  30.3 0.7 copy-done.9
  31.0 0.6 shard_map.232
  31.6 3.2 %collective-permute-start.10 = (bf16[304,256]{1,0:T(8,128)(2,1)S(1)}, bf16[304,256]{1,0:T(8,128)(2,1)S(1)}, u32[]{:S(2)}, u32[]{:S(2)}) collective-permute-start(bf16[304,256]{1,0:T(8,128)(2,1)S(1)} %get-tuple-element.31), channel_id=1, source_target_pairs={{0,4},{2,6},{4,8},{6,10},{8,12},{10,14},{12,0},{14,2},{1,5},{3,7},... | collective-permute-start | bytes 466952 | tf_op jit(solution)/shard_map/ppermute | solution.py:355
  34.8 1.0 %collective-permute-start.6 = (bf16[304,256]{1,0:T(8,128)(2,1)S(1)}, bf16[304,256]{1,0:T(8,128)(2,1)S(1)}, u32[]{:S(2)}, u32[]{:S(2)}) collective-permute-start(bf16[304,256]{1,0:T(8,128)(2,1)S(1)} %get-tuple-element.25), channel_id=1, source_target_pairs={{0,12},{2,14},{4,0},{6,2},{8,4},{10,6},{12,8},{14,10},{1,13},{3,15... | collective-permute-start | bytes 466952 | tf_op jit(solution)/shard_map/ppermute | solution.py:355
  35.8 0.5 collective-permute-start.8
  36.3 0.7 collective-permute-start.16
  37.0 1.2 %collective-permute-done.refs_3_ = bf16[1024,512]{1,0:T(8,128)(2,1)S(1)} collective-permute-done((bf16[1024,512]{1,0:T(8,128)(2,1)}, bf16[1024,512]{1,0:T(8,128)(2,1)S(1)}, u32[]{:S(2)}, u32[]{:S(2)}) %collective-permute-start) | collective-permute-done | bytes 1048608 | tf_op jit(solution)/shard_map/ppermute | solution.py:352
  38.2 1.5 %collective-permute-start.12 = (bf16[4,256,512]{2,1,0:T(8,128)(2,1)}, bf16[4,256,512]{2,1,0:T(8,128)(2,1)}, u32[]{:S(2)}, u32[]{:S(2)}) collective-permute-start(bf16[4,256,512]{2,1,0:T(8,128)(2,1)} %bitcast.10.refs_3_), channel_id=1, source_target_pairs={{0,2},{2,0},{4,6},{6,4},{8,10},{10,8},{12,14},{14,12},{1,3},{3,1},... | collective-permute-start | bytes 3145736 | tf_op jit(solution)/shard_map/ppermute | solution.py:352
  39.7 2.1 %shard_map.230 = (bf16[272,256]{1,0:T(8,128)(2,1)S(1)}, bf16[272,256]{1,0:T(8,128)(2,1)}, bf16[272,256]{1,0:T(8,128)(2,1)}, bf16[272,256]{1,0:T(8,128)(2,1)}) custom-call(s32[1]{0:T(128)} %bitcast.4.refs_0_.me, s32[1]{0:T(128)S(6)} %copy.36.refs_1_.owner, bf16[1024,512]{1,0:T(8,128)(2,1)} %bitcast.5.refs_2_, ...), custom_call_target="tpu_custom_call" | custom-call | flops 49999998976 | bytes 150000000 | tf_op jit(solution)/shard_map/pallas_call | solution.py:414
  41.8 0.7 copy-done.3
  42.5 2.6 %collective-permute-start.11 = (bf16[272,256]{1,0:T(8,128)(2,1)}, bf16[272,256]{1,0:T(8,128)(2,1)}, u32[]{:S(2)}, u32[]{:S(2)}) collective-permute-start(bf16[272,256]{1,0:T(8,128)(2,1)} %get-tuple-element.32), channel_id=1, source_target_pairs={{0,4},{2,6},{4,8},{6,10},{8,12},{10,14},{12,0},{14,2},{1,5},{3,7},... | collective-permute-start | bytes 417800 | tf_op jit(solution)/shard_map/ppermute | solution.py:355
  45.1 10.4 %collective-permute-done.8.refs_2_ = bf16[304,256]{1,0:T(8,128)(2,1)S(1)} collective-permute-done((bf16[304,256]{1,0:T(8,128)(2,1)S(1)}, bf16[304,256]{1,0:T(8,128)(2,1)S(1)}, u32[]{:S(2)}, u32[]{:S(2)}) %collective-permute-start.8) | collective-permute-done | bytes 155680 | tf_op jit(solution)/shard_map/ppermute | solution.py:355
  55.5 0.1 collective-permute-start.7
  55.5 0.1 copy.26.refs_1_
  55.6 0.5 copy-done.20
  56.1 0.1 copy.27.refs_2_
  56.3 3.1 %collective-permute-start.17 = (bf16[304,256]{1,0:T(8,128)(2,1)S(1)}, bf16[304,256]{1,0:T(8,128)(2,1)S(1)}, u32[]{:S(2)}, u32[]{:S(2)}) collective-permute-start(bf16[304,256]{1,0:T(8,128)(2,1)S(1)} %shard_map.236.kept), channel_id=1, source_target_pairs={{0,4},{2,6},{4,0},{6,2},{8,12},{10,14},{12,8},{14,10},{1,5},{3,7},... | collective-permute-start | bytes 466952 | tf_op jit(solution)/shard_map/ppermute | solution.py:394
  59.4 3.8 %collective-permute-done.9.refs_5_ = bf16[272,256]{1,0:T(8,128)(2,1)} collective-permute-done((bf16[272,256]{1,0:T(8,128)(2,1)}, bf16[272,256]{1,0:T(8,128)(2,1)}, u32[]{:S(2)}, u32[]{:S(2)}) %collective-permute-start.9) | collective-permute-done | bytes 139296 | tf_op jit(solution)/shard_map/ppermute | solution.py:355
  63.2 2.0 %collective-permute-done.7.refs_4_ = bf16[272,256]{1,0:T(8,128)(2,1)} collective-permute-done((bf16[272,256]{1,0:T(8,128)(2,1)}, bf16[272,256]{1,0:T(8,128)(2,1)}, u32[]{:S(2)}, u32[]{:S(2)}) %collective-permute-start.7) | collective-permute-done | bytes 139296 | tf_op jit(solution)/shard_map/ppermute | solution.py:355
  65.3 5.7 %shard_map.233 = (bf16[272,256]{1,0:T(8,128)(2,1)S(1)}, bf16[272,256]{1,0:T(8,128)(2,1)}, bf16[272,256]{1,0:T(8,128)(2,1)}, bf16[272,256]{1,0:T(8,128)(2,1)}) custom-call(s32[1]{0:T(128)} %bitcast.4.refs_0_.me, s32[8,4]{1,0:T(8,128)S(1)} %copy.26.refs_1_, s32[8,4]{1,0:T(8,128)S(1)} %copy.27.refs_2_, bf16[4,256,512]{2,1,0:T(8,128)(2,1)} %bitcast.10.refs_3_, ...), custom_call_target="tpu_custom_call" | custom-call | flops 20000000000 | bytes 60000000 | tf_op jit(solution)/shard_map/pallas_call | solution.py:428
  70.9 1.2 %collective-permute-start.13 = (bf16[272,256]{1,0:T(8,128)(2,1)}, bf16[272,256]{1,0:T(8,128)(2,1)}, u32[]{:S(2)}, u32[]{:S(2)}) collective-permute-start(bf16[272,256]{1,0:T(8,128)(2,1)} %get-tuple-element.37), channel_id=1, source_target_pairs={{0,12},{2,14},{4,0},{6,2},{8,4},{10,6},{12,8},{14,10},{1,13},{3,15... | collective-permute-start | bytes 417800 | tf_op jit(solution)/shard_map/ppermute | solution.py:355
  72.1 0.8 collective-permute-start.15
  73.6 0.6 shard_map.238
  74.4 0.8 copy-done.1
  75.2 1.2 %shard_map.239 = f32[2,32,32]{2,1,0:T(8,128)S(1)} custom-call(s32[1]{0:T(128)S(6)} %copy.37.refs_0_.flag, bf16[3,4096]{1,0:T(4,128)(2,1)S(1)} %reshape.46.st0, bf16[3,4096]{1,0:T(4,128)(2,1)S(1)} %reshape.47.st1, bf16[2,32,4096]{2,1,0:T(8,128)(2,1)S(1)} %bitcast.49, f32[4,4096]{1,0:T(4,128)S(1)} %copy-done.2, f32[1,4096]{1,0:T(1,128)S(1)} %bitcast.59, ...), custom_call_target="tpu_custom_call" | custom-call | flops 16777216 | bytes 2097152 | tf_op jit(solution)/shard_map/pallas_call | solution.py:443
  76.6 0.1 reshape.49.st0
  76.7 1.0 %collective-permute-done.18 = f32[2,32,32]{2,1,0:T(8,128)S(1)} collective-permute-done((f32[2,32,32]{2,1,0:T(8,128)S(1)}, f32[2,32,32]{2,1,0:T(8,128)S(1)}, u32[]{:S(2)}, u32[]{:S(2)}) %collective-permute-start.18) | collective-permute-done | bytes 8224 | tf_op jit(solution)/shard_map/ppermute | solution.py:450
  77.7 8.1 %shard_map.240 = bf16[2,32,32,128]{3,2,1,0:T(8,128)(2,1)S(1)} custom-call(s32[1]{0:T(128)S(6)} %copy.37.refs_0_.flag, f32[64,32]{1,0:T(8,128)S(1)} %bitcast.58, bf16[19,32,128]{2,1,0:T(8,128)(2,1)S(1)} %reshape.49.st0, bf16[19,32,128]{2,1,0:T(8,128)(2,1)S(1)} %reshape.50.st1, bf16[2,32,32,128]{3,2,1,0:T(8,128)(2,1)S(1)} %bitcast.50, ...), custom_call_target="tpu_custom_call" | custom-call | flops 25165824 | bytes 4194304 | tf_op jit(solution)/shard_map/pallas_call | solution.py:452
  85.8 1.0 %reshape.56 = bf16[1,2,32,4096]{3,2,1,0:T(8,128)(2,1)} reshape(bf16[2,32,32,128]{3,2,1,0:T(8,128)(2,1)S(1)} %shard_map.240) | data formatting | bytes 1048576 | tf_op jit(solution)/shard_map/reshape | solution.py:478
  86.8 2.9 %shard_map.234 = bf16[2,32,2048]{2,1,0:T(8,128)(2,1)} custom-call(s32[1]{0:T(128)S(6)} %copy.37.refs_0_.flag, bf16[1040,128]{1,0:T(8,128)(2,1)S(1)} %concatenate.6.refs_4_.refs_5_.refs_1_, bf16[2,32,512]{2,1,0:T(8,128)(2,1)S(1)} %bitcast.56, bf16[272,256]{1,0:T(8,128)(2,1)S(1)} %copy-done.4, bf16[272,256]{1,0:T(8,128)(2,1)} %collective-permute-done.7.refs_4_, ...), custom_call_target="tpu_custom_call" | custom-call | flops 16777216 | bytes 2097152 | tf_op jit(solution)/shard_map/pallas_call | solution.py:480
  (63 shorter events, 0.5 us)
Async XLA Ops:
  1.7 3.3 %copy-start.17 = (bf16[1,2,32,2048]{3,2,1,0:T(8,128)(2,1)S(1)}, bf16[1,2,32,2048]{3,2,1,0:T(8,128)(2,1)}, u32[]{:S(2)}) copy-start(bf16[1,2,32,2048]{3,2,1,0:T(8,128)(2,1)} %param.23) | copy-start | bytes 786436
  1.9 10.4 %collective-permute-start.4 = (bf16[608,256]{1,0:T(8,128)(2,1)S(1)}, bf16[608,256]{1,0:T(8,128)(2,1)S(1)}, u32[]{:S(2)}, u32[]{:S(2)}) collective-permute-start(bf16[608,256]{1,0:T(8,128)(2,1)S(1)} %reshape.45.kept.own), channel_id=1, source_target_pairs={{0,2},{2,0},{4,6},{6,4},{8,10},{10,8},{12,14},{14,12},{1,3},{3,1},... | collective-permute-start | bytes 933896 | tf_op jit(solution)/shard_map/ppermute | solution.py:352
  5.8 10.0 %copy-start = (bf16[1,2,32,4096]{3,2,1,0:T(8,128)(2,1)S(1)}, bf16[1,2,32,4096]{3,2,1,0:T(8,128)(2,1)}, u32[]{:S(2)}) copy-start(bf16[1,2,32,4096]{3,2,1,0:T(8,128)(2,1)} %param.37) | copy-start | bytes 1572868
  5.8 12.1 %collective-permute-start.1 = (bf16[1040,128]{1,0:T(8,128)(2,1)S(1)}, bf16[1040,128]{1,0:T(8,128)(2,1)S(1)}, u32[]{:S(2)}, u32[]{:S(2)}) collective-permute-start(bf16[1040,128]{1,0:T(8,128)(2,1)S(1)} %concatenate.6.refs_4_.refs_5_.refs_1_), channel_id=1, source_target_pairs={{0,4},{2,6},{4,8},{6,10},{8,12},{10,14},{12,0},{14,2},{1,5},{3,7},... | collective-permute-start | bytes 798728 | tf_op jit(solution)/shard_map/ppermute | solution.py:355
  7.4 19.8 %collective-permute-start.2 = (bf16[1040,128]{1,0:T(8,128)(2,1)S(1)}, bf16[1040,128]{1,0:T(8,128)(2,1)}, u32[]{:S(2)}, u32[]{:S(2)}) collective-permute-start(bf16[1040,128]{1,0:T(8,128)(2,1)S(1)} %concatenate.6.refs_4_.refs_5_.refs_1_), channel_id=1, source_target_pairs={{0,8},{2,10},{4,12},{6,14},{8,0},{10,2},{12,4},{14,6},{1,9},{3,11}... | collective-permute-start | bytes 798728 | tf_op jit(solution)/shard_map/ppermute | solution.py:355
  10.0 17.2 %collective-permute-start.3 = (bf16[1040,128]{1,0:T(8,128)(2,1)S(1)}, bf16[1040,128]{1,0:T(8,128)(2,1)}, u32[]{:S(2)}, u32[]{:S(2)}) collective-permute-start(bf16[1040,128]{1,0:T(8,128)(2,1)S(1)} %concatenate.6.refs_4_.refs_5_.refs_1_), channel_id=1, source_target_pairs={{0,12},{2,14},{4,0},{6,2},{8,4},{10,6},{12,8},{14,10},{1,13},{3,15... | collective-permute-start | bytes 798728 | tf_op jit(solution)/shard_map/ppermute | solution.py:355
  12.4 17.9 %collective-permute-start.5 = (bf16[304,256]{1,0:T(8,128)(2,1)S(1)}, bf16[304,256]{1,0:T(8,128)(2,1)S(1)}, u32[]{:S(2)}, u32[]{:S(2)}) collective-permute-start(bf16[304,256]{1,0:T(8,128)(2,1)S(1)} %shard_map.231.kept), channel_id=1, source_target_pairs={{0,4},{2,6},{4,0},{6,2},{8,12},{10,14},{12,8},{14,10},{1,5},{3,7},... | collective-permute-start | bytes 466952 | tf_op jit(solution)/shard_map/ppermute | solution.py:394
  14.2 24.0 %collective-permute-start = (bf16[1024,512]{1,0:T(8,128)(2,1)}, bf16[1024,512]{1,0:T(8,128)(2,1)S(1)}, u32[]{:S(2)}, u32[]{:S(2)}) collective-permute-start(bf16[1024,512]{1,0:T(8,128)(2,1)} %bitcast.5.refs_2_), channel_id=1, source_target_pairs={{0,2},{2,0},{4,6},{6,4},{8,10},{10,8},{12,14},{14,12},{1,3},{3,1},... | collective-permute-start | bytes 3145736 | tf_op jit(solution)/shard_map/ppermute | solution.py:352
  15.7 1.0 %copy-start.15 = (bf16[1,2,32,4096]{3,2,1,0:T(8,128)(2,1)S(1)}, bf16[1,2,32,4096]{3,2,1,0:T(8,128)(2,1)}, u32[]{:S(2)}) copy-start(bf16[1,2,32,4096]{3,2,1,0:T(8,128)(2,1)} %param.39) | copy-start | bytes 1572868
  16.8 1.0 %copy-start.16 = (bf16[1,2,32,4096]{3,2,1,0:T(8,128)(2,1)S(1)}, bf16[1,2,32,4096]{3,2,1,0:T(8,128)(2,1)}, u32[]{:S(2)}) copy-start(bf16[1,2,32,4096]{3,2,1,0:T(8,128)(2,1)} %param.38) | copy-start | bytes 1572868
  17.9 0.7 copy-start.10
  30.3 0.7 copy-start.9
  31.6 8.1 %copy-start.11 = (bf16[1040,128]{1,0:T(8,128)(2,1)S(1)}, bf16[1040,128]{1,0:T(8,128)(2,1)}, u32[]{:S(2)}) copy-start(bf16[1040,128]{1,0:T(8,128)(2,1)} %copy-done.10) | copy-start | bytes 798724
  31.6 10.9 %collective-permute-start.10 = (bf16[304,256]{1,0:T(8,128)(2,1)S(1)}, bf16[304,256]{1,0:T(8,128)(2,1)S(1)}, u32[]{:S(2)}, u32[]{:S(2)}) collective-permute-start(bf16[304,256]{1,0:T(8,128)(2,1)S(1)} %get-tuple-element.31), channel_id=1, source_target_pairs={{0,4},{2,6},{4,8},{6,10},{8,12},{10,14},{12,0},{14,2},{1,5},{3,7},... | collective-permute-start | bytes 466952 | tf_op jit(solution)/shard_map/ppermute | solution.py:355
  34.8 20.7 %collective-permute-start.6 = (bf16[304,256]{1,0:T(8,128)(2,1)S(1)}, bf16[304,256]{1,0:T(8,128)(2,1)S(1)}, u32[]{:S(2)}, u32[]{:S(2)}) collective-permute-start(bf16[304,256]{1,0:T(8,128)(2,1)S(1)} %get-tuple-element.25), channel_id=1, source_target_pairs={{0,12},{2,14},{4,0},{6,2},{8,4},{10,6},{12,8},{14,10},{1,13},{3,15... | collective-permute-start | bytes 466952 | tf_op jit(solution)/shard_map/ppermute | solution.py:355
  35.8 19.6 %collective-permute-start.8 = (bf16[304,256]{1,0:T(8,128)(2,1)S(1)}, bf16[304,256]{1,0:T(8,128)(2,1)S(1)}, u32[]{:S(2)}, u32[]{:S(2)}) collective-permute-start(bf16[304,256]{1,0:T(8,128)(2,1)S(1)} %get-tuple-element.28), channel_id=1, source_target_pairs={{0,8},{2,10},{4,12},{6,14},{8,0},{10,2},{12,4},{14,6},{1,9},{3,11}... | collective-permute-start | bytes 466952 | tf_op jit(solution)/shard_map/ppermute | solution.py:355
  36.3 19.9 %collective-permute-start.16 = (bf16[304,256]{1,0:T(8,128)(2,1)S(1)}, bf16[304,256]{1,0:T(8,128)(2,1)S(1)}, u32[]{:S(2)}, u32[]{:S(2)}) collective-permute-start(bf16[304,256]{1,0:T(8,128)(2,1)S(1)} %shard_map.235.kept), channel_id=1, source_target_pairs={{4,8},{6,10},{8,4},{10,6},{5,9},{7,11},{9,5},{11,7},{20,24},{22,26... | collective-permute-start | bytes 466952 | tf_op jit(solution)/shard_map/ppermute | solution.py:394
  38.2 27.1 %collective-permute-start.12 = (bf16[4,256,512]{2,1,0:T(8,128)(2,1)}, bf16[4,256,512]{2,1,0:T(8,128)(2,1)}, u32[]{:S(2)}, u32[]{:S(2)}) collective-permute-start(bf16[4,256,512]{2,1,0:T(8,128)(2,1)} %bitcast.10.refs_3_), channel_id=1, source_target_pairs={{0,2},{2,0},{4,6},{6,4},{8,10},{10,8},{12,14},{14,12},{1,3},{3,1},... | collective-permute-start | bytes 3145736 | tf_op jit(solution)/shard_map/ppermute | solution.py:352
  41.8 0.7 copy-start.3
  42.5 13.0 %copy-start.19 = (s32[8,4]{0,1:T(4,128)S(1)}, s32[8,4]{0,1:T(4,128)}, u32[]{:S(2)}) copy-start(s32[8,4]{0,1:T(4,128)} %param.33) | copy-start | bytes 388
  42.5 16.9 %collective-permute-start.11 = (bf16[272,256]{1,0:T(8,128)(2,1)}, bf16[272,256]{1,0:T(8,128)(2,1)}, u32[]{:S(2)}, u32[]{:S(2)}) collective-permute-start(bf16[272,256]{1,0:T(8,128)(2,1)} %get-tuple-element.32), channel_id=1, source_target_pairs={{0,4},{2,6},{4,8},{6,10},{8,12},{10,14},{12,0},{14,2},{1,5},{3,7},... | collective-permute-start | bytes 417800 | tf_op jit(solution)/shard_map/ppermute | solution.py:355
  55.4 7.8 %collective-permute-start.9 = (bf16[272,256]{1,0:T(8,128)(2,1)}, bf16[272,256]{1,0:T(8,128)(2,1)}, u32[]{:S(2)}, u32[]{:S(2)}) collective-permute-start(bf16[272,256]{1,0:T(8,128)(2,1)} %get-tuple-element.29), channel_id=1, source_target_pairs={{0,8},{2,10},{4,12},{6,14},{8,0},{10,2},{12,4},{14,6},{1,9},{3,11}... | collective-permute-start | bytes 417800 | tf_op jit(solution)/shard_map/ppermute | solution.py:355
  55.4 0.7 copy-start.20
  55.5 9.8 %collective-permute-start.7 = (bf16[272,256]{1,0:T(8,128)(2,1)}, bf16[272,256]{1,0:T(8,128)(2,1)}, u32[]{:S(2)}, u32[]{:S(2)}) collective-permute-start(bf16[272,256]{1,0:T(8,128)(2,1)} %get-tuple-element.26), channel_id=1, source_target_pairs={{0,12},{2,14},{4,0},{6,2},{8,4},{10,6},{12,8},{14,10},{1,13},{3,15... | collective-permute-start | bytes 417800 | tf_op jit(solution)/shard_map/ppermute | solution.py:355
  56.2 9.0 %copy-start.12 = (bf16[1040,128]{1,0:T(8,128)(2,1)S(1)}, bf16[1040,128]{1,0:T(8,128)(2,1)}, u32[]{:S(2)}) copy-start(bf16[1040,128]{1,0:T(8,128)(2,1)} %copy-done.10) | copy-start | bytes 798724
  56.3 18.0 %collective-permute-start.17 = (bf16[304,256]{1,0:T(8,128)(2,1)S(1)}, bf16[304,256]{1,0:T(8,128)(2,1)S(1)}, u32[]{:S(2)}, u32[]{:S(2)}) collective-permute-start(bf16[304,256]{1,0:T(8,128)(2,1)S(1)} %shard_map.236.kept), channel_id=1, source_target_pairs={{0,4},{2,6},{4,0},{6,2},{8,12},{10,14},{12,8},{14,10},{1,5},{3,7},... | collective-permute-start | bytes 466952 | tf_op jit(solution)/shard_map/ppermute | solution.py:394
  65.3 9.1 %copy-start.8 = (f32[4096]{0:T(1024)S(1)}, f32[4096]{0:T(1024)}, u32[]{:S(2)}) copy-start(f32[4096]{0:T(1024)} %param.44) | copy-start | bytes 49156
  70.9 3.3 %copy-start.5 = (bf16[272,256]{1,0:T(8,128)(2,1)}, bf16[272,256]{1,0:T(8,128)(2,1)S(1)}, u32[]{:S(2)}) copy-start(bf16[272,256]{1,0:T(8,128)(2,1)S(1)} %get-tuple-element.36.refs_7_) | copy-start | bytes 417796
  70.9 15.8 %collective-permute-start.13 = (bf16[272,256]{1,0:T(8,128)(2,1)}, bf16[272,256]{1,0:T(8,128)(2,1)}, u32[]{:S(2)}, u32[]{:S(2)}) collective-permute-start(bf16[272,256]{1,0:T(8,128)(2,1)} %get-tuple-element.37), channel_id=1, source_target_pairs={{0,12},{2,14},{4,0},{6,2},{8,4},{10,6},{12,8},{14,10},{1,13},{3,15... | collective-permute-start | bytes 417800 | tf_op jit(solution)/shard_map/ppermute | solution.py:355
  72.1 14.7 %collective-permute-start.14 = (bf16[272,256]{1,0:T(8,128)(2,1)}, bf16[272,256]{1,0:T(8,128)(2,1)}, u32[]{:S(2)}, u32[]{:S(2)}) collective-permute-start(bf16[272,256]{1,0:T(8,128)(2,1)} %get-tuple-element.38), channel_id=1, source_target_pairs={{0,8},{2,10},{4,12},{6,14},{8,0},{10,2},{12,4},{14,6},{1,9},{3,11}... | collective-permute-start | bytes 417800 | tf_op jit(solution)/shard_map/ppermute | solution.py:355
  72.1 14.7 %collective-permute-start.15 = (bf16[272,256]{1,0:T(8,128)(2,1)}, bf16[272,256]{1,0:T(8,128)(2,1)}, u32[]{:S(2)}, u32[]{:S(2)}) collective-permute-start(bf16[272,256]{1,0:T(8,128)(2,1)} %get-tuple-element.39), channel_id=1, source_target_pairs={{0,4},{2,6},{4,8},{6,10},{8,12},{10,14},{12,0},{14,2},{1,5},{3,7},... | collective-permute-start | bytes 417800 | tf_op jit(solution)/shard_map/ppermute | solution.py:355
  74.2 1.0 %copy-start.1 = (bf16[4096,32]{0,1:T(8,128)(2,1)S(1)}, bf16[4096,32]{0,1:T(8,128)(2,1)}, u32[]{:S(2)}) copy-start(bf16[4096,32]{0,1:T(8,128)(2,1)} %param.45) | copy-start | bytes 786436
  74.3 0.9 copy-start.2
  75.2 1.2 %copy-start.18 = (f32[16,4096]{1,0:T(8,128)S(1)}, f32[16,4096]{1,0:T(8,128)}, u32[]{:S(2)}) copy-start(f32[16,4096]{1,0:T(8,128)} %param.41) | copy-start | bytes 786436
  76.4 1.2 %collective-permute-start.18 = (f32[2,32,32]{2,1,0:T(8,128)S(1)}, f32[2,32,32]{2,1,0:T(8,128)S(1)}, u32[]{:S(2)}, u32[]{:S(2)}) collective-permute-start(f32[2,32,32]{2,1,0:T(8,128)S(1)} %shard_map.239), channel_id=1, source_target_pairs={{0,1},{1,0},{2,3},{3,2},{4,5},{5,4},{6,7},{7,6},{8,9},{9,8},{10,11... | collective-permute-start | bytes 24584 | tf_op jit(solution)/shard_map/ppermute | solution.py:450
  76.6 1.0 %copy-start.13 = (f32[4096]{0:T(1024)S(1)}, f32[4096]{0:T(1024)}, u32[]{:S(2)}) copy-start(f32[4096]{0:T(1024)} %param.40) | copy-start | bytes 49156
  76.7 1.0 %copy-start.14 = (f32[4096]{0:T(1024)S(1)}, f32[4096]{0:T(1024)}, u32[]{:S(2)}) copy-start(f32[4096]{0:T(1024)} %param.42) | copy-start | bytes 49156
  85.7 1.1 %copy-start.4 = (bf16[272,256]{1,0:T(8,128)(2,1)S(1)}, bf16[272,256]{1,0:T(8,128)(2,1)}, u32[]{:S(2)}) copy-start(bf16[272,256]{1,0:T(8,128)(2,1)} %copy-done.3) | copy-start | bytes 417796
  85.7 1.1 %copy-start.6 = (bf16[272,256]{1,0:T(8,128)(2,1)S(1)}, bf16[272,256]{1,0:T(8,128)(2,1)}, u32[]{:S(2)}) copy-start(bf16[272,256]{1,0:T(8,128)(2,1)} %copy-done.5) | copy-start | bytes 417796
  85.7 1.1 %copy-start.7 = (bf16[1,2,32,512]{3,2,1,0:T(8,128)(2,1)S(1)}, bf16[1,2,32,512]{3,2,1,0:T(8,128)(2,1)}, u32[]{:S(2)}) copy-start(bf16[1,2,32,512]{3,2,1,0:T(8,128)(2,1)} %param.24) | copy-start | bytes 196612

commit v3 on v2

--- a/solution.py
+++ b/solution.py
@@ -110,81 +110,104 @@
             out[rows:, :] = stat_block((pieces(low, 3) + [zero, zero]) * heads, wide)
 
 
-def blocks_body(heads, spans, slots, pair, *refs):
-    me, src, blk, own, nbr = refs[:5]
-    qs = refs[5 : 5 + spans]
-    outs = refs[5 + spans : 5 + 2 * spans]
-    acc, top, tot = refs[5 + 2 * spans :]
-    z, y = me[0] // pair, lax.rem(me[0], pair)
+def blocks_body(last, heads, spans, slots, pair, *refs):
+    me, src, blk, pool = refs[:4]
+    qs = refs[4 : 4 + spans]
+    refs = refs[4 + spans :]
+    if last:
+        before, outs, (top, tot, acc) = refs[:3], refs[3 : 3 + spans], refs[3 + spans :]
+    else:
+        top, tot, acc = refs
+    z = me[0] // pair
     rows = heads * HD
     full = qs[0].shape[0] - STAT
-    wide = outs[0].shape[1]
+    wide = acc.shape[-1]
     ctxs = [jnp.max(q[full:, :].astype(F32)) for q in qs]
-    for k, (q, out, ctx) in enumerate(zip(qs, outs, ctxs)):
-        reader = lax.rem(z + (spans - k), spans) * pair + y
-        acc[...] = jnp.zeros_like(acc)
+    if last:
+        for ref, old in zip((top, tot, acc), before):
+            ref[...] = old[...]
+    else:
         top[...] = jnp.full(top.shape, LOW, F32)
         tot[...] = jnp.zeros_like(tot)
-
-        def slot(j, carry, q=q, reader=reader, ctx=ctx):
+        acc[...] = jnp.zeros_like(acc)
+    for k, (q, ctx) in enumerate(zip(qs, ctxs)):
+        reader = lax.rem(z + (spans - k), spans) * pair + lax.rem(me[0], pair)
+
+        def slot(j, carry, k=k, q=q, reader=reader, ctx=ctx):
             source = src[reader, j]
-            live = (source // pair == z) & (j.astype(F32) < ctx)
-
-            @pl.when(live)
+            held = (source // pair == z) & (source != me[0]) if last else source == me[0]
+
+            @pl.when(held & (j.astype(F32) < ctx))
             def _():
                 b = blk[reader, j]
-                mine = lax.rem(source, pair) == y
                 for h in range(heads):
-                    at = slice(2 * h * HD, 2 * (h + 1) * HD)
-                    kv = jnp.where(mine, own[b, :, at], nbr[b, :, at])
+                    kv = pool[b, :, 2 * h * HD : 2 * (h + 1) * HD]
                     lo = full // 2 + h * wide
-                    done = [(top[h], tot[h], acc[h])]
-                    top[h], tot[h], acc[h] = folded_softmax(done, kv, 0, q[lo : lo + wide, :])
+                    done = [(top[k, h], tot[k, h], acc[k, h])]
+                    top[k, h], tot[k, h], acc[k, h] = folded_softmax(done, kv, 0, q[lo : lo + wide, :])
 
             return carry
 
         lax.fori_loop(0, slots, slot, 0)
-        stats = []
-        for h in range(heads):
-            out[h * HD : (h + 1) * HD, :] = acc[h].astype(BF16)
-            stats += pieces(top[h], 3) + pieces(tot[h], 2)
-        out[rows:, :] = stat_block(stats, wide)
-
-
-def join_body(heads, spans, *refs):
-    flag, q, new = refs[:3]
-    parts = [refs[3 : 3 + spans], refs[3 + spans : 3 + 2 * spans]]
-    out = refs[3 + 2 * spans]
+    if last:
+        for k, out in enumerate(outs):
+            stats = []
+            for h in range(heads):
+                out[h * HD : (h + 1) * HD, :] = acc[k, h].astype(BF16)
+                stats += pieces(top[k, h], 3) + pieces(tot[k, h], 2)
+            out[rows:, :] = stat_block(stats, wide)
+
+
+def fresh_softmax(new, r, h, q):
+    fresh, wide = new.shape[1], q.shape[0]
+    s = dot(new[r, :, 2 * h * HD : (2 * h + 1) * HD], q, 1, 1)
+    key = lax.broadcasted_iota(jnp.int32, (fresh, wide), 0)
+    token = lax.rem(lax.broadcasted_iota(jnp.int32, (fresh, wide), 1), fresh)
+    seen = key <= token
+    m = jnp.max(jnp.where(seen, s, LOW), axis=0, keepdims=True)
+    p = jnp.where(seen, jnp.exp2((s - m) * SCORE2), 0.0)
+    o = dot(new[r, :, (2 * h + 1) * HD : (2 * h + 2) * HD], p.astype(BF16), 0, 0)
+    return m, jnp.sum(p, axis=0, keepdims=True), o
+
+
+def join(parts):
+    m = functools.reduce(jnp.maximum, [part[0] for part in parts])
+    fades = [jnp.exp2((part[0] - m) * SCORE2) for part in parts]
+    total = sum(f * part[1] for f, part in zip(fades, parts))
+    return jnp.transpose(sum(f * part[2] for f, part in zip(fades, parts)) / total).astype(BF16)
+
+
+def part_of(ref, heads, h):
+    m, l = stats_of(ref, heads * HD, h)
+    return m, l, ref[h * HD : (h + 1) * HD, :].astype(F32)
+
+
+def join0_body(heads, spans, flag, q, new, *refs):
+    parts, (out, top, tot, acc) = refs[:spans], refs[spans:]
     fresh = new.shape[1]
-    half = q.shape[0] - STAT
-    wide = half // (2 * heads)
-    rows = heads * HD
-    for r in range(2):
-        for h in range(heads):
-            lo = r * half // 2 + h * wide
-            s = dot(new[r, :, 2 * h * HD : (2 * h + 1) * HD], q[lo : lo + wide, :], 1, 1)
-            key = lax.broadcasted_iota(jnp.int32, (fresh, wide), 0)
-            token = lax.rem(lax.broadcasted_iota(jnp.int32, (fresh, wide), 1), fresh)
-            seen = key <= token
-            s = jnp.where(seen, s, LOW)
-            best = jnp.max(s, axis=0, keepdims=True)
-            at = h * HD
-            stats = [stats_of(part, rows, h) for part in parts[r]]
-            if r == 0:
-                stats = [(jnp.where(flag[0] > 0, m, LOW), l) for m, l in stats]
-            for m, _ in stats:
-                best = jnp.maximum(best, m)
-            p = jnp.where(seen, jnp.exp2((s - best) * SCORE2), 0.0)
-            total = jnp.sum(p, axis=0, keepdims=True)
-            o = dot(new[r, :, (2 * h + 1) * HD : (2 * h + 2) * HD], p.astype(BF16), 0, 0)
-            for part, (m, l) in zip(parts[r], stats):
-                w = jnp.exp2((m - best) * SCORE2)
-                total = total + w * l
-                o = o + w * part[at : at + HD, :].astype(F32)
-            done = jnp.transpose(o / total).astype(BF16)
-            for g in range(Q_PER_KV):
-                col = (h * Q_PER_KV + g) * HD
-                out[r, :, col : col + HD] = done[g * fresh : (g + 1) * fresh, :]
+    wide = acc.shape[-1]
+    half = heads * wide
+    for h in range(heads):
+        found = [fresh_softmax(new, 0, h, q[h * wide : (h + 1) * wide, :])]
+        for part in parts:
+            m, l, o = part_of(part, heads, h)
+            found.append((jnp.where(flag[0] > 0, m, LOW), l, o))
+        done = join(found)
+        for g in range(Q_PER_KV):
+            col = (h * Q_PER_KV + g) * HD
+            out[:, col : col + HD] = done[g * fresh : (g + 1) * fresh, :]
+        top[h], tot[h], acc[h] = fresh_softmax(new, 1, h, q[half + h * wide : half + (h + 1) * wide, :])
+
+
+def join1_body(heads, spans, first, top, tot, acc, *refs):
+    parts, out = refs[:spans], refs[spans]
+    fresh = first.shape[0]
+    out[0] = first[...]
+    for h in range(heads):
+        done = join([(top[h], tot[h], acc[h])] + [part_of(part, heads, h) for part in parts])
+        for g in range(Q_PER_KV):
+            col = (h * Q_PER_KV + g) * HD
+            out[1, :, col : col + HD] = done[g * fresh : (g + 1) * fresh, :]
 
 
 def reach(away, spans, rounds, here):
@@ -253,48 +276,51 @@
         out[r] = total[r]
 
 
-def scan_body(state, flag, bc, st0, st1, x, dt, zg, dtb, alog, gain, w, b, out, pad, step, push, res, dec):
-    taps = w.shape[0]
-    keep = taps - 1
-    length = x.shape[1]
-    sub = x.shape[2]
+def ready_body(x, dt, zg, dtb, alog, w, b, step, act, gate, dec):
+    taps, length = w.shape[0], x.shape[1]
+    dec[...] = jnp.exp(alog[...]) * (-LOG2E)
+    for r in range(2):
+
+        def basics(t, carry, r=r):
+            raw = dt[r, t].astype(F32) + dtb[...]
+            step[r, t] = jnp.maximum(raw, 0.0) + jnp.log1p(jnp.exp(-jnp.abs(raw)))
+            gate[r, t] = silu(zg[r, t].astype(F32))
+            return carry
+
+        lax.fori_loop(0, length, basics, 0, unroll=4)
+
+        def total(t, first, r=r):
+            acc = b[...]
+            for k in range(first, taps):
+                acc = acc + w[k] * x[r, t + k - taps + 1].astype(F32)
+            return acc
+
+        for t in range(taps - 1):
+            act[r, t] = total(t, taps - 1 - t)
+
+        def later(t, carry, r=r):
+            act[r, t] = silu(total(t, 0))
+            return carry
+
+        lax.fori_loop(taps - 1, length, later, 0)
+
+
+def scan_body(state, flag, bc, st0, st1, step, act, gate, dec, gain, w, out):
+    keep = w.shape[0] - 1
+    length, sub = step.shape[1], step.shape[2]
     block = 16
-    dec[...] = jnp.exp(alog[...]) * (-LOG2E)
-    for r, st in enumerate((st0, st1)):
-        first = st[state : state + keep].astype(F32)
-        if r == 0:
-            first = jnp.where(flag[0] > 0, first, 0.0)
-        pad[0:keep] = first
-        pad[keep:] = x[r].astype(F32)
-
-        def prepare(t, carry, r=r):
-            acc = b[...] + w[0] * pad[t]
-            for k in range(1, taps):
-                acc = acc + w[k] * pad[t + k]
-            sig = silu(acc)
-            raw = dt[r, t].astype(F32) + dtb[...]
-            now = jnp.maximum(raw, 0.0) + jnp.log1p(jnp.exp(-jnp.abs(raw)))
-            step[r, t] = now
-            push[r, t] = now * sig
-            res[r, t] = gain[...] * sig
-            return carry
-
-        lax.fori_loop(0, length, prepare, 0, unroll=4)
-
     for r, st in enumerate((st0, st1)):
         for c in range(0, sub, block):
             at = slice(c, c + block)
-            start = []
-            for n in range(state):
-                h = st[n, at, :].astype(F32)
-                if r == 0:
-                    h = jnp.where(flag[0] > 0, h, 0.0)
-                start.append(h)
-
-            def advance(t, hs, r=r, at=at):
+
+            def held(n, r=r, st=st, at=at):
+                value = st[n, at, :].astype(F32)
+                return jnp.where(flag[0] > 0, value, 0.0) if r == 0 else value
+
+            def advance(t, hs, sig, r=r, at=at):
                 now = step[r, t, at, :]
-                add = push[r, t, at, :]
-                sums = [res[r, t, at, :], None, None, None]
+                add = now * sig
+                sums = [gain[at, :] * sig, None, None, None]
                 after = []
                 for n in range(state):
                     h = jnp.exp2(now * dec[n, at, :]) * hs[n] + bc[r * length + t, n] * add
@@ -303,11 +329,23 @@
                     sums[i] = term if sums[i] is None else sums[i] + term
                     after.append(h)
                 y = (sums[0] + sums[1]) + (sums[2] + sums[3])
-                gate = silu(zg[r, t, at, :].astype(F32))
-                out[r, t, at, :] = (y * gate).astype(BF16)
+                out[r, t, at, :] = (y * gate[r, t, at, :]).astype(BF16)
                 return tuple(after)
 
-            lax.fori_loop(0, length, advance, tuple(start), unroll=2)
+            hs = tuple(held(n) for n in range(state))
+            peel = keep + (length - keep) % 2
+            for t in range(peel):
+                sig = act[r, t, at, :]
+                if t < keep:
+                    for k in range(keep - t):
+                        sig = sig + w[k, at, :] * held(state + t + k)
+                    sig = silu(sig)
+                hs = advance(t, hs, sig)
+
+            def body(t, hs, r=r, at=at, advance=advance):
+                return advance(t, hs, act[r, t, at, :])
+
+            lax.fori_loop(peel, length, body, hs, unroll=2)
 
 
 def local(
@@ -376,6 +414,12 @@
     asked = [message] + [turn(message, k) for k in range(1, spans)]
 
     x_t, dt_t, z_t = tiled(mamba_x[0]), tiled(mamba_dt[0]), tiled(mamba_z[0])
+    f32_rows = jax.ShapeDtypeStruct((2, length, sub, HD), F32)
+    prepared = call(
+        ready_body,
+        [f32_rows] * 3 + [jax.ShapeDtypeStruct((state, sub, HD), F32)],
+        [VSPEC] * 7,
+    )(x_t, dt_t, z_t, tiled(dt_bias), tiled(a_log), tiled(conv_w), tiled(conv_b))
     prefix_nbr = across(cached_lookup_pairs[0])
 
     one = jax.ShapeDtypeStruct((unit, cols), BF16)
@@ -385,6 +429,8 @@
             functools.partial(shared_body, spans, pair, unit, rounds),
             one,
             [SSPEC] * 2 + [VSPEC] * 2,
+            (),
+            pl.CostEstimate(flops=50 * 10**9, bytes_accessed=150 * 10**6, transcendentals=0) if rounds == 0 else None,
         )(me, owner_id, kept, came)
 
     def hop(value, r):
@@ -402,7 +448,7 @@
         [SSPEC] * 2 + [VSPEC] * 2,
         (),
         pl.CostEstimate(flops=50 * 10**9, bytes_accessed=150 * 10**6, transcendentals=0),
-    )(after(me, x_t, dt_t, z_t, *asked[1:], *hops[:1]), state_src, states, states_nbr)
+    )(after(me, *prepared, *asked[1:], *hops[:1]), state_src, states, states_nbr)
     came = [sent[0]] + [turn(sent[k], k) for k in range(1, spans)]
     state1 = call(
         functools.partial(state_take_body, spans, pair),
@@ -416,23 +462,13 @@
         [part_shape] * spans,
         [SSPEC] * 2 + [VSPEC] * (2 + spans),
         [pltpu.VMEM(cached_lookup_pairs.shape[1:], BF16)],
-        pl.CostEstimate(flops=50 * 10**9, bytes_accessed=150 * 10**6, transcendentals=0),
+        pl.CostEstimate(flops=10**6, bytes_accessed=10**4, transcendentals=0),
     )(me, owner_id, cached_lookup_pairs[0], prefix_nbr, *asked)
     for r in range(1, spans):
-        state0 = shared(r, state0, hops[-1])
+        state0 = shared(r, after(state0, part0[0]) if r > 1 else state0, hops[-1])
         if r < spans - 1:
             hops.append(hop(after(state0, sent[0]), r))
     got0 = [part0[0]] + [turn(after(part0[k], came[spans - k]), spans - k) for k in range(1, spans)]
-
-    pool_nbr = across(after(pool_kv[0], sent[0]))
-    part1 = call(
-        functools.partial(blocks_body, heads, spans, slots, pair),
-        [part_shape] * spans,
-        [SSPEC] * 3 + [VSPEC] * (2 + spans),
-        [pltpu.VMEM((heads, HD, wide), F32), pltpu.VMEM((heads, 1, wide), F32), pltpu.VMEM((heads, 1, wide), F32)],
-        pl.CostEstimate(flops=20 * 10**9, bytes_accessed=60 * 10**6, transcendentals=0),
-    )(after(me, *got0[1:]), restore_src, restore_blk, pool_kv[0], pool_nbr, *asked)
-    got1 = [part1[0]] + [turn(part1[k], spans - k) for k in range(1, spans)]
 
     first = state * inner // cols
 
@@ -449,41 +485,46 @@
     )(readers, taps_of(state0), taps_of(state1), mamba_x[0], conv_w, conv_b[None], w_bc.T)
     both = partial + lax.ppermute(partial, "channel", [(0, 1), (1, 0)])
     bc = both.reshape(2 * length, w_bc.shape[1])
+    pool_nbr = across(pool_kv[0])
+    kept = [
+        jax.ShapeDtypeStruct((spans, heads, 1, wide), F32),
+        jax.ShapeDtypeStruct((spans, heads, 1, wide), F32),
+        jax.ShapeDtypeStruct((spans, heads, HD, wide), F32),
+    ]
+    before = call(
+        functools.partial(blocks_body, False, heads, spans, slots, pair),
+        kept,
+        [SSPEC] * 3 + [VSPEC] * (1 + spans),
+    )(after(me, part0[0]), restore_src, restore_blk, pool_kv[0], *asked)
+    fresh_shape = jax.ShapeDtypeStruct((length, heads * Q_PER_KV * HD), BF16)
+    joined = call(
+        functools.partial(join0_body, heads, spans),
+        [fresh_shape] + [jax.ShapeDtypeStruct(v.shape[1:], F32) for v in kept],
+        [SSPEC] + [VSPEC] * (2 + spans),
+    )(readers, message, new_kv[0], *got0)
+    part1 = call(
+        functools.partial(blocks_body, True, heads, spans, slots, pair),
+        [part_shape] * spans,
+        [SSPEC] * 3 + [VSPEC] * (4 + spans),
+        [pltpu.VMEM(v.shape, F32) for v in kept],
+        pl.CostEstimate(flops=20 * 10**9, bytes_accessed=60 * 10**6, transcendentals=0),
+    )(after(me, bc, *got0[1:]), restore_src, restore_blk, pool_nbr, *asked, *before)
+    got1 = [part1[0]] + [turn(part1[k], spans - k) for k in range(1, spans)]
+
     scan_out = call(
         functools.partial(scan_body, state),
         jax.ShapeDtypeStruct((2, length, sub, HD), BF16),
-        [SSPEC] * 2 + [VSPEC] * 10,
-        [
-            pltpu.VMEM((length + keep, sub, HD), F32),
-            pltpu.VMEM((2, length, sub, HD), F32),
-            pltpu.VMEM((2, length, sub, HD), F32),
-            pltpu.VMEM((2, length, sub, HD), F32),
-            pltpu.VMEM((state, sub, HD), F32),
-        ],
+        [SSPEC] * 2 + [VSPEC] * 8,
+        (),
         pl.CostEstimate(flops=2 * length * inner * state * 6, bytes_accessed=4 << 20, transcendentals=2 * length * inner * state),
-    )(
-        readers,
-        bc,
-        state0.reshape(rows, sub, HD),
-        state1.reshape(rows, sub, HD),
-        x_t,
-        dt_t,
-        z_t,
-        tiled(dt_bias),
-        tiled(a_log),
-        tiled(bypass_gain),
-        tiled(conv_w),
-        tiled(conv_b),
-    )
+    )(readers, bc, state0.reshape(rows, sub, HD), state1.reshape(rows, sub, HD), *prepared, tiled(bypass_gain), tiled(conv_w))
     mamba_out = scan_out.reshape(1, 2, length, inner)
 
     attention_out = call(
-        functools.partial(join_body, heads, spans),
-        jax.ShapeDtypeStruct((2, length, heads * Q_PER_KV * HD), BF16),
-        [SSPEC] + [VSPEC] * (2 + 2 * spans),
-        (),
-        pl.CostEstimate(flops=1 << 24, bytes_accessed=2 << 20, transcendentals=1 << 16),
-    )(readers, message, new_kv[0], *got0, *got1)[None]
+        functools.partial(join1_body, heads, spans),
+        jax.ShapeDtypeStruct((2,) + fresh_shape.shape, BF16),
+        [VSPEC] * (4 + spans),
+    )(*joined, *got1)[None]
     return (attention_out, mamba_out)
 
 

time: 90.3 us -> 87.4 us (0.968)
  waiting for transfers between devices: 30.4 us -> 9.98 us
  starting transfers between devices: 26.7 us -> 38.3 us
  local copies, waits for them, and re-layouts: 7.31 us -> 13.1 us
    ppermute x12, waiting for transfers between devices: 24.9 us -> 3.71 us  [turn(): lax.ppermute(value, axis, [(s, (s + k * pair) % size) for s in range(size)])]
    ppermute x12, starting transfers between devices: 15 us -> 28.2 us  [turn(): lax.ppermute(value, axis, [(s, (s + k * pair) % size) for s in range(size)])]
    unnamed x50 -> x68, local copies, waits for them, and re-layouts: 5.85 us -> 11.7 us
    pallas_call x2 -> x5, Pallas kernels: 8.6 us -> 11.2 us  [the longest x1 3.98 us: local(): call(functools.partial(blocks_body, True, heads, spans, slots, pair), [pa...]
    ppermute x3, waiting for transfers between devices: 1.48 us -> 3.12 us  [across(): return lax.ppermute(value, axis, [(s, s ^ 1) for s in range(size)])]
    pallas_call x1, Pallas kernels: 8.06 us -> 6.56 us  [local(): call(functools.partial(scan_body, state), jax.ShapeDtypeStruct((2, length...]
    pallas_call x1, Pallas kernels: 2.13 us -> 0.84 us  [local(): call(functools.partial(prefix_body, heads, spans, pair), [part_shape] * s...]
    ppermute x1, waiting for transfers between devices: 0.96 us -> 0.01 us  [local(): both = partial + lax.ppermute(partial, 'channel', [(0, 1), (1, 0)])]
  transfers between devices with their start and end apart: 19 -> 19, of which waited for: 8 -> 4; matrix products, arithmetic and copies ran while one was open for 2% -> 2% of each run, Pallas kernels for 20% -> 19%
where the time goes in v3:
time: 87.4 us; the launch traced here: 86.7 us
  starting transfers between devices  38.3 us (44%)
  Pallas kernels  21.1 us (24%)
  local copies, waits for them, and re-layouts  13.1 us (15%)
  waiting for transfers between devices  9.98 us (11%)
  between operations  3.04 us (3%)
  other arithmetic  1.09 us (1%)
    ppermute x12, starting transfers between devices, turn(): lax.ppermute(value, axis, [(s, (s + k * pair) % size) for s in range(size)])  28.2 us
    unnamed x68, local copies, waits for them, and re-layouts  11.7 us
    pallas_call x1, Pallas kernels, local(): call(functools.partial(scan_body, state), jax.ShapeDtypeStruct((2, length...  6.56 us
    ppermute x3, starting transfers between devices, across(): return lax.ppermute(value, axis, [(s, s ^ 1) for s in range(size)])  5.12 us
    ppermute x3, starting transfers between devices, hop(): return lax.ppermute(value, axis, links)  4.92 us
    pallas_call x1, Pallas kernels, local(): call(functools.partial(blocks_body, True, heads, spans, slots, pair), [pa...  3.98 us
    ppermute x12, waiting for transfers between devices, turn(): lax.ppermute(value, axis, [(s, (s + k * pair) % size) for s in range(size)])  3.71 us
    ppermute x3, waiting for transfers between devices, hop(): return lax.ppermute(value, axis, links)  3.16 us
  transfers between devices with their start and end apart: 19, of which 4 were waited for; matrix products, arithmetic and copies ran while one was open for 2% of the time, Pallas kernels for 19%

profile of v3, /device:TPU:0, one launch (start us, length us, event | category | flops | bytes accessed | tf_op | source)
XLA Modules:
  0.0 86.7 jit_solution(2880199676515736578)
XLA Ops:
  0.6 1.1 %pad_maximum_fusion = bf16[38,4096]{1,0:T(8,128)(2,1)S(1)} fusion(bf16[3,4096]{1,0:T(4,128)(2,1)} %bitcast.77, bf16[16,4096]{1,0:T(8,128)(2,1)} %bitcast.75, bf16[3,4096]{1,0:T(4,128)(2,1)} %bitcast.78, bf16[16,4096]{1,0:T(8,128)(2,1)} %bitcast.76), kind=kLoop, calls=%fused_computation | loop fusion | flops 1245184 | bytes 622592 | tf_op jit(solution)/shard_map/concatenate | solution.py:406
  1.7 0.2 reshape.50.kept.own
  1.9 3.0 %collective-permute-start.4 = (bf16[608,256]{1,0:T(8,128)(2,1)S(1)}, bf16[608,256]{1,0:T(8,128)(2,1)S(1)}, u32[]{:S(2)}, u32[]{:S(2)}) collective-permute-start(bf16[608,256]{1,0:T(8,128)(2,1)S(1)} %reshape.50.kept.own), channel_id=1, source_target_pairs={{0,2},{2,0},{4,6},{6,4},{8,10},{10,8},{12,14},{14,12},{1,3},{3,1},... | collective-permute-start | bytes 933896 | tf_op jit(solution)/shard_map/ppermute | solution.py:390
  5.8 1.6 %collective-permute-start.1 = (bf16[1040,128]{1,0:T(8,128)(2,1)S(1)}, bf16[1040,128]{1,0:T(8,128)(2,1)S(1)}, u32[]{:S(2)}, u32[]{:S(2)}) collective-permute-start(bf16[1040,128]{1,0:T(8,128)(2,1)S(1)} %concatenate.6.refs_4_.q), channel_id=1, source_target_pairs={{0,4},{2,6},{4,8},{6,10},{8,12},{10,14},{12,0},{14,2},{1,5},{3,7},... | collective-permute-start | bytes 798728 | tf_op jit(solution)/shard_map/ppermute | solution.py:393
  7.4 2.6 %collective-permute-start.2 = (bf16[1040,128]{1,0:T(8,128)(2,1)S(1)}, bf16[1040,128]{1,0:T(8,128)(2,1)S(1)}, u32[]{:S(2)}, u32[]{:S(2)}) collective-permute-start(bf16[1040,128]{1,0:T(8,128)(2,1)S(1)} %concatenate.6.refs_4_.q), channel_id=1, source_target_pairs={{0,8},{2,10},{4,12},{6,14},{8,0},{10,2},{12,4},{14,6},{1,9},{3,11}... | collective-permute-start | bytes 798728 | tf_op jit(solution)/shard_map/ppermute | solution.py:393
  10.0 1.3 %collective-permute-start.3 = (bf16[1040,128]{1,0:T(8,128)(2,1)S(1)}, bf16[1040,128]{1,0:T(8,128)(2,1)S(1)}, u32[]{:S(2)}, u32[]{:S(2)}) collective-permute-start(bf16[1040,128]{1,0:T(8,128)(2,1)S(1)} %concatenate.6.refs_4_.q), channel_id=1, source_target_pairs={{0,12},{2,14},{4,0},{6,2},{8,4},{10,6},{12,8},{14,10},{1,13},{3,15... | collective-permute-start | bytes 798728 | tf_op jit(solution)/shard_map/ppermute | solution.py:393
  12.0 0.3 collective-permute-done.4.came.nbr
  12.4 0.7 copy-done.19
  13.1 1.8 %collective-permute-start.5 = (bf16[304,256]{1,0:T(8,128)(2,1)S(1)}, bf16[304,256]{1,0:T(8,128)(2,1)S(1)}, u32[]{:S(2)}, u32[]{:S(2)}) collective-permute-start(bf16[304,256]{1,0:T(8,128)(2,1)S(1)} %shard_map.232.kept), channel_id=1, source_target_pairs={{0,4},{2,6},{4,0},{6,2},{8,12},{10,14},{12,8},{14,10},{1,5},{3,7},... | collective-permute-start | bytes 466952 | tf_op jit(solution)/shard_map/ppermute | solution.py:440
  14.8 1.5 %collective-permute-start = (bf16[1024,512]{1,0:T(8,128)(2,1)S(1)}, bf16[1024,512]{1,0:T(8,128)(2,1)S(1)}, u32[]{:S(2)}, u32[]{:S(2)}) collective-permute-start(bf16[1024,512]{1,0:T(8,128)(2,1)S(1)} %bitcast.55), channel_id=1, source_target_pairs={{0,2},{2,0},{4,6},{6,4},{8,10},{10,8},{12,14},{14,12},{1,3},{3,1},... | collective-permute-start | bytes 3145736 | tf_op jit(solution)/shard_map/ppermute | solution.py:390
  16.5 0.9 %copy-done.24 = bf16[1,2,32,4096]{3,2,1,0:T(8,128)(2,1)S(1)} copy-done((bf16[1,2,32,4096]{3,2,1,0:T(8,128)(2,1)S(1)}, bf16[1,2,32,4096]{3,2,1,0:T(8,128)(2,1)}, u32[]{:S(2)}) %copy-start.24) | copy-done | bytes 524312
  17.5 0.9 %copy-done.25 = bf16[1,2,32,4096]{3,2,1,0:T(8,128)(2,1)S(1)} copy-done((bf16[1,2,32,4096]{3,2,1,0:T(8,128)(2,1)S(1)}, bf16[1,2,32,4096]{3,2,1,0:T(8,128)(2,1)}, u32[]{:S(2)}) %copy-start.25) | copy-done | bytes 524312
  18.6 0.8 copy-done.27
  19.5 0.6 copy-done.9
  20.2 2.6 %shard_map.231 = (f32[2,32,32,128]{3,2,1,0:T(8,128)S(1)}, f32[2,32,32,128]{3,2,1,0:T(8,128)S(1)}, f32[2,32,32,128]{3,2,1,0:T(8,128)S(1)}, f32[16,32,128]{2,1,0:T(8,128)S(1)}) custom-call(bf16[2,32,32,128]{3,2,1,0:T(8,128)(2,1)S(1)} %bitcast.50, bf16[2,32,32,128]{3,2,1,0:T(8,128)(2,1)S(1)} %bitcast.51, bf16[2,32,32,128]{3,2,1,0:T(8,128)(2,1)S(1)} %bitcast.52, ...), custom_call_target="tpu_custom_call" | custom-call | tf_op jit(solution)/shard_map/pallas_call | solution.py:418
  22.9 0.6 collective-permute-start.15
  23.5 3.7 %collective-permute-done.2.refs_6_ = bf16[1040,128]{1,0:T(8,128)(2,1)S(1)} collective-permute-done((bf16[1040,128]{1,0:T(8,128)(2,1)S(1)}, bf16[1040,128]{1,0:T(8,128)(2,1)S(1)}, u32[]{:S(2)}, u32[]{:S(2)}) %collective-permute-start.2) | collective-permute-done | bytes 266272 | tf_op jit(solution)/shard_map/ppermute | solution.py:393
  27.1 3.2 %collective-permute-done.5.came = bf16[304,256]{1,0:T(8,128)(2,1)S(1)} collective-permute-done((bf16[304,256]{1,0:T(8,128)(2,1)S(1)}, bf16[304,256]{1,0:T(8,128)(2,1)S(1)}, u32[]{:S(2)}, u32[]{:S(2)}) %collective-permute-start.5) | collective-permute-done | bytes 155680 | tf_op jit(solution)/shard_map/ppermute | solution.py:440
  30.3 0.7 copy-done.12
  30.9 0.6 shard_map.233
  31.6 0.7 collective-permute-start.12
  32.3 4.3 %collective-permute-start.10 = (bf16[304,256]{1,0:T(8,128)(2,1)S(1)}, bf16[304,256]{1,0:T(8,128)(2,1)S(1)}, u32[]{:S(2)}, u32[]{:S(2)}) collective-permute-start(bf16[304,256]{1,0:T(8,128)(2,1)S(1)} %get-tuple-element.48), channel_id=1, source_target_pairs={{0,4},{2,6},{4,8},{6,10},{8,12},{10,14},{12,0},{14,2},{1,5},{3,7},... | collective-permute-start | bytes 466952 | tf_op jit(solution)/shard_map/ppermute | solution.py:393
  36.6 1.5 %collective-permute-start.8 = (bf16[304,256]{1,0:T(8,128)(2,1)S(1)}, bf16[304,256]{1,0:T(8,128)(2,1)S(1)}, u32[]{:S(2)}, u32[]{:S(2)}) collective-permute-start(bf16[304,256]{1,0:T(8,128)(2,1)S(1)} %get-tuple-element.45), channel_id=1, source_target_pairs={{0,8},{2,10},{4,12},{6,14},{8,0},{10,2},{12,4},{14,6},{1,9},{3,11}... | collective-permute-start | bytes 466952 | tf_op jit(solution)/shard_map/ppermute | solution.py:393
  38.2 2.8 %collective-permute-done.refs_3_ = bf16[1024,512]{1,0:T(8,128)(2,1)S(1)} collective-permute-done((bf16[1024,512]{1,0:T(8,128)(2,1)S(1)}, bf16[1024,512]{1,0:T(8,128)(2,1)S(1)}, u32[]{:S(2)}, u32[]{:S(2)}) %collective-permute-start) | collective-permute-done | bytes 1048608 | tf_op jit(solution)/shard_map/ppermute | solution.py:390
  40.9 2.6 %collective-permute-start.6 = (bf16[304,256]{1,0:T(8,128)(2,1)S(1)}, bf16[304,256]{1,0:T(8,128)(2,1)S(1)}, u32[]{:S(2)}, u32[]{:S(2)}) collective-permute-start(bf16[304,256]{1,0:T(8,128)(2,1)S(1)} %get-tuple-element.42), channel_id=1, source_target_pairs={{0,12},{2,14},{4,0},{6,2},{8,4},{10,6},{12,8},{14,10},{1,13},{3,15... | collective-permute-start | bytes 466952 | tf_op jit(solution)/shard_map/ppermute | solution.py:393
  43.6 0.8 shard_map.230
  44.5 0.6 copy-done.7
  45.1 2.4 %collective-permute-start.13 = (bf16[304,256]{1,0:T(8,128)(2,1)S(1)}, bf16[304,256]{1,0:T(8,128)(2,1)S(1)}, u32[]{:S(2)}, u32[]{:S(2)}) collective-permute-start(bf16[304,256]{1,0:T(8,128)(2,1)S(1)} %shard_map.236.kept), channel_id=1, source_target_pairs={{0,4},{2,6},{4,0},{6,2},{8,12},{10,14},{12,8},{14,10},{1,5},{3,7},... | collective-permute-start | bytes 466952 | tf_op jit(solution)/shard_map/ppermute | solution.py:440
  47.5 3.4 %collective-permute-start.11 = (bf16[272,256]{1,0:T(8,128)(2,1)}, bf16[272,256]{1,0:T(8,128)(2,1)}, u32[]{:S(2)}, u32[]{:S(2)}) collective-permute-start(bf16[272,256]{1,0:T(8,128)(2,1)} %get-tuple-element.49), channel_id=1, source_target_pairs={{0,4},{2,6},{4,8},{6,10},{8,12},{10,14},{12,0},{14,2},{1,5},{3,7},... | collective-permute-start | bytes 417800 | tf_op jit(solution)/shard_map/ppermute | solution.py:393
  50.9 1.9 %collective-permute-start.9 = (bf16[272,256]{1,0:T(8,128)(2,1)}, bf16[272,256]{1,0:T(8,128)(2,1)}, u32[]{:S(2)}, u32[]{:S(2)}) collective-permute-start(bf16[272,256]{1,0:T(8,128)(2,1)} %get-tuple-element.46), channel_id=1, source_target_pairs={{0,8},{2,10},{4,12},{6,14},{8,0},{10,2},{12,4},{14,6},{1,9},{3,11}... | collective-permute-start | bytes 417800 | tf_op jit(solution)/shard_map/ppermute | solution.py:393
  52.9 4.4 %collective-permute-start.7 = (bf16[272,256]{1,0:T(8,128)(2,1)}, bf16[272,256]{1,0:T(8,128)(2,1)}, u32[]{:S(2)}, u32[]{:S(2)}) collective-permute-start(bf16[272,256]{1,0:T(8,128)(2,1)} %get-tuple-element.43), channel_id=1, source_target_pairs={{0,12},{2,14},{4,0},{6,2},{8,4},{10,6},{12,8},{14,10},{1,13},{3,15... | collective-permute-start | bytes 417800 | tf_op jit(solution)/shard_map/ppermute | solution.py:393
  57.9 0.6 shard_map.238
  58.6 0.7 copy-done.5
  59.2 0.9 %copy-done.6 = bf16[304,256]{1,0:T(8,128)(2,1)S(1)} copy-done((bf16[304,256]{1,0:T(8,128)(2,1)S(1)}, bf16[304,256]{1,0:T(8,128)(2,1)}, u32[]{:S(2)}) %copy-start.6) | copy-done | bytes 155672
  60.2 1.2 %shard_map.239 = f32[2,32,32]{2,1,0:T(8,128)S(1)} custom-call(s32[1]{0:T(128)S(6)} %copy.39.flag, bf16[3,4096]{1,0:T(4,128)(2,1)S(1)} %reshape.51.st0, bf16[3,4096]{1,0:T(4,128)(2,1)S(1)} %reshape.52.st1, bf16[2,32,4096]{2,1,0:T(8,128)(2,1)S(1)} %bitcast.49, f32[4,4096]{1,0:T(4,128)S(1)} %copy-done.4, f32[1,4096]{1,0:T(1,128)S(1)} %bitcast.63, ...), custom_call_target="tpu_custom_call" | custom-call | flops 16777216 | bytes 2097152 | tf_op jit(solution)/shard_map/pallas_call | solution.py:479
  61.6 0.5 copy-done.29
  62.2 1.7 %shard_map.240 = (f32[4,2,1,256]{3,2,1,0:T(1,128)S(1)}, f32[4,2,1,256]{3,2,1,0:T(1,128)S(1)}, f32[4,2,128,256]{3,2,1,0:T(8,128)S(1)}) custom-call(s32[1]{0:T(128)} %bitcast.4.refs_0_.me, s32[8,4]{1,0:T(8,128)S(1)} %copy.28.refs_1_, s32[8,4]{1,0:T(8,128)S(1)} %copy.29.refs_2_, bf16[4,256,512]{2,1,0:T(8,128)(2,1)S(1)} %bitcast.54, ...), custom_call_target="tpu_custom_call" | custom-call | tf_op jit(solution)/shard_map/pallas_call | solution.py:494
  64.0 4.0 %shard_map.241 = (bf16[272,256]{1,0:T(8,128)(2,1)S(1)}, bf16[272,256]{1,0:T(8,128)(2,1)}, bf16[272,256]{1,0:T(8,128)(2,1)}, bf16[272,256]{1,0:T(8,128)(2,1)}) custom-call(s32[1]{0:T(128)} %bitcast.4.refs_0_.me, s32[8,4]{1,0:T(8,128)S(1)} %copy.28.refs_1_, s32[8,4]{1,0:T(8,128)S(1)} %copy.29.refs_2_, bf16[4,256,512]{2,1,0:T(8,128)(2,1)} %collective-permute-done.15.refs_3_, ...), custom_call_target="tpu_custom_call" | custom-call | flops 20000000000 | bytes 60000000 | tf_op jit(solution)/shard_map/pallas_call | solution.py:505
  68.0 3.9 %collective-permute-start.16 = (bf16[272,256]{1,0:T(8,128)(2,1)}, bf16[272,256]{1,0:T(8,128)(2,1)S(1)}, u32[]{:S(2)}, u32[]{:S(2)}) collective-permute-start(bf16[272,256]{1,0:T(8,128)(2,1)} %get-tuple-element.65), channel_id=1, source_target_pairs={{0,12},{2,14},{4,0},{6,2},{8,4},{10,6},{12,8},{14,10},{1,13},{3,15... | collective-permute-start | bytes 417800 | tf_op jit(solution)/shard_map/ppermute | solution.py:393
  71.9 0.6 collective-permute-start.18
  72.5 0.3 copy-done.8
  72.8 1.9 %shard_map.234 = (bf16[32,2048]{1,0:T(8,128)(2,1)S(1)}, f32[2,1,256]{2,1,0:T(1,128)S(1)}, f32[2,1,256]{2,1,0:T(1,128)S(1)}, f32[2,128,256]{2,1,0:T(8,128)S(1)}) custom-call(s32[1]{0:T(128)S(6)} %copy.39.flag, bf16[1040,128]{1,0:T(8,128)(2,1)S(1)} %concatenate.6.refs_4_.q, bf16[2,32,512]{2,1,0:T(8,128)(2,1)S(1)} %bitcast.64, bf16[272,256]{1,0:T(8,128)(2,1)S(1)} %copy-done.8, ...), custom_call_target="tpu_custom_call" | custom-call | tf_op jit(solution)/shard_map/pallas_call | solution.py:500
  74.8 0.9 copy-done.22
  75.7 1.2 %copy-done.16 = f32[2,32,32,128]{3,2,1,0:T(8,128)S(1)} copy-done((f32[2,32,32,128]{3,2,1,0:T(8,128)S(1)}, f32[2,32,32,128]{3,2,1,0:T(8,128)}, u32[]{:S(2)}) %copy-start.16) | copy-done | bytes 1048600
  76.9 1.2 %copy-done.18 = f32[2,32,32,128]{3,2,1,0:T(8,128)S(1)} copy-done((f32[2,32,32,128]{3,2,1,0:T(8,128)S(1)}, f32[2,32,32,128]{3,2,1,0:T(8,128)}, u32[]{:S(2)}) %copy-start.18) | copy-done | bytes 1048600
  78.1 6.6 %shard_map.243 = bf16[2,32,32,128]{3,2,1,0:T(8,128)(2,1)S(1)} custom-call(s32[1]{0:T(128)S(6)} %copy.39.flag, f32[64,32]{1,0:T(8,128)S(1)} %bitcast.65, bf16[19,32,128]{2,1,0:T(8,128)(2,1)S(1)} %reshape.54.st0, bf16[19,32,128]{2,1,0:T(8,128)(2,1)S(1)} %reshape.55.st1, f32[2,32,32,128]{3,2,1,0:T(8,128)S(1)} %copy-done.14, f32[2,32,32,128]{3,2,1,0:T(8,128)S(1)} %copy-done.16, ...), custom_call_target="tpu_custom_call" | custom-call | flops 25165824 | bytes 4194304 | tf_op jit(solution)/shard_map/pallas_call | solution.py:514
  84.7 1.0 %reshape.57 = bf16[1,2,32,4096]{3,2,1,0:T(8,128)(2,1)} reshape(bf16[2,32,32,128]{3,2,1,0:T(8,128)(2,1)S(1)} %shard_map.243) | data formatting | bytes 1048576 | tf_op jit(solution)/shard_map/reshape | solution.py:521
  85.7 0.9 %shard_map.242 = bf16[2,32,2048]{2,1,0:T(8,128)(2,1)} custom-call(bf16[32,2048]{1,0:T(8,128)(2,1)S(1)} %get-tuple-element.50.first, f32[2,1,256]{2,1,0:T(1,128)S(1)} %get-tuple-element.51.top, f32[2,1,256]{2,1,0:T(1,128)S(1)} %get-tuple-element.52.tot, f32[2,128,256]{2,1,0:T(8,128)S(1)} %get-tuple-element.53.acc, ...), custom_call_target="tpu_custom_call" | custom-call | tf_op jit(solution)/shard_map/pallas_call | solution.py:523
  (84 shorter events, 1.1 us)
Async XLA Ops:
  1.7 3.3 %copy-start.26 = (bf16[1,2,32,2048]{3,2,1,0:T(8,128)(2,1)S(1)}, bf16[1,2,32,2048]{3,2,1,0:T(8,128)(2,1)}, u32[]{:S(2)}) copy-start(bf16[1,2,32,2048]{3,2,1,0:T(8,128)(2,1)} %param.23) | copy-start | bytes 786436
  1.9 10.4 %collective-permute-start.4 = (bf16[608,256]{1,0:T(8,128)(2,1)S(1)}, bf16[608,256]{1,0:T(8,128)(2,1)S(1)}, u32[]{:S(2)}, u32[]{:S(2)}) collective-permute-start(bf16[608,256]{1,0:T(8,128)(2,1)S(1)} %reshape.50.kept.own), channel_id=1, source_target_pairs={{0,2},{2,0},{4,6},{6,4},{8,10},{10,8},{12,14},{14,12},{1,3},{3,1},... | collective-permute-start | bytes 933896 | tf_op jit(solution)/shard_map/ppermute | solution.py:390
  5.8 17.1 %collective-permute-start.1 = (bf16[1040,128]{1,0:T(8,128)(2,1)S(1)}, bf16[1040,128]{1,0:T(8,128)(2,1)S(1)}, u32[]{:S(2)}, u32[]{:S(2)}) collective-permute-start(bf16[1040,128]{1,0:T(8,128)(2,1)S(1)} %concatenate.6.refs_4_.q), channel_id=1, source_target_pairs={{0,4},{2,6},{4,8},{6,10},{8,12},{10,14},{12,0},{14,2},{1,5},{3,7},... | collective-permute-start | bytes 798728 | tf_op jit(solution)/shard_map/ppermute | solution.py:393
  7.4 19.7 %collective-permute-start.2 = (bf16[1040,128]{1,0:T(8,128)(2,1)S(1)}, bf16[1040,128]{1,0:T(8,128)(2,1)S(1)}, u32[]{:S(2)}, u32[]{:S(2)}) collective-permute-start(bf16[1040,128]{1,0:T(8,128)(2,1)S(1)} %concatenate.6.refs_4_.q), channel_id=1, source_target_pairs={{0,8},{2,10},{4,12},{6,14},{8,0},{10,2},{12,4},{14,6},{1,9},{3,11}... | collective-permute-start | bytes 798728 | tf_op jit(solution)/shard_map/ppermute | solution.py:393
  10.0 17.1 %collective-permute-start.3 = (bf16[1040,128]{1,0:T(8,128)(2,1)S(1)}, bf16[1040,128]{1,0:T(8,128)(2,1)S(1)}, u32[]{:S(2)}, u32[]{:S(2)}) collective-permute-start(bf16[1040,128]{1,0:T(8,128)(2,1)S(1)} %concatenate.6.refs_4_.q), channel_id=1, source_target_pairs={{0,12},{2,14},{4,0},{6,2},{8,4},{10,6},{12,8},{14,10},{1,13},{3,15... | collective-permute-start | bytes 798728 | tf_op jit(solution)/shard_map/ppermute | solution.py:393
  12.3 0.7 copy-start.19
  12.3 2.5 %copy-start.2 = (bf16[1,1024,512]{2,1,0:T(8,128)(2,1)S(1)}, bf16[1,1024,512]{2,1,0:T(8,128)(2,1)}, u32[]{:S(2)}) copy-start(bf16[1,1024,512]{2,1,0:T(8,128)(2,1)} %param.25) | copy-start | bytes 3145732
  12.3 4.0 %copy-start.4 = (f32[4,4096]{1,0:T(4,128)S(1)}, f32[4,4096]{1,0:T(4,128)}, u32[]{:S(2)}) copy-start(f32[4,4096]{1,0:T(4,128)} %w.1) | copy-start | bytes 196612
  12.3 4.0 %copy-start = (bf16[1,2,32,4096]{3,2,1,0:T(8,128)(2,1)S(1)}, bf16[1,2,32,4096]{3,2,1,0:T(8,128)(2,1)}, u32[]{:S(2)}) copy-start(bf16[1,2,32,4096]{3,2,1,0:T(8,128)(2,1)} %param.37) | copy-start | bytes 1572868
  13.1 17.2 %collective-permute-start.5 = (bf16[304,256]{1,0:T(8,128)(2,1)S(1)}, bf16[304,256]{1,0:T(8,128)(2,1)S(1)}, u32[]{:S(2)}, u32[]{:S(2)}) collective-permute-start(bf16[304,256]{1,0:T(8,128)(2,1)S(1)} %shard_map.232.kept), channel_id=1, source_target_pairs={{0,4},{2,6},{4,0},{6,2},{8,12},{10,14},{12,8},{14,10},{1,5},{3,7},... | collective-permute-start | bytes 466952 | tf_op jit(solution)/shard_map/ppermute | solution.py:440
  14.8 26.1 %collective-permute-start = (bf16[1024,512]{1,0:T(8,128)(2,1)S(1)}, bf16[1024,512]{1,0:T(8,128)(2,1)S(1)}, u32[]{:S(2)}, u32[]{:S(2)}) collective-permute-start(bf16[1024,512]{1,0:T(8,128)(2,1)S(1)} %bitcast.55), channel_id=1, source_target_pairs={{0,2},{2,0},{4,6},{6,4},{8,10},{10,8},{12,14},{14,12},{1,3},{3,1},... | collective-permute-start | bytes 3145736 | tf_op jit(solution)/shard_map/ppermute | solution.py:390
  16.4 1.0 %copy-start.24 = (bf16[1,2,32,4096]{3,2,1,0:T(8,128)(2,1)S(1)}, bf16[1,2,32,4096]{3,2,1,0:T(8,128)(2,1)}, u32[]{:S(2)}) copy-start(bf16[1,2,32,4096]{3,2,1,0:T(8,128)(2,1)} %param.39) | copy-start | bytes 1572868
  17.4 1.0 %copy-start.25 = (bf16[1,2,32,4096]{3,2,1,0:T(8,128)(2,1)S(1)}, bf16[1,2,32,4096]{3,2,1,0:T(8,128)(2,1)}, u32[]{:S(2)}) copy-start(bf16[1,2,32,4096]{3,2,1,0:T(8,128)(2,1)} %param.38) | copy-start | bytes 1572868
  18.5 0.9 %copy-start.27 = (f32[16,4096]{1,0:T(8,128)S(1)}, f32[16,4096]{1,0:T(8,128)}, u32[]{:S(2)}) copy-start(f32[16,4096]{1,0:T(8,128)} %param.41) | copy-start | bytes 786436
  19.4 0.7 copy-start.9
  19.4 0.7 copy-start.11
  19.5 3.4 %copy-start.1 = (bf16[1,4,256,512]{3,2,1,0:T(8,128)(2,1)S(1)}, bf16[1,4,256,512]{3,2,1,0:T(8,128)(2,1)}, u32[]{:S(2)}) copy-start(bf16[1,4,256,512]{3,2,1,0:T(8,128)(2,1)} %param.28) | copy-start | bytes 3145732
  20.2 10.1 %copy-start.20 = (bf16[608,256]{1,0:T(8,128)(2,1)S(1)}, bf16[608,256]{1,0:T(8,128)(2,1)}, u32[]{:S(2)}) copy-start(bf16[608,256]{1,0:T(8,128)(2,1)} %copy-done.19) | copy-start | bytes 933892
  22.8 8.7 %copy-start.13 = (f32[2,32,32,128]{3,2,1,0:T(8,128)}, f32[2,32,32,128]{3,2,1,0:T(8,128)S(1)}, u32[]{:S(2)}) copy-start(f32[2,32,32,128]{3,2,1,0:T(8,128)S(1)} %get-tuple-element.37.step) | copy-start | bytes 3145732
  22.8 8.7 %copy-start.15 = (f32[2,32,32,128]{3,2,1,0:T(8,128)}, f32[2,32,32,128]{3,2,1,0:T(8,128)S(1)}, u32[]{:S(2)}) copy-start(f32[2,32,32,128]{3,2,1,0:T(8,128)S(1)} %get-tuple-element.38.act) | copy-start | bytes 3145732
  22.8 8.7 %copy-start.17 = (f32[2,32,32,128]{3,2,1,0:T(8,128)}, f32[2,32,32,128]{3,2,1,0:T(8,128)S(1)}, u32[]{:S(2)}) copy-start(f32[2,32,32,128]{3,2,1,0:T(8,128)S(1)} %get-tuple-element.39.gate) | copy-start | bytes 3145732
  22.8 8.7 %copy-start.21 = (f32[16,32,128]{2,1,0:T(8,128)}, f32[16,32,128]{2,1,0:T(8,128)S(1)}, u32[]{:S(2)}) copy-start(f32[16,32,128]{2,1,0:T(8,128)S(1)} %get-tuple-element.40.dec) | copy-start | bytes 786436
  22.9 41.1 %collective-permute-start.15 = (bf16[4,256,512]{2,1,0:T(8,128)(2,1)S(1)}, bf16[4,256,512]{2,1,0:T(8,128)(2,1)}, u32[]{:S(2)}, u32[]{:S(2)}) collective-permute-start(bf16[4,256,512]{2,1,0:T(8,128)(2,1)S(1)} %bitcast.53), channel_id=1, source_target_pairs={{0,2},{2,0},{4,6},{6,4},{8,10},{10,8},{12,14},{14,12},{1,3},{3,1},... | collective-permute-start | bytes 3145736 | tf_op jit(solution)/shard_map/ppermute | solution.py:390
  31.6 12.8 %collective-permute-start.12 = (bf16[304,256]{1,0:T(8,128)(2,1)S(1)}, bf16[304,256]{1,0:T(8,128)(2,1)S(1)}, u32[]{:S(2)}, u32[]{:S(2)}) collective-permute-start(bf16[304,256]{1,0:T(8,128)(2,1)S(1)} %shard_map.235.kept), channel_id=1, source_target_pairs={{4,8},{6,10},{8,4},{10,6},{5,9},{7,11},{9,5},{11,7},{20,24},{22,26... | collective-permute-start | bytes 466952 | tf_op jit(solution)/shard_map/ppermute | solution.py:440
  32.3 15.2 %collective-permute-start.10 = (bf16[304,256]{1,0:T(8,128)(2,1)S(1)}, bf16[304,256]{1,0:T(8,128)(2,1)S(1)}, u32[]{:S(2)}, u32[]{:S(2)}) collective-permute-start(bf16[304,256]{1,0:T(8,128)(2,1)S(1)} %get-tuple-element.48), channel_id=1, source_target_pairs={{0,4},{2,6},{4,8},{6,10},{8,12},{10,14},{12,0},{14,2},{1,5},{3,7},... | collective-permute-start | bytes 466952 | tf_op jit(solution)/shard_map/ppermute | solution.py:393
  36.6 14.3 %collective-permute-start.8 = (bf16[304,256]{1,0:T(8,128)(2,1)S(1)}, bf16[304,256]{1,0:T(8,128)(2,1)S(1)}, u32[]{:S(2)}, u32[]{:S(2)}) collective-permute-start(bf16[304,256]{1,0:T(8,128)(2,1)S(1)} %get-tuple-element.45), channel_id=1, source_target_pairs={{0,8},{2,10},{4,12},{6,14},{8,0},{10,2},{12,4},{14,6},{1,9},{3,11}... | collective-permute-start | bytes 466952 | tf_op jit(solution)/shard_map/ppermute | solution.py:393
  40.9 11.9 %collective-permute-start.6 = (bf16[304,256]{1,0:T(8,128)(2,1)S(1)}, bf16[304,256]{1,0:T(8,128)(2,1)S(1)}, u32[]{:S(2)}, u32[]{:S(2)}) collective-permute-start(bf16[304,256]{1,0:T(8,128)(2,1)S(1)} %get-tuple-element.42), channel_id=1, source_target_pairs={{0,12},{2,14},{4,0},{6,2},{8,4},{10,6},{12,8},{14,10},{1,13},{3,15... | collective-permute-start | bytes 466952 | tf_op jit(solution)/shard_map/ppermute | solution.py:393
  44.4 0.7 copy-start.7
  45.1 13.4 %collective-permute-start.13 = (bf16[304,256]{1,0:T(8,128)(2,1)S(1)}, bf16[304,256]{1,0:T(8,128)(2,1)S(1)}, u32[]{:S(2)}, u32[]{:S(2)}) collective-permute-start(bf16[304,256]{1,0:T(8,128)(2,1)S(1)} %shard_map.236.kept), channel_id=1, source_target_pairs={{0,4},{2,6},{4,0},{6,2},{8,12},{10,14},{12,8},{14,10},{1,5},{3,7},... | collective-permute-start | bytes 466952 | tf_op jit(solution)/shard_map/ppermute | solution.py:440
  47.5 16.4 %collective-permute-start.11 = (bf16[272,256]{1,0:T(8,128)(2,1)}, bf16[272,256]{1,0:T(8,128)(2,1)}, u32[]{:S(2)}, u32[]{:S(2)}) collective-permute-start(bf16[272,256]{1,0:T(8,128)(2,1)} %get-tuple-element.49), channel_id=1, source_target_pairs={{0,4},{2,6},{4,8},{6,10},{8,12},{10,14},{12,0},{14,2},{1,5},{3,7},... | collective-permute-start | bytes 417800 | tf_op jit(solution)/shard_map/ppermute | solution.py:393
  50.9 13.0 %collective-permute-start.9 = (bf16[272,256]{1,0:T(8,128)(2,1)}, bf16[272,256]{1,0:T(8,128)(2,1)}, u32[]{:S(2)}, u32[]{:S(2)}) collective-permute-start(bf16[272,256]{1,0:T(8,128)(2,1)} %get-tuple-element.46), channel_id=1, source_target_pairs={{0,8},{2,10},{4,12},{6,14},{8,0},{10,2},{12,4},{14,6},{1,9},{3,11}... | collective-permute-start | bytes 417800 | tf_op jit(solution)/shard_map/ppermute | solution.py:393
  52.9 11.1 %collective-permute-start.7 = (bf16[272,256]{1,0:T(8,128)(2,1)}, bf16[272,256]{1,0:T(8,128)(2,1)}, u32[]{:S(2)}, u32[]{:S(2)}) collective-permute-start(bf16[272,256]{1,0:T(8,128)(2,1)} %get-tuple-element.43), channel_id=1, source_target_pairs={{0,12},{2,14},{4,0},{6,2},{8,4},{10,6},{12,8},{14,10},{1,13},{3,15... | collective-permute-start | bytes 417800 | tf_op jit(solution)/shard_map/ppermute | solution.py:393
  58.5 1.7 %copy-start.3 = (bf16[4096,32]{0,1:T(8,128)(2,1)S(1)}, bf16[4096,32]{0,1:T(8,128)(2,1)}, u32[]{:S(2)}) copy-start(bf16[4096,32]{0,1:T(8,128)(2,1)} %param.45) | copy-start | bytes 786436
  58.5 0.7 copy-start.5
  59.2 0.9 %copy-start.6 = (bf16[304,256]{1,0:T(8,128)(2,1)S(1)}, bf16[304,256]{1,0:T(8,128)(2,1)}, u32[]{:S(2)}) copy-start(bf16[304,256]{1,0:T(8,128)(2,1)} %copy-done.5) | copy-start | bytes 466948
  60.2 1.3 %copy-start.28 = (s32[8,4]{0,1:T(4,128)S(1)}, s32[8,4]{0,1:T(4,128)}, u32[]{:S(2)}) copy-start(s32[8,4]{0,1:T(4,128)} %param.33) | copy-start | bytes 388
  61.4 0.7 copy-start.29
  61.4 2.5 %collective-permute-start.14 = (f32[2,32,32]{2,1,0:T(8,128)S(1)}, f32[2,32,32]{2,1,0:T(8,128)S(1)}, u32[]{:S(2)}, u32[]{:S(2)}) collective-permute-start(f32[2,32,32]{2,1,0:T(8,128)S(1)} %shard_map.239), channel_id=1, source_target_pairs={{0,1},{1,0},{2,3},{3,2},{4,5},{5,4},{6,7},{7,6},{8,9},{9,8},{10,11... | collective-permute-start | bytes 24584 | tf_op jit(solution)/shard_map/ppermute | solution.py:486
  64.0 10.8 %copy-start.14 = (f32[2,32,32,128]{3,2,1,0:T(8,128)S(1)}, f32[2,32,32,128]{3,2,1,0:T(8,128)}, u32[]{:S(2)}) copy-start(f32[2,32,32,128]{3,2,1,0:T(8,128)} %copy-done.13) | copy-start | bytes 3145732
  68.0 17.7 %collective-permute-start.16 = (bf16[272,256]{1,0:T(8,128)(2,1)}, bf16[272,256]{1,0:T(8,128)(2,1)S(1)}, u32[]{:S(2)}, u32[]{:S(2)}) collective-permute-start(bf16[272,256]{1,0:T(8,128)(2,1)} %get-tuple-element.65), channel_id=1, source_target_pairs={{0,12},{2,14},{4,0},{6,2},{8,4},{10,6},{12,8},{14,10},{1,13},{3,15... | collective-permute-start | bytes 417800 | tf_op jit(solution)/shard_map/ppermute | solution.py:393
  71.9 13.8 %collective-permute-start.17 = (bf16[272,256]{1,0:T(8,128)(2,1)}, bf16[272,256]{1,0:T(8,128)(2,1)S(1)}, u32[]{:S(2)}, u32[]{:S(2)}) collective-permute-start(bf16[272,256]{1,0:T(8,128)(2,1)} %get-tuple-element.66), channel_id=1, source_target_pairs={{0,8},{2,10},{4,12},{6,14},{8,0},{10,2},{12,4},{14,6},{1,9},{3,11}... | collective-permute-start | bytes 417800 | tf_op jit(solution)/shard_map/ppermute | solution.py:393
  71.9 0.9 %copy-start.8 = (bf16[272,256]{1,0:T(8,128)(2,1)S(1)}, bf16[272,256]{1,0:T(8,128)(2,1)}, u32[]{:S(2)}) copy-start(bf16[272,256]{1,0:T(8,128)(2,1)} %copy-done.7) | copy-start | bytes 417796
  71.9 0.9 %copy-start.10 = (bf16[1,2,32,512]{3,2,1,0:T(8,128)(2,1)S(1)}, bf16[1,2,32,512]{3,2,1,0:T(8,128)(2,1)}, u32[]{:S(2)}) copy-start(bf16[1,2,32,512]{3,2,1,0:T(8,128)(2,1)} %param.24) | copy-start | bytes 196612
  71.9 13.8 %collective-permute-start.18 = (bf16[272,256]{1,0:T(8,128)(2,1)}, bf16[272,256]{1,0:T(8,128)(2,1)S(1)}, u32[]{:S(2)}, u32[]{:S(2)}) collective-permute-start(bf16[272,256]{1,0:T(8,128)(2,1)} %get-tuple-element.67), channel_id=1, source_target_pairs={{0,4},{2,6},{4,8},{6,10},{8,12},{10,14},{12,0},{14,2},{1,5},{3,7},... | collective-permute-start | bytes 417800 | tf_op jit(solution)/shard_map/ppermute | solution.py:393
  74.7 1.0 %copy-start.22 = (f32[16,32,128]{2,1,0:T(8,128)S(1)}, f32[16,32,128]{2,1,0:T(8,128)}, u32[]{:S(2)}) copy-start(f32[16,32,128]{2,1,0:T(8,128)} %copy-done.21) | copy-start | bytes 786436
  74.7 1.0 %copy-start.23 = (f32[4096]{0:T(1024)S(1)}, f32[4096]{0:T(1024)}, u32[]{:S(2)}) copy-start(f32[4096]{0:T(1024)} %param.42) | copy-start | bytes 49156
  75.7 1.2 %copy-start.16 = (f32[2,32,32,128]{3,2,1,0:T(8,128)S(1)}, f32[2,32,32,128]{3,2,1,0:T(8,128)}, u32[]{:S(2)}) copy-start(f32[2,32,32,128]{3,2,1,0:T(8,128)} %copy-done.15) | copy-start | bytes 3145732
  76.9 1.2 %copy-start.18 = (f32[2,32,32,128]{3,2,1,0:T(8,128)S(1)}, f32[2,32,32,128]{3,2,1,0:T(8,128)}, u32[]{:S(2)}) copy-start(f32[2,32,32,128]{3,2,1,0:T(8,128)} %copy-done.17) | copy-start | bytes 3145732
  (1 other events, 0.7 us)

commit v4 on v3

--- a/solution.py
+++ b/solution.py
@@ -333,7 +333,7 @@
                 return tuple(after)
 
             hs = tuple(held(n) for n in range(state))
-            peel = keep + (length - keep) % 2
+            peel = keep + (length - keep) % 4
             for t in range(peel):
                 sig = act[r, t, at, :]
                 if t < keep:
@@ -345,7 +345,7 @@
             def body(t, hs, r=r, at=at, advance=advance):
                 return advance(t, hs, act[r, t, at, :])
 
-            lax.fori_loop(peel, length, body, hs, unroll=2)
+            lax.fori_loop(peel, length, body, hs, unroll=4)
 
 
 def local(
@@ -465,7 +465,7 @@
         pl.CostEstimate(flops=10**6, bytes_accessed=10**4, transcendentals=0),
     )(me, owner_id, cached_lookup_pairs[0], prefix_nbr, *asked)
     for r in range(1, spans):
-        state0 = shared(r, after(state0, part0[0]) if r > 1 else state0, hops[-1])
+        state0 = shared(r, state0, hops[-1])
         if r < spans - 1:
             hops.append(hop(after(state0, sent[0]), r))
     got0 = [part0[0]] + [turn(after(part0[k], came[spans - k]), spans - k) for k in range(1, spans)]

time: 87.4 us -> 87.2 us (level)
  local copies, waits for them, and re-layouts: 13.1 us -> 11.2 us
  starting transfers between devices: 38.3 us -> 39.2 us
    ppermute x3, starting transfers between devices: 4.92 us -> 8.95 us  [hop(): return lax.ppermute(value, axis, links)]
    ppermute x12, starting transfers between devices: 28.2 us -> 25.1 us  [turn(): lax.ppermute(value, axis, [(s, (s + k * pair) % size) for s in range(size)])]
    ppermute x3, waiting for transfers between devices: 3.12 us -> 0.34 us  [across(): return lax.ppermute(value, axis, [(s, s ^ 1) for s in range(size)])]
    unnamed x68 -> x64, local copies, waits for them, and re-layouts: 11.7 us -> 9.78 us
    ppermute x12, waiting for transfers between devices: 3.71 us -> 5.28 us  [turn(): lax.ppermute(value, axis, [(s, (s + k * pair) % size) for s in range(size)])]
    ppermute x3, waiting for transfers between devices: 3.16 us -> 4.63 us  [hop(): return lax.ppermute(value, axis, links)]
    pallas_call x4, Pallas kernels: 0.11 us -> 1.02 us  [shared(): call(functools.partial(shared_body, spans, pair, unit, rounds), one, [SSP...]
  transfers between devices with their start and end apart: 19 -> 19, of which waited for: 4 -> 8; matrix products, arithmetic and copies ran while one was open for 2% -> 2% of each run, Pallas kernels for 19% -> 18%
where the time goes in v4:
time: 87.2 us; the launch traced here: 86.8 us
  starting transfers between devices  39.2 us (45%)
  Pallas kernels  21.5 us (25%)
  local copies, waits for them, and re-layouts  11.2 us (13%)
  waiting for transfers between devices  10.8 us (12%)
  between operations  2.99 us (3%)
  other arithmetic  1.09 us (1%)
    ppermute x12, starting transfers between devices, turn(): lax.ppermute(value, axis, [(s, (s + k * pair) % size) for s in range(size)])  25.1 us
    unnamed x64, local copies, waits for them, and re-layouts  9.78 us
    ppermute x3, starting transfers between devices, hop(): return lax.ppermute(value, axis, links)  8.95 us
    pallas_call x1, Pallas kernels, local(): call(functools.partial(scan_body, state), jax.ShapeDtypeStruct((2, length...  6.15 us
    ppermute x12, waiting for transfers between devices, turn(): lax.ppermute(value, axis, [(s, (s + k * pair) % size) for s in range(size)])  5.28 us
    ppermute x3, starting transfers between devices, across(): return lax.ppermute(value, axis, [(s, s ^ 1) for s in range(size)])  5.12 us
    ppermute x3, waiting for transfers between devices, hop(): return lax.ppermute(value, axis, links)  4.63 us
    pallas_call x1, Pallas kernels, local(): call(functools.partial(blocks_body, True, heads, spans, slots, pair), [pa...  4.62 us
  transfers between devices with their start and end apart: 19, of which 8 were waited for; matrix products, arithmetic and copies ran while one was open for 2% of the time, Pallas kernels for 18%

profile of v4, /device:TPU:0, one launch (start us, length us, event | category | flops | bytes accessed | tf_op | source)
XLA Modules:
  0.0 86.8 jit_solution(13260222515086784686)
XLA Ops:
  0.6 1.1 %pad_maximum_fusion = bf16[38,4096]{1,0:T(8,128)(2,1)S(1)} fusion(bf16[3,4096]{1,0:T(4,128)(2,1)} %bitcast.77, bf16[16,4096]{1,0:T(8,128)(2,1)} %bitcast.75, bf16[3,4096]{1,0:T(4,128)(2,1)} %bitcast.78, bf16[16,4096]{1,0:T(8,128)(2,1)} %bitcast.76), kind=kLoop, calls=%fused_computation | loop fusion | flops 1245184 | bytes 622592 | tf_op jit(solution)/shard_map/concatenate | solution.py:406
  1.9 3.0 %collective-permute-start.4 = (bf16[608,256]{1,0:T(8,128)(2,1)S(1)}, bf16[608,256]{1,0:T(8,128)(2,1)S(1)}, u32[]{:S(2)}, u32[]{:S(2)}) collective-permute-start(bf16[608,256]{1,0:T(8,128)(2,1)S(1)} %reshape.50.kept.own), channel_id=1, source_target_pairs={{0,2},{2,0},{4,6},{6,4},{8,10},{10,8},{12,14},{14,12},{1,3},{3,1},... | collective-permute-start | bytes 933896 | tf_op jit(solution)/shard_map/ppermute | solution.py:390
  5.8 1.6 %collective-permute-start.1 = (bf16[1040,128]{1,0:T(8,128)(2,1)S(1)}, bf16[1040,128]{1,0:T(8,128)(2,1)S(1)}, u32[]{:S(2)}, u32[]{:S(2)}) collective-permute-start(bf16[1040,128]{1,0:T(8,128)(2,1)S(1)} %concatenate.6.refs_4_.q), channel_id=1, source_target_pairs={{0,4},{2,6},{4,8},{6,10},{8,12},{10,14},{12,0},{14,2},{1,5},{3,7},... | collective-permute-start | bytes 798728 | tf_op jit(solution)/shard_map/ppermute | solution.py:393
  7.4 2.6 %collective-permute-start.2 = (bf16[1040,128]{1,0:T(8,128)(2,1)S(1)}, bf16[1040,128]{1,0:T(8,128)(2,1)S(1)}, u32[]{:S(2)}, u32[]{:S(2)}) collective-permute-start(bf16[1040,128]{1,0:T(8,128)(2,1)S(1)} %concatenate.6.refs_4_.q), channel_id=1, source_target_pairs={{0,8},{2,10},{4,12},{6,14},{8,0},{10,2},{12,4},{14,6},{1,9},{3,11}... | collective-permute-start | bytes 798728 | tf_op jit(solution)/shard_map/ppermute | solution.py:393
  10.0 1.3 %collective-permute-start.3 = (bf16[1040,128]{1,0:T(8,128)(2,1)S(1)}, bf16[1040,128]{1,0:T(8,128)(2,1)S(1)}, u32[]{:S(2)}, u32[]{:S(2)}) collective-permute-start(bf16[1040,128]{1,0:T(8,128)(2,1)S(1)} %concatenate.6.refs_4_.q), channel_id=1, source_target_pairs={{0,12},{2,14},{4,0},{6,2},{8,4},{10,6},{12,8},{14,10},{1,13},{3,15... | collective-permute-start | bytes 798728 | tf_op jit(solution)/shard_map/ppermute | solution.py:393
  12.0 0.3 collective-permute-done.4.came.nbr
  12.4 0.7 copy-done.17
  13.1 1.8 %collective-permute-start.5 = (bf16[304,256]{1,0:T(8,128)(2,1)S(1)}, bf16[304,256]{1,0:T(8,128)(2,1)S(1)}, u32[]{:S(2)}, u32[]{:S(2)}) collective-permute-start(bf16[304,256]{1,0:T(8,128)(2,1)S(1)} %shard_map.232.kept), channel_id=1, source_target_pairs={{0,4},{2,6},{4,0},{6,2},{8,12},{10,14},{12,8},{14,10},{1,5},{3,7},... | collective-permute-start | bytes 466952 | tf_op jit(solution)/shard_map/ppermute | solution.py:440
  14.8 1.5 %collective-permute-start = (bf16[1024,512]{1,0:T(8,128)(2,1)S(1)}, bf16[1024,512]{1,0:T(8,128)(2,1)S(1)}, u32[]{:S(2)}, u32[]{:S(2)}) collective-permute-start(bf16[1024,512]{1,0:T(8,128)(2,1)S(1)} %bitcast.55), channel_id=1, source_target_pairs={{0,2},{2,0},{4,6},{6,4},{8,10},{10,8},{12,14},{14,12},{1,3},{3,1},... | collective-permute-start | bytes 3145736 | tf_op jit(solution)/shard_map/ppermute | solution.py:390
  16.5 0.9 %copy-done.22 = bf16[1,2,32,4096]{3,2,1,0:T(8,128)(2,1)S(1)} copy-done((bf16[1,2,32,4096]{3,2,1,0:T(8,128)(2,1)S(1)}, bf16[1,2,32,4096]{3,2,1,0:T(8,128)(2,1)}, u32[]{:S(2)}) %copy-start.22) | copy-done | bytes 524312
  17.5 0.9 %copy-done.23 = bf16[1,2,32,4096]{3,2,1,0:T(8,128)(2,1)S(1)} copy-done((bf16[1,2,32,4096]{3,2,1,0:T(8,128)(2,1)S(1)}, bf16[1,2,32,4096]{3,2,1,0:T(8,128)(2,1)}, u32[]{:S(2)}) %copy-start.23) | copy-done | bytes 524312
  18.6 0.8 copy-done.25
  19.5 0.6 copy-done.7
  20.2 2.6 %shard_map.231 = (f32[2,32,32,128]{3,2,1,0:T(8,128)S(1)}, f32[2,32,32,128]{3,2,1,0:T(8,128)S(1)}, f32[2,32,32,128]{3,2,1,0:T(8,128)S(1)}, f32[16,32,128]{2,1,0:T(8,128)S(1)}) custom-call(bf16[2,32,32,128]{3,2,1,0:T(8,128)(2,1)S(1)} %bitcast.50, bf16[2,32,32,128]{3,2,1,0:T(8,128)(2,1)S(1)} %bitcast.51, bf16[2,32,32,128]{3,2,1,0:T(8,128)(2,1)S(1)} %bitcast.52, ...), custom_call_target="tpu_custom_call" | custom-call | tf_op jit(solution)/shard_map/pallas_call | solution.py:418
  22.9 0.6 collective-permute-start.15
  23.5 3.7 %collective-permute-done.2.refs_6_ = bf16[1040,128]{1,0:T(8,128)(2,1)S(1)} collective-permute-done((bf16[1040,128]{1,0:T(8,128)(2,1)S(1)}, bf16[1040,128]{1,0:T(8,128)(2,1)S(1)}, u32[]{:S(2)}, u32[]{:S(2)}) %collective-permute-start.2) | collective-permute-done | bytes 266272 | tf_op jit(solution)/shard_map/ppermute | solution.py:393
  27.1 3.2 %collective-permute-done.5.came = bf16[304,256]{1,0:T(8,128)(2,1)S(1)} collective-permute-done((bf16[304,256]{1,0:T(8,128)(2,1)S(1)}, bf16[304,256]{1,0:T(8,128)(2,1)S(1)}, u32[]{:S(2)}, u32[]{:S(2)}) %collective-permute-start.5) | collective-permute-done | bytes 155680 | tf_op jit(solution)/shard_map/ppermute | solution.py:440
  30.3 0.7 copy-done.10
  30.9 0.6 shard_map.233
  31.6 0.7 collective-permute-start.12
  32.3 4.3 %collective-permute-start.10 = (bf16[304,256]{1,0:T(8,128)(2,1)S(1)}, bf16[304,256]{1,0:T(8,128)(2,1)S(1)}, u32[]{:S(2)}, u32[]{:S(2)}) collective-permute-start(bf16[304,256]{1,0:T(8,128)(2,1)S(1)} %get-tuple-element.46), channel_id=1, source_target_pairs={{0,4},{2,6},{4,8},{6,10},{8,12},{10,14},{12,0},{14,2},{1,5},{3,7},... | collective-permute-start | bytes 466952 | tf_op jit(solution)/shard_map/ppermute | solution.py:393
  36.6 1.5 %collective-permute-start.8 = (bf16[304,256]{1,0:T(8,128)(2,1)S(1)}, bf16[304,256]{1,0:T(8,128)(2,1)S(1)}, u32[]{:S(2)}, u32[]{:S(2)}) collective-permute-start(bf16[304,256]{1,0:T(8,128)(2,1)S(1)} %get-tuple-element.43), channel_id=1, source_target_pairs={{0,8},{2,10},{4,12},{6,14},{8,0},{10,2},{12,4},{14,6},{1,9},{3,11}... | collective-permute-start | bytes 466952 | tf_op jit(solution)/shard_map/ppermute | solution.py:393
  38.2 2.8 %collective-permute-start.6 = (bf16[304,256]{1,0:T(8,128)(2,1)S(1)}, bf16[304,256]{1,0:T(8,128)(2,1)S(1)}, u32[]{:S(2)}, u32[]{:S(2)}) collective-permute-start(bf16[304,256]{1,0:T(8,128)(2,1)S(1)} %get-tuple-element.40), channel_id=1, source_target_pairs={{0,12},{2,14},{4,0},{6,2},{8,4},{10,6},{12,8},{14,10},{1,13},{3,15... | collective-permute-start | bytes 466952 | tf_op jit(solution)/shard_map/ppermute | solution.py:393
  41.1 6.5 %collective-permute-start.13 = (bf16[304,256]{1,0:T(8,128)(2,1)S(1)}, bf16[304,256]{1,0:T(8,128)(2,1)}, u32[]{:S(2)}, u32[]{:S(2)}) collective-permute-start(bf16[304,256]{1,0:T(8,128)(2,1)S(1)} %shard_map.236.kept), channel_id=1, source_target_pairs={{0,4},{2,6},{4,0},{6,2},{8,12},{10,14},{12,8},{14,10},{1,5},{3,7},... | collective-permute-start | bytes 466952 | tf_op jit(solution)/shard_map/ppermute | solution.py:440
  47.5 0.8 shard_map.230
  48.3 0.7 copy-done.5
  49.0 1.9 %collective-permute-start.11 = (bf16[272,256]{1,0:T(8,128)(2,1)}, bf16[272,256]{1,0:T(8,128)(2,1)}, u32[]{:S(2)}, u32[]{:S(2)}) collective-permute-start(bf16[272,256]{1,0:T(8,128)(2,1)} %get-tuple-element.47), channel_id=1, source_target_pairs={{0,4},{2,6},{4,8},{6,10},{8,12},{10,14},{12,0},{14,2},{1,5},{3,7},... | collective-permute-start | bytes 417800 | tf_op jit(solution)/shard_map/ppermute | solution.py:393
  50.9 4.8 %collective-permute-start.9 = (bf16[272,256]{1,0:T(8,128)(2,1)}, bf16[272,256]{1,0:T(8,128)(2,1)}, u32[]{:S(2)}, u32[]{:S(2)}) collective-permute-start(bf16[272,256]{1,0:T(8,128)(2,1)} %get-tuple-element.44), channel_id=1, source_target_pairs={{0,8},{2,10},{4,12},{6,14},{8,0},{10,2},{12,4},{14,6},{1,9},{3,11}... | collective-permute-start | bytes 417800 | tf_op jit(solution)/shard_map/ppermute | solution.py:393
  55.7 1.4 %collective-permute-start.7 = (bf16[272,256]{1,0:T(8,128)(2,1)}, bf16[272,256]{1,0:T(8,128)(2,1)}, u32[]{:S(2)}, u32[]{:S(2)}) collective-permute-start(bf16[272,256]{1,0:T(8,128)(2,1)} %get-tuple-element.41), channel_id=1, source_target_pairs={{0,12},{2,14},{4,0},{6,2},{8,4},{10,6},{12,8},{14,10},{1,13},{3,15... | collective-permute-start | bytes 417800 | tf_op jit(solution)/shard_map/ppermute | solution.py:393
  57.8 0.6 shard_map.238
  58.4 1.5 %collective-permute-done.13.came = bf16[304,256]{1,0:T(8,128)(2,1)} collective-permute-done((bf16[304,256]{1,0:T(8,128)(2,1)S(1)}, bf16[304,256]{1,0:T(8,128)(2,1)}, u32[]{:S(2)}, u32[]{:S(2)}) %collective-permute-start.13) | collective-permute-done | bytes 155680 | tf_op jit(solution)/shard_map/ppermute | solution.py:440
  59.9 0.9 %shard_map.237 = bf16[304,256]{1,0:T(8,128)(2,1)S(1)} custom-call(s32[1]{0:T(128)} %bitcast.4.refs_0_.me, s32[1]{0:T(128)S(6)} %copy.38.refs_1_.owner, bf16[304,256]{1,0:T(8,128)(2,1)S(1)} %shard_map.236.kept, bf16[304,256]{1,0:T(8,128)(2,1)} %collective-permute-done.13.came), custom_call_target="tpu_custom_call" | custom-call | tf_op jit(solution)/shard_map/pallas_call | solution.py:428
  60.9 1.2 %shard_map.239 = f32[2,32,32]{2,1,0:T(8,128)S(1)} custom-call(s32[1]{0:T(128)S(6)} %copy.39.flag, bf16[3,4096]{1,0:T(4,128)(2,1)S(1)} %reshape.51.st0, bf16[3,4096]{1,0:T(4,128)(2,1)S(1)} %reshape.52.st1, bf16[2,32,4096]{2,1,0:T(8,128)(2,1)S(1)} %bitcast.49, f32[4,4096]{1,0:T(4,128)S(1)} %copy-done.4, f32[1,4096]{1,0:T(1,128)S(1)} %bitcast.63, ...), custom_call_target="tpu_custom_call" | custom-call | flops 16777216 | bytes 2097152 | tf_op jit(solution)/shard_map/pallas_call | solution.py:479
  62.3 0.5 copy-done.27
  62.9 0.5 collective-permute-done.14
  63.4 1.0 %shard_map.240 = (f32[4,2,1,256]{3,2,1,0:T(1,128)S(1)}, f32[4,2,1,256]{3,2,1,0:T(1,128)S(1)}, f32[4,2,128,256]{3,2,1,0:T(8,128)S(1)}) custom-call(s32[1]{0:T(128)} %bitcast.4.refs_0_.me, s32[8,4]{1,0:T(8,128)S(1)} %copy.28.refs_1_, s32[8,4]{1,0:T(8,128)S(1)} %copy.29.refs_2_, bf16[4,256,512]{2,1,0:T(8,128)(2,1)S(1)} %bitcast.54, ...), custom_call_target="tpu_custom_call" | custom-call | tf_op jit(solution)/shard_map/pallas_call | solution.py:494
  64.5 0.4 collective-permute-done.9.refs_2_
  64.9 0.9 %collective-permute-done.7.refs_1_ = bf16[272,256]{1,0:T(8,128)(2,1)} collective-permute-done((bf16[272,256]{1,0:T(8,128)(2,1)}, bf16[272,256]{1,0:T(8,128)(2,1)}, u32[]{:S(2)}, u32[]{:S(2)}) %collective-permute-start.7) | collective-permute-done | bytes 139296 | tf_op jit(solution)/shard_map/ppermute | solution.py:393
  65.8 4.6 %shard_map.241 = (bf16[272,256]{1,0:T(8,128)(2,1)S(1)}, bf16[272,256]{1,0:T(8,128)(2,1)}, bf16[272,256]{1,0:T(8,128)(2,1)}, bf16[272,256]{1,0:T(8,128)(2,1)}) custom-call(s32[1]{0:T(128)} %bitcast.4.refs_0_.me, s32[8,4]{1,0:T(8,128)S(1)} %copy.28.refs_1_, s32[8,4]{1,0:T(8,128)S(1)} %copy.29.refs_2_, bf16[4,256,512]{2,1,0:T(8,128)(2,1)} %collective-permute-done.15.refs_3_, ...), custom_call_target="tpu_custom_call" | custom-call | flops 20000000000 | bytes 60000000 | tf_op jit(solution)/shard_map/pallas_call | solution.py:505
  70.5 1.4 %collective-permute-start.16 = (bf16[272,256]{1,0:T(8,128)(2,1)}, bf16[272,256]{1,0:T(8,128)(2,1)S(1)}, u32[]{:S(2)}, u32[]{:S(2)}) collective-permute-start(bf16[272,256]{1,0:T(8,128)(2,1)} %get-tuple-element.61), channel_id=1, source_target_pairs={{0,12},{2,14},{4,0},{6,2},{8,4},{10,6},{12,8},{14,10},{1,13},{3,15... | collective-permute-start | bytes 417800 | tf_op jit(solution)/shard_map/ppermute | solution.py:393
  71.9 1.3 %collective-permute-start.17 = (bf16[272,256]{1,0:T(8,128)(2,1)}, bf16[272,256]{1,0:T(8,128)(2,1)S(1)}, u32[]{:S(2)}, u32[]{:S(2)}) collective-permute-start(bf16[272,256]{1,0:T(8,128)(2,1)} %get-tuple-element.62), channel_id=1, source_target_pairs={{0,8},{2,10},{4,12},{6,14},{8,0},{10,2},{12,4},{14,6},{1,9},{3,11}... | collective-permute-start | bytes 417800 | tf_op jit(solution)/shard_map/ppermute | solution.py:393
  73.3 0.8 copy-done.20
  74.1 1.2 %copy-done.14 = f32[2,32,32,128]{3,2,1,0:T(8,128)S(1)} copy-done((f32[2,32,32,128]{3,2,1,0:T(8,128)S(1)}, f32[2,32,32,128]{3,2,1,0:T(8,128)}, u32[]{:S(2)}) %copy-start.14) | copy-done | bytes 1048600
  75.3 1.2 %copy-done.16 = f32[2,32,32,128]{3,2,1,0:T(8,128)S(1)} copy-done((f32[2,32,32,128]{3,2,1,0:T(8,128)S(1)}, f32[2,32,32,128]{3,2,1,0:T(8,128)}, u32[]{:S(2)}) %copy-start.16) | copy-done | bytes 1048600
  76.5 6.2 %shard_map.243 = bf16[2,32,32,128]{3,2,1,0:T(8,128)(2,1)S(1)} custom-call(s32[1]{0:T(128)S(6)} %copy.39.flag, f32[64,32]{1,0:T(8,128)S(1)} %bitcast.65, bf16[19,32,128]{2,1,0:T(8,128)(2,1)S(1)} %reshape.54.st0, bf16[19,32,128]{2,1,0:T(8,128)(2,1)S(1)} %reshape.55.st1, f32[2,32,32,128]{3,2,1,0:T(8,128)S(1)} %copy-done.12, f32[2,32,32,128]{3,2,1,0:T(8,128)S(1)} %copy-done.14, ...), custom_call_target="tpu_custom_call" | custom-call | flops 25165824 | bytes 4194304 | tf_op jit(solution)/shard_map/pallas_call | solution.py:514
  82.7 1.0 %reshape.57 = bf16[1,2,32,4096]{3,2,1,0:T(8,128)(2,1)} reshape(bf16[2,32,32,128]{3,2,1,0:T(8,128)(2,1)S(1)} %shard_map.243) | data formatting | bytes 1048576 | tf_op jit(solution)/shard_map/reshape | solution.py:521
  83.7 1.9 %shard_map.234 = (bf16[32,2048]{1,0:T(8,128)(2,1)S(1)}, f32[2,1,256]{2,1,0:T(1,128)S(1)}, f32[2,1,256]{2,1,0:T(1,128)S(1)}, f32[2,128,256]{2,1,0:T(8,128)S(1)}) custom-call(s32[1]{0:T(128)S(6)} %copy.39.flag, bf16[1040,128]{1,0:T(8,128)(2,1)S(1)} %concatenate.6.refs_4_.q, bf16[2,32,512]{2,1,0:T(8,128)(2,1)S(1)} %bitcast.64, bf16[272,256]{1,0:T(8,128)(2,1)S(1)} %copy-done.6, ...), custom_call_target="tpu_custom_call" | custom-call | tf_op jit(solution)/shard_map/pallas_call | solution.py:500
  85.9 0.9 %shard_map.242 = bf16[2,32,2048]{2,1,0:T(8,128)(2,1)} custom-call(bf16[32,2048]{1,0:T(8,128)(2,1)S(1)} %get-tuple-element.48.first, f32[2,1,256]{2,1,0:T(1,128)S(1)} %get-tuple-element.49.top, f32[2,1,256]{2,1,0:T(1,128)S(1)} %get-tuple-element.50.tot, f32[2,128,256]{2,1,0:T(8,128)S(1)} %get-tuple-element.51.acc, ...), custom_call_target="tpu_custom_call" | custom-call | tf_op jit(solution)/shard_map/pallas_call | solution.py:523
  (80 shorter events, 1.5 us)
Async XLA Ops:
  1.7 3.3 %copy-start.24 = (bf16[1,2,32,2048]{3,2,1,0:T(8,128)(2,1)S(1)}, bf16[1,2,32,2048]{3,2,1,0:T(8,128)(2,1)}, u32[]{:S(2)}) copy-start(bf16[1,2,32,2048]{3,2,1,0:T(8,128)(2,1)} %param.23) | copy-start | bytes 786436
  1.9 10.4 %collective-permute-start.4 = (bf16[608,256]{1,0:T(8,128)(2,1)S(1)}, bf16[608,256]{1,0:T(8,128)(2,1)S(1)}, u32[]{:S(2)}, u32[]{:S(2)}) collective-permute-start(bf16[608,256]{1,0:T(8,128)(2,1)S(1)} %reshape.50.kept.own), channel_id=1, source_target_pairs={{0,2},{2,0},{4,6},{6,4},{8,10},{10,8},{12,14},{14,12},{1,3},{3,1},... | collective-permute-start | bytes 933896 | tf_op jit(solution)/shard_map/ppermute | solution.py:390
  5.8 17.1 %collective-permute-start.1 = (bf16[1040,128]{1,0:T(8,128)(2,1)S(1)}, bf16[1040,128]{1,0:T(8,128)(2,1)S(1)}, u32[]{:S(2)}, u32[]{:S(2)}) collective-permute-start(bf16[1040,128]{1,0:T(8,128)(2,1)S(1)} %concatenate.6.refs_4_.q), channel_id=1, source_target_pairs={{0,4},{2,6},{4,8},{6,10},{8,12},{10,14},{12,0},{14,2},{1,5},{3,7},... | collective-permute-start | bytes 798728 | tf_op jit(solution)/shard_map/ppermute | solution.py:393
  7.4 19.7 %collective-permute-start.2 = (bf16[1040,128]{1,0:T(8,128)(2,1)S(1)}, bf16[1040,128]{1,0:T(8,128)(2,1)S(1)}, u32[]{:S(2)}, u32[]{:S(2)}) collective-permute-start(bf16[1040,128]{1,0:T(8,128)(2,1)S(1)} %concatenate.6.refs_4_.q), channel_id=1, source_target_pairs={{0,8},{2,10},{4,12},{6,14},{8,0},{10,2},{12,4},{14,6},{1,9},{3,11}... | collective-permute-start | bytes 798728 | tf_op jit(solution)/shard_map/ppermute | solution.py:393
  10.0 17.1 %collective-permute-start.3 = (bf16[1040,128]{1,0:T(8,128)(2,1)S(1)}, bf16[1040,128]{1,0:T(8,128)(2,1)S(1)}, u32[]{:S(2)}, u32[]{:S(2)}) collective-permute-start(bf16[1040,128]{1,0:T(8,128)(2,1)S(1)} %concatenate.6.refs_4_.q), channel_id=1, source_target_pairs={{0,12},{2,14},{4,0},{6,2},{8,4},{10,6},{12,8},{14,10},{1,13},{3,15... | collective-permute-start | bytes 798728 | tf_op jit(solution)/shard_map/ppermute | solution.py:393
  12.3 0.7 copy-start.17
  12.3 2.5 %copy-start.2 = (bf16[1,1024,512]{2,1,0:T(8,128)(2,1)S(1)}, bf16[1,1024,512]{2,1,0:T(8,128)(2,1)}, u32[]{:S(2)}) copy-start(bf16[1,1024,512]{2,1,0:T(8,128)(2,1)} %param.25) | copy-start | bytes 3145732
  12.3 4.0 %copy-start.4 = (f32[4,4096]{1,0:T(4,128)S(1)}, f32[4,4096]{1,0:T(4,128)}, u32[]{:S(2)}) copy-start(f32[4,4096]{1,0:T(4,128)} %w.1) | copy-start | bytes 196612
  12.3 4.0 %copy-start = (bf16[1,2,32,4096]{3,2,1,0:T(8,128)(2,1)S(1)}, bf16[1,2,32,4096]{3,2,1,0:T(8,128)(2,1)}, u32[]{:S(2)}) copy-start(bf16[1,2,32,4096]{3,2,1,0:T(8,128)(2,1)} %param.37) | copy-start | bytes 1572868
  13.1 17.2 %collective-permute-start.5 = (bf16[304,256]{1,0:T(8,128)(2,1)S(1)}, bf16[304,256]{1,0:T(8,128)(2,1)S(1)}, u32[]{:S(2)}, u32[]{:S(2)}) collective-permute-start(bf16[304,256]{1,0:T(8,128)(2,1)S(1)} %shard_map.232.kept), channel_id=1, source_target_pairs={{0,4},{2,6},{4,0},{6,2},{8,12},{10,14},{12,8},{14,10},{1,5},{3,7},... | collective-permute-start | bytes 466952 | tf_op jit(solution)/shard_map/ppermute | solution.py:440
  14.8 26.2 %collective-permute-start = (bf16[1024,512]{1,0:T(8,128)(2,1)S(1)}, bf16[1024,512]{1,0:T(8,128)(2,1)S(1)}, u32[]{:S(2)}, u32[]{:S(2)}) collective-permute-start(bf16[1024,512]{1,0:T(8,128)(2,1)S(1)} %bitcast.55), channel_id=1, source_target_pairs={{0,2},{2,0},{4,6},{6,4},{8,10},{10,8},{12,14},{14,12},{1,3},{3,1},... | collective-permute-start | bytes 3145736 | tf_op jit(solution)/shard_map/ppermute | solution.py:390
  16.4 1.0 %copy-start.22 = (bf16[1,2,32,4096]{3,2,1,0:T(8,128)(2,1)S(1)}, bf16[1,2,32,4096]{3,2,1,0:T(8,128)(2,1)}, u32[]{:S(2)}) copy-start(bf16[1,2,32,4096]{3,2,1,0:T(8,128)(2,1)} %param.39) | copy-start | bytes 1572868
  17.4 1.0 %copy-start.23 = (bf16[1,2,32,4096]{3,2,1,0:T(8,128)(2,1)S(1)}, bf16[1,2,32,4096]{3,2,1,0:T(8,128)(2,1)}, u32[]{:S(2)}) copy-start(bf16[1,2,32,4096]{3,2,1,0:T(8,128)(2,1)} %param.38) | copy-start | bytes 1572868
  18.5 0.9 %copy-start.25 = (f32[16,4096]{1,0:T(8,128)S(1)}, f32[16,4096]{1,0:T(8,128)}, u32[]{:S(2)}) copy-start(f32[16,4096]{1,0:T(8,128)} %param.41) | copy-start | bytes 786436
  19.4 0.7 copy-start.7
  19.4 0.7 copy-start.9
  19.5 3.4 %copy-start.1 = (bf16[1,4,256,512]{3,2,1,0:T(8,128)(2,1)S(1)}, bf16[1,4,256,512]{3,2,1,0:T(8,128)(2,1)}, u32[]{:S(2)}) copy-start(bf16[1,4,256,512]{3,2,1,0:T(8,128)(2,1)} %param.28) | copy-start | bytes 3145732
  20.2 10.1 %copy-start.18 = (bf16[608,256]{1,0:T(8,128)(2,1)S(1)}, bf16[608,256]{1,0:T(8,128)(2,1)}, u32[]{:S(2)}) copy-start(bf16[608,256]{1,0:T(8,128)(2,1)} %copy-done.17) | copy-start | bytes 933892
  22.8 8.7 %copy-start.11 = (f32[2,32,32,128]{3,2,1,0:T(8,128)}, f32[2,32,32,128]{3,2,1,0:T(8,128)S(1)}, u32[]{:S(2)}) copy-start(f32[2,32,32,128]{3,2,1,0:T(8,128)S(1)} %get-tuple-element.35.step) | copy-start | bytes 3145732
  22.8 8.7 %copy-start.13 = (f32[2,32,32,128]{3,2,1,0:T(8,128)}, f32[2,32,32,128]{3,2,1,0:T(8,128)S(1)}, u32[]{:S(2)}) copy-start(f32[2,32,32,128]{3,2,1,0:T(8,128)S(1)} %get-tuple-element.36.act) | copy-start | bytes 3145732
  22.8 8.7 %copy-start.15 = (f32[2,32,32,128]{3,2,1,0:T(8,128)}, f32[2,32,32,128]{3,2,1,0:T(8,128)S(1)}, u32[]{:S(2)}) copy-start(f32[2,32,32,128]{3,2,1,0:T(8,128)S(1)} %get-tuple-element.37.gate) | copy-start | bytes 3145732
  22.8 8.7 %copy-start.19 = (f32[16,32,128]{2,1,0:T(8,128)}, f32[16,32,128]{2,1,0:T(8,128)S(1)}, u32[]{:S(2)}) copy-start(f32[16,32,128]{2,1,0:T(8,128)S(1)} %get-tuple-element.38.dec) | copy-start | bytes 786436
  22.9 43.0 %collective-permute-start.15 = (bf16[4,256,512]{2,1,0:T(8,128)(2,1)S(1)}, bf16[4,256,512]{2,1,0:T(8,128)(2,1)}, u32[]{:S(2)}, u32[]{:S(2)}) collective-permute-start(bf16[4,256,512]{2,1,0:T(8,128)(2,1)S(1)} %bitcast.53), channel_id=1, source_target_pairs={{0,2},{2,0},{4,6},{6,4},{8,10},{10,8},{12,14},{14,12},{1,3},{3,1},... | collective-permute-start | bytes 3145736 | tf_op jit(solution)/shard_map/ppermute | solution.py:390
  30.3 0.7 copy-start.10
  31.6 6.5 %collective-permute-start.12 = (bf16[304,256]{1,0:T(8,128)(2,1)S(1)}, bf16[304,256]{1,0:T(8,128)(2,1)S(1)}, u32[]{:S(2)}, u32[]{:S(2)}) collective-permute-start(bf16[304,256]{1,0:T(8,128)(2,1)S(1)} %shard_map.235.kept), channel_id=1, source_target_pairs={{4,8},{6,10},{8,4},{10,6},{5,9},{7,11},{9,5},{11,7},{20,24},{22,26... | collective-permute-start | bytes 466952 | tf_op jit(solution)/shard_map/ppermute | solution.py:440
  32.3 16.7 %collective-permute-start.10 = (bf16[304,256]{1,0:T(8,128)(2,1)S(1)}, bf16[304,256]{1,0:T(8,128)(2,1)S(1)}, u32[]{:S(2)}, u32[]{:S(2)}) collective-permute-start(bf16[304,256]{1,0:T(8,128)(2,1)S(1)} %get-tuple-element.46), channel_id=1, source_target_pairs={{0,4},{2,6},{4,8},{6,10},{8,12},{10,14},{12,0},{14,2},{1,5},{3,7},... | collective-permute-start | bytes 466952 | tf_op jit(solution)/shard_map/ppermute | solution.py:393
  36.6 14.3 %collective-permute-start.8 = (bf16[304,256]{1,0:T(8,128)(2,1)S(1)}, bf16[304,256]{1,0:T(8,128)(2,1)S(1)}, u32[]{:S(2)}, u32[]{:S(2)}) collective-permute-start(bf16[304,256]{1,0:T(8,128)(2,1)S(1)} %get-tuple-element.43), channel_id=1, source_target_pairs={{0,8},{2,10},{4,12},{6,14},{8,0},{10,2},{12,4},{14,6},{1,9},{3,11}... | collective-permute-start | bytes 466952 | tf_op jit(solution)/shard_map/ppermute | solution.py:393
  38.2 17.5 %collective-permute-start.6 = (bf16[304,256]{1,0:T(8,128)(2,1)S(1)}, bf16[304,256]{1,0:T(8,128)(2,1)S(1)}, u32[]{:S(2)}, u32[]{:S(2)}) collective-permute-start(bf16[304,256]{1,0:T(8,128)(2,1)S(1)} %get-tuple-element.40), channel_id=1, source_target_pairs={{0,12},{2,14},{4,0},{6,2},{8,4},{10,6},{12,8},{14,10},{1,13},{3,15... | collective-permute-start | bytes 466952 | tf_op jit(solution)/shard_map/ppermute | solution.py:393
  41.1 18.8 %collective-permute-start.13 = (bf16[304,256]{1,0:T(8,128)(2,1)S(1)}, bf16[304,256]{1,0:T(8,128)(2,1)}, u32[]{:S(2)}, u32[]{:S(2)}) collective-permute-start(bf16[304,256]{1,0:T(8,128)(2,1)S(1)} %shard_map.236.kept), channel_id=1, source_target_pairs={{0,4},{2,6},{4,0},{6,2},{8,12},{10,14},{12,8},{14,10},{1,5},{3,7},... | collective-permute-start | bytes 466952 | tf_op jit(solution)/shard_map/ppermute | solution.py:440
  48.3 0.7 copy-start.5
  49.0 15.5 %collective-permute-start.11 = (bf16[272,256]{1,0:T(8,128)(2,1)}, bf16[272,256]{1,0:T(8,128)(2,1)}, u32[]{:S(2)}, u32[]{:S(2)}) collective-permute-start(bf16[272,256]{1,0:T(8,128)(2,1)} %get-tuple-element.47), channel_id=1, source_target_pairs={{0,4},{2,6},{4,8},{6,10},{8,12},{10,14},{12,0},{14,2},{1,5},{3,7},... | collective-permute-start | bytes 417800 | tf_op jit(solution)/shard_map/ppermute | solution.py:393
  50.9 14.0 %collective-permute-start.9 = (bf16[272,256]{1,0:T(8,128)(2,1)}, bf16[272,256]{1,0:T(8,128)(2,1)}, u32[]{:S(2)}, u32[]{:S(2)}) collective-permute-start(bf16[272,256]{1,0:T(8,128)(2,1)} %get-tuple-element.44), channel_id=1, source_target_pairs={{0,8},{2,10},{4,12},{6,14},{8,0},{10,2},{12,4},{14,6},{1,9},{3,11}... | collective-permute-start | bytes 417800 | tf_op jit(solution)/shard_map/ppermute | solution.py:393
  55.7 10.1 %collective-permute-start.7 = (bf16[272,256]{1,0:T(8,128)(2,1)}, bf16[272,256]{1,0:T(8,128)(2,1)}, u32[]{:S(2)}, u32[]{:S(2)}) collective-permute-start(bf16[272,256]{1,0:T(8,128)(2,1)} %get-tuple-element.41), channel_id=1, source_target_pairs={{0,12},{2,14},{4,0},{6,2},{8,4},{10,6},{12,8},{14,10},{1,13},{3,15... | collective-permute-start | bytes 417800 | tf_op jit(solution)/shard_map/ppermute | solution.py:393
  58.4 2.5 %copy-start.3 = (bf16[4096,32]{0,1:T(8,128)(2,1)S(1)}, bf16[4096,32]{0,1:T(8,128)(2,1)}, u32[]{:S(2)}) copy-start(bf16[4096,32]{0,1:T(8,128)(2,1)} %param.45) | copy-start | bytes 786436
  60.9 1.3 %copy-start.26 = (s32[8,4]{0,1:T(4,128)S(1)}, s32[8,4]{0,1:T(4,128)}, u32[]{:S(2)}) copy-start(s32[8,4]{0,1:T(4,128)} %param.33) | copy-start | bytes 388
  62.1 0.7 copy-start.27
  62.1 1.3 %collective-permute-start.14 = (f32[2,32,32]{2,1,0:T(8,128)S(1)}, f32[2,32,32]{2,1,0:T(8,128)S(1)}, u32[]{:S(2)}, u32[]{:S(2)}) collective-permute-start(f32[2,32,32]{2,1,0:T(8,128)S(1)} %shard_map.239), channel_id=1, source_target_pairs={{0,1},{1,0},{2,3},{3,2},{4,5},{5,4},{6,7},{7,6},{8,9},{9,8},{10,11... | collective-permute-start | bytes 24584 | tf_op jit(solution)/shard_map/ppermute | solution.py:486
  65.8 7.4 %copy-start.12 = (f32[2,32,32,128]{3,2,1,0:T(8,128)S(1)}, f32[2,32,32,128]{3,2,1,0:T(8,128)}, u32[]{:S(2)}) copy-start(f32[2,32,32,128]{3,2,1,0:T(8,128)} %copy-done.11) | copy-start | bytes 3145732
  70.5 15.2 %collective-permute-start.16 = (bf16[272,256]{1,0:T(8,128)(2,1)}, bf16[272,256]{1,0:T(8,128)(2,1)S(1)}, u32[]{:S(2)}, u32[]{:S(2)}) collective-permute-start(bf16[272,256]{1,0:T(8,128)(2,1)} %get-tuple-element.61), channel_id=1, source_target_pairs={{0,12},{2,14},{4,0},{6,2},{8,4},{10,6},{12,8},{14,10},{1,13},{3,15... | collective-permute-start | bytes 417800 | tf_op jit(solution)/shard_map/ppermute | solution.py:393
  71.9 14.0 %collective-permute-start.17 = (bf16[272,256]{1,0:T(8,128)(2,1)}, bf16[272,256]{1,0:T(8,128)(2,1)S(1)}, u32[]{:S(2)}, u32[]{:S(2)}) collective-permute-start(bf16[272,256]{1,0:T(8,128)(2,1)} %get-tuple-element.62), channel_id=1, source_target_pairs={{0,8},{2,10},{4,12},{6,14},{8,0},{10,2},{12,4},{14,6},{1,9},{3,11}... | collective-permute-start | bytes 417800 | tf_op jit(solution)/shard_map/ppermute | solution.py:393
  73.1 0.9 %copy-start.20 = (f32[16,32,128]{2,1,0:T(8,128)S(1)}, f32[16,32,128]{2,1,0:T(8,128)}, u32[]{:S(2)}) copy-start(f32[16,32,128]{2,1,0:T(8,128)} %copy-done.19) | copy-start | bytes 786436
  73.1 12.7 %collective-permute-start.18 = (bf16[272,256]{1,0:T(8,128)(2,1)}, bf16[272,256]{1,0:T(8,128)(2,1)S(1)}, u32[]{:S(2)}, u32[]{:S(2)}) collective-permute-start(bf16[272,256]{1,0:T(8,128)(2,1)} %get-tuple-element.63), channel_id=1, source_target_pairs={{0,4},{2,6},{4,8},{6,10},{8,12},{10,14},{12,0},{14,2},{1,5},{3,7},... | collective-permute-start | bytes 417800 | tf_op jit(solution)/shard_map/ppermute | solution.py:393
  73.2 0.9 %copy-start.21 = (f32[4096]{0:T(1024)S(1)}, f32[4096]{0:T(1024)}, u32[]{:S(2)}) copy-start(f32[4096]{0:T(1024)} %param.42) | copy-start | bytes 49156
  74.1 1.2 %copy-start.14 = (f32[2,32,32,128]{3,2,1,0:T(8,128)S(1)}, f32[2,32,32,128]{3,2,1,0:T(8,128)}, u32[]{:S(2)}) copy-start(f32[2,32,32,128]{3,2,1,0:T(8,128)} %copy-done.13) | copy-start | bytes 3145732
  75.3 1.2 %copy-start.16 = (f32[2,32,32,128]{3,2,1,0:T(8,128)S(1)}, f32[2,32,32,128]{3,2,1,0:T(8,128)}, u32[]{:S(2)}) copy-start(f32[2,32,32,128]{3,2,1,0:T(8,128)} %copy-done.15) | copy-start | bytes 3145732
  82.7 1.0 %copy-start.6 = (bf16[272,256]{1,0:T(8,128)(2,1)S(1)}, bf16[272,256]{1,0:T(8,128)(2,1)}, u32[]{:S(2)}) copy-start(bf16[272,256]{1,0:T(8,128)(2,1)} %copy-done.5) | copy-start | bytes 417796
  82.7 1.0 %copy-start.8 = (bf16[1,2,32,512]{3,2,1,0:T(8,128)(2,1)S(1)}, bf16[1,2,32,512]{3,2,1,0:T(8,128)(2,1)}, u32[]{:S(2)}) copy-start(bf16[1,2,32,512]{3,2,1,0:T(8,128)(2,1)} %param.24) | copy-start | bytes 196612
